TPU v7x, 32 devices: a whole 2x2x4 slice. The times are simulated.
32 devices in a mesh: row: 8 (over y, x, core), col: 4 (over z).
Axes of the slice: x: 2, y: 2, z: 4, core: 2. Of those that a mesh axis runs over, the one named last changes fastest.
Arguments:
- tokens: bfloat16 [1280, 2048], P('row', 'col'), may hold values from -1600 to 1600, as said below
- norm_gain: float32 [2048], P('col'), may hold values from 0.1 to 1.9
- lengths: int32 [16], replicated, may hold values from 1 to 320, 1280 in all
- request_adapter: int32 [16], replicated, may hold values from 0 to 63
- routes: int32 [1280, 2], P('row'), may hold values from 0 to 7, all different within a row; in each aligned block of 160 rows (0 to 159, 160 to 319, ...) at most 60 rows name the same one
- route_weights: float32 [1280, 2], P('row'), may hold values from 0.2 to 1
- gate_weight: bfloat16 [8, 5632, 2048], P('row', 'col'), may hold values from -0.125 to 0.125
- up_weight: bfloat16 [8, 5632, 2048], P('row', 'col'), may hold values from -0.125 to 0.125
- down_weight: bfloat16 [8, 5632, 2048], P('row', None, 'col'), may hold values from -0.078125 to 0.078125
- adapter_down: bfloat16 [64, 2048, 16], P('row', 'col'), may hold values from -0.125 to 0.125
- adapter_up: bfloat16 [64, 16, 2048], P('row', None, 'col'), may hold values from -1.5 to 1.5
Outputs:
- mixed: bfloat16 [1280, 2048], P('row', 'col')
Inputs may be any that keep to these rules, and one draw needn't show every extreme that they name: Feature scales differ over the features and token scales over the tokens. The lengths sum to 1280. `routes`: A token's two experts differ. Among the tokens of one index of row (aligned blocks of 160 tokens) no expert is named by more than 60 tokens, a bound that some block reaches.
All inputs are finite; a program needn't handle non-finite values.
Results may differ from a plain program's by a relative error of at most 0.008.
Values may be sent and summed in bfloat16 or wider, within the bound.
No kernel may reach another device: no remote copies, remote signals or barrier semaphores. Data moves between devices by JAX's collectives and lax.ppermute only.
A program may use at most 64 MiB of HBM per device.

v0:
```python
import jax
import jax.numpy as jnp
from jax import lax
from jax.sharding import PartitionSpec as P

D = 2048
EXPERTS = 8
TOPK = 2
RANK = 16
CAP = 60


def contract_last(left, right):
    return lax.dot_general(
        left, right, (((1,), (1,)), ((), ())), preferred_element_type=jnp.float32
    )


def body(
    tokens,
    norm_gain,
    lengths,
    request_adapter,
    routes,
    route_weights,
    gate_weight,
    up_weight,
    down_weight,
    adapter_down,
    adapter_up,
):
    tok_rows, width_part = tokens.shape
    rows_axis = lax.axis_size("row")
    splits = rows_axis // EXPERTS
    widened = tokens.astype(jnp.float32)
    squares = lax.psum(jnp.sum(widened * widened, axis=1), "col")
    normed = (widened * lax.rsqrt(squares[:, None] / D + 1e-06) * norm_gain[None, :]).astype(
        jnp.bfloat16
    )
    req_ends = jnp.cumsum(lengths)
    position = lax.axis_index("row") * tok_rows + jnp.arange(tok_rows, dtype=jnp.int32)
    request = jnp.sum((position[:, None] >= req_ends[None, :]).astype(jnp.int32), axis=1)
    request_hot = request[:, None] == jnp.arange(lengths.shape[0], dtype=jnp.int32)[None, :]
    adapter = jnp.sum(jnp.where(request_hot, request_adapter[None, :], 0), axis=1)
    adapter_count = adapter_down.shape[0] * rows_axis
    select = (adapter[:, None] == jnp.arange(adapter_count, dtype=jnp.int32)[None, :]).astype(
        jnp.float32
    )
    down_all, up_all = (
        lax.all_gather(adapter_down, "row", axis=0, tiled=True),
        lax.all_gather(adapter_up, "row", axis=0, tiled=True),
    )
    down_matrix = jnp.transpose(down_all, (1, 0, 2)).reshape(width_part, adapter_count * RANK)
    projected = jnp.dot(normed, down_matrix, preferred_element_type=jnp.float32).reshape(
        tok_rows, adapter_count, RANK
    )
    partial_low = jnp.sum(projected * select[:, :, None], axis=1)
    low_rank = lax.psum(partial_low, "col").astype(jnp.bfloat16)
    expanded = (select.astype(jnp.bfloat16)[:, :, None] * low_rank[:, None, :]).reshape(
        tok_rows, adapter_count * RANK
    )
    branch = jnp.dot(
        expanded,
        up_all.reshape(adapter_count * RANK, width_part),
        preferred_element_type=jnp.float32,
    )
    assigned = routes.reshape(-1)
    assign_count = assigned.shape[0]
    expert_hot = (assigned[:, None] == jnp.arange(EXPERTS, dtype=jnp.int32)[None, :]).astype(
        jnp.int32
    )
    earlier = (
        jnp.arange(assign_count, dtype=jnp.int32)[:, None]
        > jnp.arange(assign_count, dtype=jnp.int32)[None, :]
    ).astype(jnp.int32)
    before = jnp.dot(earlier, expert_hot)
    slot_index = jnp.sum(before * expert_hot, axis=1)
    placed_at = assigned * CAP + slot_index
    placing = (jnp.arange(EXPERTS * CAP, dtype=jnp.int32)[:, None] == placed_at[None, :]).astype(
        jnp.bfloat16
    )
    unit_gate = gate_weight[0]
    unit_up = up_weight[0]
    unit_down = down_weight[0]
    block_rows = rows_axis * CAP
    width_now = normed.shape[1]
    buffer = jnp.dot(
        placing, jnp.repeat(normed, TOPK, axis=0), preferred_element_type=jnp.float32
    ).astype(jnp.bfloat16)
    tiled = jnp.broadcast_to(
        buffer.reshape(EXPERTS, 1, CAP, width_now), (EXPERTS, splits, CAP, width_now)
    )
    arrived = lax.all_to_all(
        tiled.reshape(rows_axis, CAP, width_now), "row", split_axis=0, concat_axis=0, tiled=True
    ).reshape(block_rows, width_part)
    portion = lax.all_gather(arrived, "col", axis=1, tiled=True)
    gate_sum = contract_last(portion, unit_gate)
    up_sum = contract_last(portion, unit_up)
    hidden = (jax.nn.silu(gate_sum) * up_sum).astype(jnp.bfloat16)
    partial_value = jnp.dot(
        lax.all_gather(hidden, "col", axis=1, tiled=True),
        unit_down,
        preferred_element_type=jnp.float32,
    )
    block_out = partial_value.astype(jnp.bfloat16).reshape(rows_axis, CAP, width_part)
    returned = lax.all_to_all(block_out, "row", split_axis=0, concat_axis=0, tiled=True).astype(
        jnp.float32
    )
    per_expert = jnp.sum(returned.reshape(EXPERTS, splits, CAP, width_part), axis=1).reshape(
        EXPERTS * CAP, width_part
    )
    gathered = jnp.dot(placing.astype(jnp.float32).T, per_expert, precision=lax.Precision.HIGHEST)
    weighted = jnp.sum(
        gathered.reshape(tok_rows, TOPK, width_part) * route_weights[:, :, None], axis=1
    )
    return (weighted + branch).astype(jnp.bfloat16)


def solution(mesh):
    in_specs = (
        P("row", "col"),
        P("col"),
        P(),
        P(),
        P("row", None),
        P("row", None),
        P("row", "col", None),
        P("row", "col", None),
        P("row", None, "col"),
        P("row", "col", None),
        P("row", None, "col"),
    )
    out_specs = P("row", "col")
    return jax.shard_map(body, mesh=mesh, in_specs=in_specs, out_specs=out_specs, check_vma=False)
```

profile of v0, /device:TPU:0, one launch (start us, length us, event | category | flops | bytes accessed | tf_op | source)
XLA Modules:
  0.0 250.5 jit_solution(18265249144313198987)
XLA Ops:
  6.5 0.0 all-gather.5.cloned.1.call-start
  6.5 0.8 copy.29
  7.3 0.1 reshape.138
  7.5 0.2 fusion.19
  7.7 1.0 fusion.24
  8.7 13.5 %psum.14 = f32[160]{0:T(256)S(1)} all-reduce(f32[160]{0:T(256)S(1)} %fusion.24), channel_id=1, replica_groups=mesh['row'=8,'col'=4] {'col'}, use_global_device_ids=true, to_apply=%region_2.0 | all-reduce | flops 160 | bytes 1280 | tf_op jit(solution)/shard_map/psum | solution.py:36
  22.2 1.0 fusion.26
  23.2 0.2 broadcast_in_dim.10
  23.4 0.1 reshape.139
  23.5 0.4 convolution_convert_fusion
  24.0 0.1 reshape_reshape.3
  24.1 13.3 %all_to_all.10 = bf16[8,60,512]{2,1,0:T(8,128)(2,1)S(1)} all-to-all(bf16[8,60,512]{2,1,0:T(8,128)(2,1)S(1)} %reshape_reshape.3), channel_id=1, replica_groups=mesh['row'=8,'col'=4] {'row'}, dimensions={0} | all-to-all | bytes 983040 | tf_op jit(solution)/shard_map/all_to_all | solution.py:93
  37.3 0.9 reshape.140
  38.2 0.0 all-gather.5.cloned.1.call-update
  38.3 0.0 all-gather.7.cloned.1.call-start
  38.3 40.0 %all-gather.5.cloned.1.call-done = bf16[480,2048]{1,0:T(8,128)(2,1)} async-done(((bf16[480,512]{1,0:T(8,128)(2,1)}), bf16[480,2048]{1,0:T(8,128)(2,1)}) %all-gather.5.cloned.1.call-update) | async-done | bytes 1966096 | tf_op jit(solution)/shard_map/all_gather | solution.py:96
  78.3 6.8 %fusion.4 = f32[480,1408]{1,0:T(8,128)S(1)} fusion(bf16[480,2048]{1,0:T(8,128)(2,1)} %all-gather.5.cloned.1.call-done, bf16[1,1408,2048]{2,1,0:T(8,128)(2,1)} %param.17), kind=kOutput, calls=%fused_computation.4 | convolution fusion | flops 2768240640 | bytes 10436608 | tf_op jit(solution)/shard_map/dot_general | solution.py:14
  85.1 0.0 copy-done.3
  85.1 0.0 copy-start
  85.1 0.0 copy-start.1
  85.1 0.0 copy-start.2
  85.1 7.7 %fusion.9 = bf16[480,1408]{1,0:T(8,128)(2,1)} fusion(bf16[480,2048]{1,0:T(8,128)(2,1)S(1)} %copy-done.3, bf16[1,1408,2048]{2,1,0:T(8,128)(2,1)} %param.18, f32[480,1408]{1,0:T(8,128)S(1)} %fusion.4), kind=kOutput, calls=%fused_computation.7 | convolution fusion | flops 2772295680 | bytes 11788288 | tf_op jit(solution)/shard_map/dot_general | solution.py:14
  92.9 0.0 all-gather.7.cloned.1.call-update
  92.9 0.0 all-gather.9.cloned.1.call-start
  92.9 0.7 all-gather.9.cloned.1.call-update
  93.6 0.0 all-gather.11.cloned.1.call-start
  93.7 0.7 copy.33
  94.4 0.0 all-gather.11.cloned.1.call-update
  94.4 0.2 iota_compare_fusion.2
  94.6 0.2 eq.80
  94.8 0.0 copy-done.1
  94.8 0.1 copy.31
  95.0 0.1 reduce
  95.1 0.1 convert_reduce_fusion
  95.2 0.1 select_reduce_fusion
  95.3 97.4 %all-gather.7.cloned.1.call-done = bf16[480,5632]{1,0:T(8,128)(2,1)} async-done(((bf16[480,1408]{1,0:T(8,128)(2,1)}), bf16[480,5632]{1,0:T(8,128)(2,1)}) %all-gather.7.cloned.1.call-update) | async-done | bytes 5406736 | tf_op jit(solution)/shard_map/all_gather | solution.py:101
  192.6 7.2 %fusion.12 = bf16[480,512]{1,0:T(8,128)(2,1)S(1)} fusion(bf16[480,5632]{1,0:T(8,128)(2,1)} %all-gather.7.cloned.1.call-done, bf16[1,5632,512]{2,1,0:T(8,128)(2,1)} %param.19), kind=kOutput, calls=%fused_computation.9 | convolution fusion | flops 2768486400 | bytes 11665408 | tf_op jit(solution)/shard_map/dot_general | solution.py:100
  199.8 0.0 copy-start.4
  199.8 0.9 reshape.141
  200.7 3.7 %all-to-all-start.1 = ((bf16[8,60,512]{2,1,0:T(8,128)(2,1)}), bf16[8,60,512]{2,1,0:T(8,128)(2,1)S(1)}, u32[]{:S(2)}, u32[]{:S(2)}) async-start(bf16[8,60,512]{2,1,0:T(8,128)(2,1)} %reshape.141), calls=%async_computation.1 | async-start | bytes 1048576 | tf_op jit(solution)/shard_map/all_to_all | solution.py:106
  204.4 13.4 %all-gather.9.cloned.1.call-done = bf16[64,512,16]{1,2,0:T(8,128)(2,1)} async-done(((bf16[8,512,16]{1,2,0:T(8,128)(2,1)}), bf16[64,512,16]{1,2,0:T(8,128)(2,1)}) %all-gather.9.cloned.1.call-update) | async-done | bytes 1048592 | tf_op jit(solution)/shard_map/all_gather | solution.py:50
  217.8 2.5 %fusion.15 = f32[160,16]{0,1:T(8,128)S(1)} fusion(bf16[64,16,512]{2,1,0:T(8,128)(2,1)} %bitcast.39, f32[160,64]{0,1:T(8,128)S(1)} %get-tuple-element.6, bf16[160,512]{1,0:T(8,128)(2,1)S(1)} %fusion.26), kind=kOutput, calls=%fused_computation.12 | convolution fusion | flops 168097280 | bytes 1263616 | tf_op jit(solution)/shard_map/dot_general | solution.py:54
  220.3 17.3 %psum.15 = bf16[160,16]{0,1:T(8,128)(2,1)S(1)} all-reduce(f32[160,16]{0,1:T(8,128)S(1)} %fusion.15), channel_id=1, replica_groups=mesh['row'=8,'col'=4] {'col'}, use_global_device_ids=true, to_apply=%region_8.9 | all-reduce | flops 2560 | bytes 15360 | tf_op jit(solution)/shard_map/psum | solution.py:58
  237.6 0.0 all-to-all-done.1
  237.6 0.1 reshape.146
  237.7 0.3 fusion.16
  238.1 3.6 %all-gather.11.cloned.1.call-done = bf16[64,16,512]{2,0,1:T(8,128)(2,1)} async-done(((bf16[8,16,512]{2,0,1:T(8,128)(2,1)}), bf16[64,16,512]{2,0,1:T(8,128)(2,1)}) %all-gather.11.cloned.1.call-update) | async-done | bytes 1048592 | tf_op jit(solution)/shard_map/all_gather | solution.py:51
  241.7 2.3 fusion.18
  (9 shorter events, 0.1 us)
Async XLA Ops:
  6.5 71.8 %all-gather.5.cloned.1.call-start = ((), (), s32[]{:S(2)}) async-start(), calls=%async_computation.2 | async-start | bytes 2457600 | tf_op jit(solution)/shard_map/all_gather | solution.py:96
  38.3 154.4 %all-gather.7.cloned.1.call-start = ((), (), s32[]{:S(2)}) async-start(), calls=%async_computation.3 | async-start | bytes 6758400 | tf_op jit(solution)/shard_map/all_gather | solution.py:101
  78.3 6.8 %copy-start.3 = (bf16[480,2048]{1,0:T(8,128)(2,1)S(1)}, bf16[480,2048]{1,0:T(8,128)(2,1)}, u32[]{:S(2)}) copy-start(bf16[480,2048]{1,0:T(8,128)(2,1)} %all-gather.5.cloned.1.call-done) | copy-start | bytes 5898244
  85.1 8.6 %copy-start = (bf16[8,16,512]{2,1,0:T(8,128)(2,1)S(1)}, bf16[8,16,512]{2,1,0:T(8,128)(2,1)}, u32[]{:S(2)}) copy-start(bf16[8,16,512]{2,1,0:T(8,128)(2,1)} %param.21) | copy-start | bytes 393220
  85.1 9.7 %copy-start.1 = (s32[16]{0:T(128)S(1)}, s32[16]{0:T(128)}, u32[]{:S(2)}) copy-start(s32[16]{0:T(128)} %param.13) | copy-start | bytes 196
  85.1 10.0 %copy-start.2 = (s32[16]{0:T(128)S(1)}, s32[16]{0:T(128)}, u32[]{:S(2)}) copy-start(s32[16]{0:T(128)} %param.14) | copy-start | bytes 196
  92.9 124.9 %all-gather.9.cloned.1.call-start = ((), (), s32[]{:S(2)}) async-start(), calls=%async_computation.4 | async-start | bytes 1179648 | tf_op jit(solution)/shard_map/all_gather | solution.py:50
  93.6 148.1 %all-gather.11.cloned.1.call-start = ((), (), s32[]{:S(2)}) async-start(), calls=%async_computation.5 | async-start | bytes 1179648 | tf_op jit(solution)/shard_map/all_gather | solution.py:51
  199.8 37.9 %copy-start.4 = (f32[160,2]{0,1:T(2,128)S(1)}, f32[160,2]{0,1:T(2,128)}, u32[]{:S(2)}) copy-start(f32[160,2]{0,1:T(2,128)} %param.16) | copy-start | bytes 3844
  200.7 36.9 %all-to-all-start.1 = ((bf16[8,60,512]{2,1,0:T(8,128)(2,1)}), bf16[8,60,512]{2,1,0:T(8,128)(2,1)S(1)}, u32[]{:S(2)}, u32[]{:S(2)}) async-start(bf16[8,60,512]{2,1,0:T(8,128)(2,1)} %reshape.141), calls=%async_computation.1 | async-start | bytes 1048576 | tf_op jit(solution)/shard_map/all_to_all | solution.py:106
Sparse Core Ops, SparseCore 0:
  38.4 39.8 all-gather.4
  93.0 99.5 all-gather.6
  194.5 23.1 all-gather.8
  219.5 22.1 all-gather.10
where the time goes:
time: 251 us
  waiting for transfers between devices  155 us (62%)
  blocking collectives  44.1 us (18%)
  matrix products  27.4 us (11%)
  between operations  13.3 us (5%)
  local copies, waits for them, and re-layouts  4.26 us (2%)
  starting transfers between devices  3.78 us (2%)
  other arithmetic  2.58 us (1%)
    all_gather x1, waiting for transfers between devices, body(): lax.all_gather(hidden, 'col', axis=1, tiled=True)  97.4 us
    all_gather x1, waiting for transfers between devices, body(): portion = lax.all_gather(arrived, 'col', axis=1, tiled=True)  40 us
    psum x1, blocking collectives, body(): low_rank = lax.psum(partial_low, 'col').astype(jnp.bfloat16)  17.3 us
    dot_general x2, matrix products, contract_last(): lax.dot_general(left, right, (((1,), (1,)), ((), ())), preferred_element_...  14.5 us
    psum x1, blocking collectives, body(): squares = lax.psum(jnp.sum(widened * widened, axis=1), 'col')  13.5 us
    all_gather x1, waiting for transfers between devices, body(): lax.all_gather(adapter_down, 'row', axis=0, tiled=True)  13.4 us
    all_to_all x1, blocking collectives, body(): lax.all_to_all(tiled.reshape(rows_axis, CAP, width_now), 'row', split_axi...  13.3 us
    dot_general x1, matrix products, body(): jnp.dot(lax.all_gather(hidden, 'col', axis=1, tiled=True), unit_down, pre...  7.19 us
  transfers between devices with their start and end apart: 5, of which 4 were waited for; matrix products, arithmetic and copies ran while one was open for 5% of the time, Pallas kernels for 0%

commit v1 on v0

v1 whole, which is shorter than its diff:
```python
import jax
import jax.numpy as jnp
from jax import lax
from jax.sharding import PartitionSpec as P

D = 2048
EXPERTS = 8
TOPK = 2
RANK = 16
CAP = 60
GAIN_ROWS = 16
LOW_ROWS = 8
LOW_STRIDE = 256


def contract_last(left, right):
    return lax.dot_general(
        left, right, (((1,), (1,)), ((), ())), preferred_element_type=jnp.float32
    )


def col_shift(value, by):
    size = lax.axis_size("col")
    return lax.ppermute(value, "col", [(i, (i + by) % size) for i in range(size)])


def row_xor(value, by):
    return lax.ppermute(value, "row", [(i, i ^ by) for i in range(lax.axis_size("row"))])


def ring_gather(value):
    size = lax.axis_size("col")
    rows = value.shape[0]
    half = -(-rows // 16) * 8
    found = [(0, 0, value)]
    from_left, from_right = value, value
    for hop in range(1, (size + 1) // 2):
        from_left, from_right = col_shift(from_left, 1), col_shift(from_right, -1)
        found += [(hop, 0, from_left), (-hop, 0, from_right)]
    if size % 2 == 0:
        found += [
            (size // 2, 0, col_shift(from_left[:half], 1)),
            (-size // 2, half, col_shift(from_right[half:], -1)),
        ]
    return found


def lay_out(pieces, rows, width):
    size = lax.axis_size("col")
    here = lax.axis_index("col")
    whole = jnp.zeros((rows, size * width), pieces[0][2].dtype)
    for distance, first, block in pieces:
        source = lax.rem(here - distance + size, size)
        whole = lax.dynamic_update_slice(whole, block, (first, source * width))
    return whole


def split_float(value, parts):
    pieces = []
    for _ in range(parts):
        piece = value.astype(jnp.bfloat16)
        pieces.append(piece)
        value = value - piece.astype(jnp.float32)
    return pieces


def body(
    tokens,
    norm_gain,
    lengths,
    request_adapter,
    routes,
    route_weights,
    gate_weight,
    up_weight,
    down_weight,
    adapter_down,
    adapter_up,
):
    tok_rows, width_part = tokens.shape
    rows_axis, cols_axis = lax.axis_size("row"), lax.axis_size("col")
    row_at, col_at = lax.axis_index("row"), lax.axis_index("col")
    splits = rows_axis // EXPERTS
    chips = rows_axis // 2
    unit_gate, unit_up, unit_down = gate_weight[0], up_weight[0], down_weight[0]
    hidden_part = unit_gate.shape[0]

    down_all, up_all = (
        lax.all_gather(adapter_down, "row", axis=0, tiled=True),
        lax.all_gather(adapter_up, "row", axis=0, tiled=True),
    )

    gain_parts = jnp.stack(split_float(norm_gain, 3))
    sent = jnp.concatenate(
        [tokens, jnp.pad(gain_parts, ((0, GAIN_ROWS - 3), (0, 0)))], axis=0
    )
    gathered_rows = sent.shape[0]
    features = lay_out(ring_gather(sent), gathered_rows, width_part)

    assigned = routes.reshape(-1)
    assign_count = assigned.shape[0]
    expert_hot = (assigned[:, None] == jnp.arange(EXPERTS, dtype=jnp.int32)[None, :]).astype(
        jnp.bfloat16
    )
    earlier = (
        jnp.arange(assign_count, dtype=jnp.int32)[:, None]
        > jnp.arange(assign_count, dtype=jnp.int32)[None, :]
    ).astype(jnp.bfloat16)
    before = jnp.dot(earlier, expert_hot, preferred_element_type=jnp.float32)
    slot_index = jnp.sum(before * expert_hot.astype(jnp.float32), axis=1).astype(jnp.int32)
    place = jnp.arange(chips * 2 * CAP, dtype=jnp.int32)
    target = row_at ^ (place // CAP)
    wanted = (target // splits) * CAP + place % CAP
    placed_at = assigned * CAP + slot_index
    placing = (wanted[:, None] == placed_at[None, :]).astype(jnp.bfloat16)
    placing_tokens = jnp.sum(placing.reshape(-1, tok_rows, TOPK), axis=2)

    widened = features[:tok_rows].astype(jnp.float32)
    gain = jnp.sum(features[tok_rows : tok_rows + 3].astype(jnp.float32), axis=0)
    scale = lax.rsqrt(jnp.mean(widened * widened, axis=1, keepdims=True) + 1e-06)
    normed = (widened * scale * gain[None, :]).astype(jnp.bfloat16)
    outgoing = jnp.dot(placing_tokens, normed, preferred_element_type=jnp.float32).astype(
        jnp.bfloat16
    ).reshape(chips, 2, CAP, D)
    here_half, there_half = outgoing[:, 0], outgoing[:, 1]
    partner_half = row_xor(there_half, 1)

    own = lax.dynamic_slice(normed, (0, col_at * width_part), (tok_rows, width_part))
    req_ends = jnp.cumsum(lengths)
    position = row_at * tok_rows + jnp.arange(tok_rows, dtype=jnp.int32)
    request = jnp.sum((position[:, None] >= req_ends[None, :]).astype(jnp.int32), axis=1)
    request_hot = request[:, None] == jnp.arange(lengths.shape[0], dtype=jnp.int32)[None, :]
    adapter = jnp.sum(jnp.where(request_hot, request_adapter[None, :], 0), axis=1)
    adapter_count = adapter_down.shape[0] * rows_axis
    select = (adapter[:, None] == jnp.arange(adapter_count, dtype=jnp.int32)[None, :]).astype(
        jnp.float32
    )
    down_matrix = jnp.transpose(down_all, (1, 0, 2)).reshape(width_part, adapter_count * RANK)
    projected = jnp.dot(own, down_matrix, preferred_element_type=jnp.float32).reshape(
        tok_rows, adapter_count, RANK
    )
    partial_low = jnp.sum(projected * select[:, :, None], axis=1)

    groups = [[0], list(range(1, chips - 1)), [chips - 1]]
    low_group = 1
    low_sum = None
    returned = [None] * chips
    for number, offsets in enumerate(groups):
        blocks = []
        for offset in offsets:
            pair = jnp.concatenate([here_half[offset], partner_half[offset]], axis=0)
            blocks.append(pair if offset == 0 else row_xor(pair, 2 * offset))
        arrived = jnp.concatenate(blocks, axis=0)
        gate_sum = contract_last(arrived, unit_gate)
        up_sum = contract_last(arrived, unit_up)
        hidden = (jax.nn.silu(gate_sum) * up_sum).astype(jnp.bfloat16)
        count = hidden.shape[0]
        if number == low_group:
            high, low = split_float(partial_low, 2)
            flat = jnp.concatenate([high, low], axis=1).reshape(-1)
            extra = -(-flat.shape[0] // hidden_part)
            extra_rows = -(-extra // 8) * 8
            flat = jnp.pad(flat, (0, extra_rows * hidden_part - flat.shape[0]))
            hidden = jnp.concatenate([hidden, flat.reshape(extra_rows, hidden_part)], axis=0)
        pieces = ring_gather(hidden)
        whole = lay_out(pieces, hidden.shape[0], hidden_part)
        if number == low_group:
            rest = whole[count:].reshape(extra_rows, cols_axis, hidden_part)
            rest = jnp.transpose(rest, (1, 0, 2)).reshape(cols_axis, -1)
            rest = rest[:, : tok_rows * 2 * RANK].reshape(cols_axis, tok_rows, 2, RANK)
            low_sum = jnp.sum(rest.astype(jnp.float32), axis=(0, 2))
        block_out = jnp.dot(
            whole[:count], unit_down, preferred_element_type=jnp.float32
        ).astype(jnp.bfloat16)
        for index, offset in enumerate(offsets):
            piece = block_out[index * 2 * CAP : (index + 1) * 2 * CAP]
            returned[offset] = piece if offset == 0 else row_xor(piece, 2 * offset)

    low_rank = low_sum.astype(jnp.bfloat16)
    expanded = (select.astype(jnp.bfloat16)[:, :, None] * low_rank[:, None, :]).reshape(
        tok_rows, adapter_count * RANK
    )
    branch = jnp.dot(
        expanded,
        up_all.reshape(adapter_count * RANK, width_part),
        preferred_element_type=jnp.float32,
    )
    back = jnp.stack(returned).reshape(chips, 2, CAP, width_part)
    back_partner = row_xor(back[:, 1], 1)
    back = jnp.stack([back[:, 0], back_partner], axis=1).reshape(-1, width_part)
    taken = lax.dot_general(
        placing, back, (((0,), (0,)), ((), ())), preferred_element_type=jnp.float32
    ).reshape(tok_rows, TOPK, width_part)
    weighted = jnp.sum(taken * route_weights[:, :, None], axis=1)
    return (weighted + branch).astype(jnp.bfloat16)


def solution(mesh):
    in_specs = (
        P("row", "col"),
        P("col"),
        P(),
        P(),
        P("row", None),
        P("row", None),
        P("row", "col", None),
        P("row", "col", None),
        P("row", None, "col"),
        P("row", "col", None),
        P("row", None, "col"),
    )
    out_specs = P("row", "col")
    return jax.shard_map(body, mesh=mesh, in_specs=in_specs, out_specs=out_specs, check_vma=False)
```

time: 251 us -> 170 us (0.68)
  waiting for transfers between devices: 155 us -> 73.1 us
  blocking collectives: 44.1 us -> 0 us
  starting transfers between devices: 3.78 us -> 37.1 us
  local copies, waits for them, and re-layouts: 4.26 us -> 12.1 us
    all_gather x2 -> x0, waiting for transfers between devices: 137 us -> none  [the longest x1 97.4 us: body(): lax.all_gather(hidden, 'col', axis=1, tiled=True)]
    ppermute x0 -> x24, waiting for transfers between devices: none -> 72.3 us  [the longest x16 61.8 us: col_shift(): lax.ppermute(value, 'col', [(i, (i + by) % size) for i in range(size)])]
    ppermute x0 -> x24, starting transfers between devices: none -> 37 us  [the longest x16 30 us: col_shift(): lax.ppermute(value, 'col', [(i, (i + by) % size) for i in range(size)])]
    psum x2 -> x0, blocking collectives: 30.8 us -> none  [the longest x1 17.3 us: body(): low_rank = lax.psum(partial_low, 'col').astype(jnp.bfloat16)]
    all_gather x1, waiting for transfers between devices: 13.4 us -> 0.02 us  [body(): lax.all_gather(adapter_down, 'row', axis=0, tiled=True)]
    all_to_all x1 -> x0, blocking collectives: 13.3 us -> none  [body(): lax.all_to_all(tiled.reshape(rows_axis, CAP, width_now), 'row', split_axi...]
    all_to_all x1 -> x0, starting transfers between devices: 3.66 us -> none  [body(): lax.all_to_all(block_out, 'row', split_axis=0, concat_axis=0, tiled=True)]
    all_gather x1, waiting for transfers between devices: 3.6 us -> 0.02 us  [body(): lax.all_gather(adapter_up, 'row', axis=0, tiled=True)]
  transfers between devices with their start and end apart: 5 -> 26, of which waited for: 4 -> 15; matrix products, arithmetic and copies ran while one was open for 5% -> 24% of each run, Pallas kernels for 0% -> 0%
where the time goes in v1:
time: 170 us
  waiting for transfers between devices  73.1 us (43%)
  starting transfers between devices  37.1 us (22%)
  matrix products  29.7 us (17%)
  between operations  14.2 us (8%)
  local copies, waits for them, and re-layouts  12.1 us (7%)
  other arithmetic  3.43 us (2%)
    ppermute x16, waiting for transfers between devices, col_shift(): lax.ppermute(value, 'col', [(i, (i + by) % size) for i in range(size)])  61.8 us
    ppermute x16, starting transfers between devices, col_shift(): lax.ppermute(value, 'col', [(i, (i + by) % size) for i in range(size)])  30 us
    dot_general x6, matrix products, contract_last(): lax.dot_general(left, right, (((1,), (1,)), ((), ())), preferred_element_...  16 us
    ppermute x8, waiting for transfers between devices, row_xor(): lax.ppermute(value, 'row', [(i, i ^ by) for i in range(lax.axis_size('row...  10.6 us
    ppermute x8, starting transfers between devices, row_xor(): lax.ppermute(value, 'row', [(i, i ^ by) for i in range(lax.axis_size('row...  7.06 us
    dot_general x3, matrix products, body(): jnp.dot(whole[:count], unit_down, preferred_element_type=jnp.float32)  6.2 us
    unnamed x40, local copies, waits for them, and re-layouts  3.84 us
  transfers between devices with their start and end apart: 26, of which 15 were waited for; matrix products, arithmetic and copies ran while one was open for 24% of the time, Pallas kernels for 0%

profile of v1, /device:TPU:0, one launch (start us, length us, event | category | flops | bytes accessed | tf_op | source)
XLA Modules:
  0.0 169.6 jit_solution(9238006984733749002)
XLA Ops:
  6.5 0.7 all-gather.3.cloned.1.call-update
  7.3 0.8 fusion.79
  8.2 0.9 pad_maximum_fusion.8
  9.2 3.1 %collective-permute-start = (bf16[176,512]{1,0:T(8,128)(2,1)S(1)}, bf16[176,512]{1,0:T(8,128)(2,1)S(1)}, u32[]{:S(2)}, u32[]{:S(2)}) collective-permute-start(bf16[176,512]{1,0:T(8,128)(2,1)S(1)} %get-tuple-element.23), channel_id=1, source_target_pairs={{0,1},{1,2},{2,3},{3,0},{4,5},{5,6},{6,7},{7,4},{8,9},{9,10},{10,1... | collective-permute-start | bytes 540680 | tf_op jit(solution)/shard_map/ppermute | solution.py:24
  12.2 2.1 %collective-permute-start.1 = (bf16[176,512]{1,0:T(8,128)(2,1)S(1)}, bf16[176,512]{1,0:T(8,128)(2,1)S(1)}, u32[]{:S(2)}, u32[]{:S(2)}) collective-permute-start(bf16[176,512]{1,0:T(8,128)(2,1)S(1)} %get-tuple-element.23), channel_id=1, source_target_pairs={{0,3},{1,0},{2,1},{3,2},{4,7},{5,4},{6,5},{7,6},{8,11},{9,8},{10,9... | collective-permute-start | bytes 540680 | tf_op jit(solution)/shard_map/ppermute | solution.py:24
  14.3 0.7 copy.74
  16.0 3.7 %collective-permute-done = bf16[176,512]{1,0:T(8,128)(2,1)S(1)} collective-permute-done((bf16[176,512]{1,0:T(8,128)(2,1)S(1)}, bf16[176,512]{1,0:T(8,128)(2,1)S(1)}, u32[]{:S(2)}, u32[]{:S(2)}) %collective-permute-start) | collective-permute-done | bytes 180256 | tf_op jit(solution)/shard_map/ppermute | solution.py:24
  19.8 2.4 %collective-permute-done.1 = bf16[176,512]{1,0:T(8,128)(2,1)S(1)} collective-permute-done((bf16[176,512]{1,0:T(8,128)(2,1)S(1)}, bf16[176,512]{1,0:T(8,128)(2,1)S(1)}, u32[]{:S(2)}, u32[]{:S(2)}) %collective-permute-start.1) | collective-permute-done | bytes 180256 | tf_op jit(solution)/shard_map/ppermute | solution.py:24
  22.1 3.2 %collective-permute-start.3 = (bf16[88,512]{1,0:T(8,128)(2,1)S(1)}, bf16[88,512]{1,0:T(8,128)(2,1)S(1)}, u32[]{:S(2)}, u32[]{:S(2)}) collective-permute-start(bf16[88,512]{1,0:T(8,128)(2,1)S(1)} %slice.114), channel_id=1, source_target_pairs={{0,3},{1,0},{2,1},{3,2},{4,7},{5,4},{6,5},{7,6},{8,11},{9,8},{10,9... | collective-permute-start | bytes 270344 | tf_op jit(solution)/shard_map/ppermute | solution.py:24
  25.3 1.4 collective-permute-done.2
  26.7 0.7 collective-permute-done.3
  27.9 0.8 copy-done.1
  28.8 2.0 %convolution_convert_fusion = bf16[480,2048]{1,0:T(8,128)(2,1)} fusion(bf16[480,160]{0,1:T(8,128)(2,1)S(1)} %fusion.47, bf16[160,2048]{1,0:T(8,128)(2,1)S(1)} %fusion.27), kind=kOutput, calls=%fused_computation.18 | convolution fusion | flops 315555840 | bytes 2775040 | tf_op jit(solution)/shard_map/dot_general | solution.py:122
  30.8 1.7 %reshape.186 = bf16[4,2,60,2048]{3,2,1,0:T(8,128)(2,1)S(1)} reshape(bf16[480,2048]{1,0:T(8,128)(2,1)} %convolution_convert_fusion) | data formatting | bytes 3932160 | tf_op jit(solution)/shard_map/reshape | solution.py:124
  32.6 1.7 %copy.63 = bf16[4,60,2048]{2,0,1:T(4,128)(2,1)} copy(bf16[4,60,2048]{2,1,0:T(8,128)(2,1)S(1)} %slice_bitcast_fusion) | data formatting | bytes 1966080 | tf_op jit(solution)/shard_map/squeeze | solution.py:125
  34.9 2.2 %collective-permute-done.4 = bf16[4,60,2048]{2,0,1:T(4,128)(2,1)S(1)} collective-permute-done((bf16[4,60,2048]{2,0,1:T(4,128)(2,1)}, bf16[4,60,2048]{2,0,1:T(4,128)(2,1)S(1)}, u32[]{:S(2)}, u32[]{:S(2)}) %collective-permute-start.4) | collective-permute-done | bytes 983072 | tf_op jit(solution)/shard_map/ppermute | solution.py:28
  37.1 1.4 fusion.77
  38.7 4.7 %fusion.16 = f32[120,1408]{1,0:T(8,128)S(1)} fusion(bf16[1,1408,2048]{2,1,0:T(8,128)(2,1)} %param.17, bf16[60,2048]{1,0:T(8,128)(2,1)S(1)} %bitcast.100, bf16[60,2048]{1,0:T(8,128)(2,1)S(1)} %get-tuple-element.12), kind=kOutput, calls=%fused_computation.16 | convolution fusion | flops 693043200 | bytes 6934528 | tf_op jit(solution)/shard_map/dot_general | solution.py:17
  43.6 2.0 %constant_dynamic-update-slice_fusion.17 = (bf16[120,5632]{1,0:T(8,128)(2,1)S(1)}, bf16[120,1408]{1,0:T(8,128)(2,1)S(1)}) fusion(bf16[120,5632]{1,0:T(8,128)(2,1)S(1)} %broadcast.148.clone, s32[]{:T(128)S(6)} %select_n.76, bf16[1,1408,2048]{2,1,0:T(8,128)(2,1)S(1)} %bitcast.110, bf16[60,2048]{1,0:T(8,128)(2,1)S(1)} %bitcast.101, ...), kind=kOutput, calls=%fused_computation.108 | convolution fusion | flops 694056960 | bytes 7643140 | tf_op jit(solution)/shard_map/dot_general | solution.py:17
  45.6 1.3 collective-permute-start.5
  46.8 3.0 %collective-permute-start.6 = (bf16[120,1408]{1,0:T(8,128)(2,1)S(1)}, bf16[120,1408]{1,0:T(8,128)(2,1)S(1)}, u32[]{:S(2)}, u32[]{:S(2)}) collective-permute-start(bf16[120,1408]{1,0:T(8,128)(2,1)S(1)} %get-tuple-element.31), channel_id=1, source_target_pairs={{0,3},{1,0},{2,1},{3,2},{4,7},{5,4},{6,5},{7,6},{8,11},{9,8},{10,9... | collective-permute-start | bytes 1013768 | tf_op jit(solution)/shard_map/ppermute | solution.py:24
  50.1 2.5 %collective-permute-start.17 = (bf16[120,2048]{1,0:T(8,128)(2,1)S(1)}, bf16[120,2048]{1,0:T(8,128)(2,1)S(1)}, u32[]{:S(2)}, u32[]{:S(2)}) collective-permute-start(bf16[120,2048]{1,0:T(8,128)(2,1)S(1)} %pad_maximum_fusion.5), channel_id=1, source_target_pairs={{0,24},{4,28},{8,16},{12,20},{16,8},{20,12},{24,0},{28,4},{1,25},{... | collective-permute-start | bytes 1474568 | tf_op jit(solution)/shard_map/ppermute | solution.py:28
  53.6 0.6 collective-permute-start.9
  54.2 4.3 %collective-permute-done.5 = bf16[120,1408]{1,0:T(8,128)(2,1)S(1)} collective-permute-done((bf16[120,1408]{1,0:T(8,128)(2,1)S(1)}, bf16[120,1408]{1,0:T(8,128)(2,1)S(1)}, u32[]{:S(2)}, u32[]{:S(2)}) %collective-permute-start.5) | collective-permute-done | bytes 337952 | tf_op jit(solution)/shard_map/ppermute | solution.py:24
  58.7 5.1 %collective-permute-done.6 = bf16[120,1408]{1,0:T(8,128)(2,1)S(1)} collective-permute-done((bf16[120,1408]{1,0:T(8,128)(2,1)S(1)}, bf16[120,1408]{1,0:T(8,128)(2,1)S(1)}, u32[]{:S(2)}, u32[]{:S(2)}) %collective-permute-start.6) | collective-permute-done | bytes 337952 | tf_op jit(solution)/shard_map/ppermute | solution.py:24
  63.8 3.6 %collective-permute-start.8 = (bf16[56,1408]{1,0:T(8,128)(2,1)S(1)}, bf16[56,1408]{1,0:T(8,128)(2,1)S(1)}, u32[]{:S(2)}, u32[]{:S(2)}) collective-permute-start(bf16[56,1408]{1,0:T(8,128)(2,1)S(1)} %slice.121), channel_id=1, source_target_pairs={{0,3},{1,0},{2,1},{3,2},{4,7},{5,4},{6,5},{7,6},{8,11},{9,8},{10,9... | collective-permute-start | bytes 473096 | tf_op jit(solution)/shard_map/ppermute | solution.py:24
  68.0 1.9 %fusion.12 = f32[120,1408]{1,0:T(8,128)S(1)} fusion(bf16[120,2048]{1,0:T(8,128)(2,1)S(1)} %collective-permute-done.17, bf16[1,1408,2048]{2,1,0:T(8,128)(2,1)S(1)} %bitcast.97), kind=kOutput, calls=%fused_computation.12 | convolution fusion | flops 692060160 | bytes 6934528 | tf_op jit(solution)/shard_map/dot_general | solution.py:17
  70.1 2.7 %constant_dynamic-update-slice_fusion.9 = (bf16[120,5632]{1,0:T(8,128)(2,1)S(1)}, bf16[120,1408]{1,0:T(8,128)(2,1)}) fusion(bf16[120,5632]{1,0:T(8,128)(2,1)S(1)} %broadcast.148.clone.1, s32[]{:T(128)S(6)} %select_n.76, f32[120,1408]{1,0:T(8,128)S(1)} %fusion.12, bf16[120,2048]{1,0:T(8,128)(2,1)S(1)} %collective-permute-done.17, ...), kind=kOutput, calls=%fused_computation.99 | convolution fusion | flops 693073920 | bytes 7610372 | tf_op jit(solution)/shard_map/dot_general | solution.py:17
  72.8 4.7 %collective-permute-done.9 = bf16[120,2048]{1,0:T(8,128)(2,1)S(1)} collective-permute-done((bf16[120,2048]{1,0:T(8,128)(2,1)S(1)}, bf16[120,2048]{1,0:T(8,128)(2,1)S(1)}, u32[]{:S(2)}, u32[]{:S(2)}) %collective-permute-start.9) | collective-permute-done | bytes 491552 | tf_op jit(solution)/shard_map/ppermute | solution.py:28
  77.5 1.7 collective-permute-start.19
  79.3 1.8 %fusion.14 = f32[240,1408]{1,0:T(8,128)S(1)} fusion(bf16[240,2048]{1,0:T(8,128)(2,1)S(1)} %constant_dynamic-update-slice_fusion, bf16[1,1408,2048]{2,1,0:T(8,128)(2,1)S(1)} %bitcast.97), kind=kOutput, calls=%fused_computation.14 | convolution fusion | flops 1384120320 | bytes 8101888 | tf_op jit(solution)/shard_map/dot_general | solution.py:17
  81.1 2.9 %multiply_convert_fusion = bf16[240,1408]{1,0:T(8,128)(2,1)} fusion(f32[240,1408]{1,0:T(8,128)S(1)} %fusion.14, bf16[240,2048]{1,0:T(8,128)(2,1)S(1)} %constant_dynamic-update-slice_fusion, bf16[1,1408,2048]{2,1,0:T(8,128)(2,1)S(1)} %bitcast.110), kind=kOutput, calls=%fused_computation.25 | convolution fusion | flops 1386147840 | bytes 8777728 | tf_op jit(solution)/shard_map/dot_general | solution.py:17
  84.0 2.6 %fusion.28 = f32[160,16]{0,1:T(8,128)S(1)} fusion(bf16[64,16,512]{2,1,0:T(8,128)(2,1)} %bitcast.111, f32[160,64]{0,1:T(8,128)S(1)} %get-tuple-element.29, bf16[160,2048]{1,0:T(8,128)(2,1)} %copy-done.1, s32[]{:T(128)S(6)} %select_n.81), kind=kOutput, calls=%fused_computation.30 | convolution fusion | flops 168097280 | bytes 1263620 | tf_op jit(solution)/shard_map/dot_general | solution.py:139
  87.2 0.9 copy-done.2
  88.6 3.5 %collective-permute-start.12 = (bf16[248,1408]{1,0:T(8,128)(2,1)S(1)}, bf16[248,1408]{1,0:T(8,128)(2,1)S(1)}, u32[]{:S(2)}, u32[]{:S(2)}) collective-permute-start(bf16[248,1408]{1,0:T(8,128)(2,1)S(1)} %get-tuple-element.17), channel_id=1, source_target_pairs={{0,3},{1,0},{2,1},{3,2},{4,7},{5,4},{6,5},{7,6},{8,11},{9,8},{10,9... | collective-permute-start | bytes 2095112 | tf_op jit(solution)/shard_map/ppermute | solution.py:24
  92.2 3.9 %collective-permute-start.21 = (bf16[56,1408]{1,0:T(8,128)(2,1)S(1)}, bf16[56,1408]{1,0:T(8,128)(2,1)S(1)}, u32[]{:S(2)}, u32[]{:S(2)}) collective-permute-start(bf16[56,1408]{1,0:T(8,128)(2,1)S(1)} %slice.134), channel_id=1, source_target_pairs={{0,3},{1,0},{2,1},{3,2},{4,7},{5,4},{6,5},{7,6},{8,11},{9,8},{10,9... | collective-permute-start | bytes 473096 | tf_op jit(solution)/shard_map/ppermute | solution.py:24
  96.2 30.6 %collective-permute-done.20 = bf16[64,1408]{1,0:T(8,128)(2,1)S(1)} collective-permute-done((bf16[64,1408]{1,0:T(8,128)(2,1)S(1)}, bf16[64,1408]{1,0:T(8,128)(2,1)S(1)}, u32[]{:S(2)}, u32[]{:S(2)}) %collective-permute-start.20) | collective-permute-done | bytes 180256 | tf_op jit(solution)/shard_map/ppermute | solution.py:24
  127.3 3.7 %fusion.40 = bf16[120,512]{1,0:T(8,128)(2,1)S(1)} fusion(bf16[120,5632]{1,0:T(8,128)(2,1)S(1)} %constant_dynamic-update-slice_fusion.22, bf16[1,5632,512]{2,1,0:T(8,128)(2,1)} %param.19), kind=kOutput, calls=%fused_computation.37 | convolution fusion | flops 692121600 | bytes 7241728 | tf_op jit(solution)/shard_map/dot_general | solution.py:172
  131.0 2.4 %collective-permute-start.22 = (bf16[120,512]{1,0:T(8,128)(2,1)S(1)}, bf16[120,512]{1,0:T(8,128)(2,1)S(1)}, u32[]{:S(2)}, u32[]{:S(2)}) collective-permute-start(bf16[120,512]{1,0:T(8,128)(2,1)S(1)} %fusion.40), channel_id=1, source_target_pairs={{0,24},{4,28},{8,16},{12,20},{16,8},{20,12},{24,0},{28,4},{1,25},{... | collective-permute-start | bytes 368648 | tf_op jit(solution)/shard_map/ppermute | solution.py:28
  133.9 3.6 %collective-permute-start.14 = (bf16[120,1408]{1,0:T(8,128)(2,1)S(1)}, bf16[120,1408]{1,0:T(8,128)(2,1)S(1)}, u32[]{:S(2)}, u32[]{:S(2)}) collective-permute-start(bf16[120,1408]{1,0:T(8,128)(2,1)S(1)} %slice.127), channel_id=1, source_target_pairs={{0,3},{1,0},{2,1},{3,2},{4,7},{5,4},{6,5},{7,6},{8,11},{9,8},{10,9... | collective-permute-start | bytes 1013768 | tf_op jit(solution)/shard_map/ppermute | solution.py:24
  137.7 8.8 %collective-permute-done.13 = bf16[128,1408]{1,0:T(8,128)(2,1)S(1)} collective-permute-done((bf16[128,1408]{1,0:T(8,128)(2,1)S(1)}, bf16[128,1408]{1,0:T(8,128)(2,1)S(1)}, u32[]{:S(2)}, u32[]{:S(2)}) %collective-permute-start.13) | collective-permute-done | bytes 360480 | tf_op jit(solution)/shard_map/ppermute | solution.py:24
  146.6 4.3 %collective-permute-done.14 = bf16[120,1408]{1,0:T(8,128)(2,1)S(1)} collective-permute-done((bf16[120,1408]{1,0:T(8,128)(2,1)S(1)}, bf16[120,1408]{1,0:T(8,128)(2,1)S(1)}, u32[]{:S(2)}, u32[]{:S(2)}) %collective-permute-start.14) | collective-permute-done | bytes 337952 | tf_op jit(solution)/shard_map/ppermute | solution.py:24
  151.0 1.6 fusion.30
  152.7 0.9 collective-permute-start.16
  153.5 0.9 fusion.37
  154.6 3.0 %collective-permute-done.15 = bf16[120,512]{1,0:T(8,128)(2,1)S(1)} collective-permute-done((bf16[120,512]{1,0:T(8,128)(2,1)S(1)}, bf16[120,512]{1,0:T(8,128)(2,1)S(1)}, u32[]{:S(2)}, u32[]{:S(2)}) %collective-permute-start.15) | collective-permute-done | bytes 122912 | tf_op jit(solution)/shard_map/ppermute | solution.py:28
  157.8 0.9 slice.137
  160.4 2.3 %fusion.36 = bf16[160,512]{1,0:T(8,128)(2,1)} fusion(f32[160,512]{1,0:T(8,128)S(1)} %fusion.29, bf16[64,16,512]{2,0,1:T(8,128)(2,1)} %all-gather.5.cloned.1.call-done, bf16[160,16]{0,1:T(8,128)(2,1)S(1)} %copy.73, bf16[160,64]{0,1:T(8,128)(2,1)S(1)} %get-tuple-element.28), kind=kOutput, calls=%fused_computation.35 | convolution fusion | flops 168099840 | bytes 1565696 | tf_op jit(solution)/shard_map/dot_general | solution.py:183
  (145 shorter events, 9.3 us)
Async XLA Ops:
  6.5 7.8 %copy-start.3 = (bf16[8,16,512]{2,1,0:T(8,128)(2,1)S(1)}, bf16[8,16,512]{2,1,0:T(8,128)(2,1)}, u32[]{:S(2)}) copy-start(bf16[8,16,512]{2,1,0:T(8,128)(2,1)} %param.21) | copy-start | bytes 393220
  6.5 8.6 %copy-start.4 = (s32[160,2]{0,1:T(2,128)S(1)}, s32[160,2]{0,1:T(2,128)}, u32[]{:S(2)}) copy-start(s32[160,2]{0,1:T(2,128)} %param.15) | copy-start | bytes 3844
  6.5 77.5 %all-gather.3.cloned.1.call-start = ((), (), s32[]{:S(2)}) async-start(), calls=%async_computation | async-start | bytes 1179648 | tf_op jit(solution)/shard_map/all_gather | solution.py:89
  7.3 153.2 %all-gather.5.cloned.1.call-start = ((), (), s32[]{:S(2)}) async-start(), calls=%async_computation.1 | async-start | bytes 1179648 | tf_op jit(solution)/shard_map/all_gather | solution.py:90
  9.2 10.5 %collective-permute-start = (bf16[176,512]{1,0:T(8,128)(2,1)S(1)}, bf16[176,512]{1,0:T(8,128)(2,1)S(1)}, u32[]{:S(2)}, u32[]{:S(2)}) collective-permute-start(bf16[176,512]{1,0:T(8,128)(2,1)S(1)} %get-tuple-element.23), channel_id=1, source_target_pairs={{0,1},{1,2},{2,3},{3,0},{4,5},{5,6},{6,7},{7,4},{8,9},{9,10},{10,1... | collective-permute-start | bytes 540680 | tf_op jit(solution)/shard_map/ppermute | solution.py:24
  12.2 9.9 %collective-permute-start.1 = (bf16[176,512]{1,0:T(8,128)(2,1)S(1)}, bf16[176,512]{1,0:T(8,128)(2,1)S(1)}, u32[]{:S(2)}, u32[]{:S(2)}) collective-permute-start(bf16[176,512]{1,0:T(8,128)(2,1)S(1)} %get-tuple-element.23), channel_id=1, source_target_pairs={{0,3},{1,0},{2,1},{3,2},{4,7},{5,4},{6,5},{7,6},{8,11},{9,8},{10,9... | collective-permute-start | bytes 540680 | tf_op jit(solution)/shard_map/ppermute | solution.py:24
  19.7 7.0 %collective-permute-start.2 = (bf16[88,512]{1,0:T(8,128)(2,1)S(1)}, bf16[88,512]{1,0:T(8,128)(2,1)S(1)}, u32[]{:S(2)}, u32[]{:S(2)}) collective-permute-start(bf16[88,512]{1,0:T(8,128)(2,1)S(1)} %slice.113), channel_id=1, source_target_pairs={{0,1},{1,2},{2,3},{3,0},{4,5},{5,6},{6,7},{7,4},{8,9},{9,10},{10,1... | collective-permute-start | bytes 270344 | tf_op jit(solution)/shard_map/ppermute | solution.py:24
  22.1 5.3 %collective-permute-start.3 = (bf16[88,512]{1,0:T(8,128)(2,1)S(1)}, bf16[88,512]{1,0:T(8,128)(2,1)S(1)}, u32[]{:S(2)}, u32[]{:S(2)}) collective-permute-start(bf16[88,512]{1,0:T(8,128)(2,1)S(1)} %slice.114), channel_id=1, source_target_pairs={{0,3},{1,0},{2,1},{3,2},{4,7},{5,4},{6,5},{7,6},{8,11},{9,8},{10,9... | collective-permute-start | bytes 270344 | tf_op jit(solution)/shard_map/ppermute | solution.py:24
  27.9 0.8 copy-start.1
  32.6 1.8 %copy-start.5 = (s32[16]{0:T(128)S(1)}, s32[16]{0:T(128)}, u32[]{:S(2)}) copy-start(s32[16]{0:T(128)} %param.13) | copy-start | bytes 196
  32.6 2.1 %copy-start.6 = (s32[16]{0:T(128)S(1)}, s32[16]{0:T(128)}, u32[]{:S(2)}) copy-start(s32[16]{0:T(128)} %param.14) | copy-start | bytes 196
  34.3 2.8 %collective-permute-start.4 = (bf16[4,60,2048]{2,0,1:T(4,128)(2,1)}, bf16[4,60,2048]{2,0,1:T(4,128)(2,1)S(1)}, u32[]{:S(2)}, u32[]{:S(2)}) collective-permute-start(bf16[4,60,2048]{2,0,1:T(4,128)(2,1)} %copy.63), channel_id=1, source_target_pairs={{0,4},{4,0},{8,12},{12,8},{16,20},{20,16},{24,28},{28,24},{1,5},{5... | collective-permute-start | bytes 2949128 | tf_op jit(solution)/shard_map/ppermute | solution.py:28
  37.1 6.4 %slice-start.4 = ((s8[5767168]{0:T(1024)(128)(4,1)}), s8[4194304]{0:T(1024)(128)(4,1)S(1)}, s32[]{:S(2)}) async-start(s8[5767168]{0:T(1024)(128)(4,1)} %bitcast.109), calls=%async_computation.6 | async-start | bytes 8388608
  38.7 4.8 %slice-start.5 = ((s8[5767168]{0:T(1024)(128)(4,1)}), s8[1572864]{0:T(1024)(128)(4,1)S(1)}, s32[]{:S(2)}) async-start(s8[5767168]{0:T(1024)(128)(4,1)} %bitcast.109), calls=%async_computation.7 | async-start | bytes 3145728
  43.4 24.6 %slice-start = ((s8[5767168]{0:T(1024)(128)(4,1)}), s8[4194304]{0:T(1024)(128)(4,1)S(1)}, s32[]{:S(2)}) async-start(s8[5767168]{0:T(1024)(128)(4,1)} %bitcast.96), calls=%async_computation.2 | async-start | bytes 8388608
  43.5 24.5 %slice-start.1 = ((s8[5767168]{0:T(1024)(128)(4,1)}), s8[1572864]{0:T(1024)(128)(4,1)S(1)}, s32[]{:S(2)}) async-start(s8[5767168]{0:T(1024)(128)(4,1)} %bitcast.96), calls=%async_computation.3 | async-start | bytes 3145728
  45.6 13.0 %collective-permute-start.5 = (bf16[120,1408]{1,0:T(8,128)(2,1)S(1)}, bf16[120,1408]{1,0:T(8,128)(2,1)S(1)}, u32[]{:S(2)}, u32[]{:S(2)}) collective-permute-start(bf16[120,1408]{1,0:T(8,128)(2,1)S(1)} %get-tuple-element.31), channel_id=1, source_target_pairs={{0,1},{1,2},{2,3},{3,0},{4,5},{5,6},{6,7},{7,4},{8,9},{9,10},{10,1... | collective-permute-start | bytes 1013768 | tf_op jit(solution)/shard_map/ppermute | solution.py:24
  46.8 16.9 %collective-permute-start.6 = (bf16[120,1408]{1,0:T(8,128)(2,1)S(1)}, bf16[120,1408]{1,0:T(8,128)(2,1)S(1)}, u32[]{:S(2)}, u32[]{:S(2)}) collective-permute-start(bf16[120,1408]{1,0:T(8,128)(2,1)S(1)} %get-tuple-element.31), channel_id=1, source_target_pairs={{0,3},{1,0},{2,1},{3,2},{4,7},{5,4},{6,5},{7,6},{8,11},{9,8},{10,9... | collective-permute-start | bytes 1013768 | tf_op jit(solution)/shard_map/ppermute | solution.py:24
  50.1 17.9 %collective-permute-start.17 = (bf16[120,2048]{1,0:T(8,128)(2,1)S(1)}, bf16[120,2048]{1,0:T(8,128)(2,1)S(1)}, u32[]{:S(2)}, u32[]{:S(2)}) collective-permute-start(bf16[120,2048]{1,0:T(8,128)(2,1)S(1)} %pad_maximum_fusion.5), channel_id=1, source_target_pairs={{0,24},{4,28},{8,16},{12,20},{16,8},{20,12},{24,0},{28,4},{1,25},{... | collective-permute-start | bytes 1474568 | tf_op jit(solution)/shard_map/ppermute | solution.py:28
  52.9 26.4 %collective-permute-start.10 = (bf16[120,2048]{1,0:T(8,128)(2,1)S(1)}, bf16[120,2048]{1,0:T(8,128)(2,1)S(1)}, u32[]{:S(2)}, u32[]{:S(2)}) collective-permute-start(bf16[120,2048]{1,0:T(8,128)(2,1)S(1)} %pad_maximum_fusion.4), channel_id=1, source_target_pairs={{0,16},{4,20},{8,24},{12,28},{16,0},{20,4},{24,8},{28,12},{1,17},{... | collective-permute-start | bytes 1474568 | tf_op jit(solution)/shard_map/ppermute | solution.py:28
  53.6 23.8 %collective-permute-start.9 = (bf16[120,2048]{1,0:T(8,128)(2,1)S(1)}, bf16[120,2048]{1,0:T(8,128)(2,1)S(1)}, u32[]{:S(2)}, u32[]{:S(2)}) collective-permute-start(bf16[120,2048]{1,0:T(8,128)(2,1)S(1)} %pad_maximum_fusion.3), channel_id=1, source_target_pairs={{0,8},{4,12},{8,0},{12,4},{16,24},{20,28},{24,16},{28,20},{1,9},{5... | collective-permute-start | bytes 1474568 | tf_op jit(solution)/shard_map/ppermute | solution.py:28
  58.6 25.4 %collective-permute-start.7 = (bf16[64,1408]{1,0:T(8,128)(2,1)S(1)}, bf16[64,1408]{1,0:T(8,128)(2,1)S(1)}, u32[]{:S(2)}, u32[]{:S(2)}) collective-permute-start(bf16[64,1408]{1,0:T(8,128)(2,1)S(1)} %slice.120), channel_id=1, source_target_pairs={{0,1},{1,2},{2,3},{3,0},{4,5},{5,6},{6,7},{7,4},{8,9},{9,10},{10,1... | collective-permute-start | bytes 540680 | tf_op jit(solution)/shard_map/ppermute | solution.py:24
  63.8 20.2 %collective-permute-start.8 = (bf16[56,1408]{1,0:T(8,128)(2,1)S(1)}, bf16[56,1408]{1,0:T(8,128)(2,1)S(1)}, u32[]{:S(2)}, u32[]{:S(2)}) collective-permute-start(bf16[56,1408]{1,0:T(8,128)(2,1)S(1)} %slice.121), channel_id=1, source_target_pairs={{0,3},{1,0},{2,1},{3,2},{4,7},{5,4},{6,5},{7,6},{8,11},{9,8},{10,9... | collective-permute-start | bytes 473096 | tf_op jit(solution)/shard_map/ppermute | solution.py:24
  72.8 19.3 %collective-permute-start.18 = (bf16[120,1408]{1,0:T(8,128)(2,1)}, bf16[120,1408]{1,0:T(8,128)(2,1)S(1)}, u32[]{:S(2)}, u32[]{:S(2)}) collective-permute-start(bf16[120,1408]{1,0:T(8,128)(2,1)} %get-tuple-element.6), channel_id=1, source_target_pairs={{0,1},{1,2},{2,3},{3,0},{4,5},{5,6},{6,7},{7,4},{8,9},{9,10},{10,1... | collective-permute-start | bytes 1013768 | tf_op jit(solution)/shard_map/ppermute | solution.py:24
  77.5 14.7 %collective-permute-start.19 = (bf16[120,1408]{1,0:T(8,128)(2,1)}, bf16[120,1408]{1,0:T(8,128)(2,1)S(1)}, u32[]{:S(2)}, u32[]{:S(2)}) collective-permute-start(bf16[120,1408]{1,0:T(8,128)(2,1)} %get-tuple-element.6), channel_id=1, source_target_pairs={{0,3},{1,0},{2,1},{3,2},{4,7},{5,4},{6,5},{7,6},{8,11},{9,8},{10,9... | collective-permute-start | bytes 1013768 | tf_op jit(solution)/shard_map/ppermute | solution.py:24
  87.0 1.1 copy-start.2
  88.2 45.1 %collective-permute-start.11 = (bf16[248,1408]{1,0:T(8,128)(2,1)S(1)}, bf16[248,1408]{1,0:T(8,128)(2,1)S(1)}, u32[]{:S(2)}, u32[]{:S(2)}) collective-permute-start(bf16[248,1408]{1,0:T(8,128)(2,1)S(1)} %get-tuple-element.17), channel_id=1, source_target_pairs={{0,1},{1,2},{2,3},{3,0},{4,5},{5,6},{6,7},{7,4},{8,9},{9,10},{10,1... | collective-permute-start | bytes 2095112 | tf_op jit(solution)/shard_map/ppermute | solution.py:24
  88.6 45.3 %collective-permute-start.12 = (bf16[248,1408]{1,0:T(8,128)(2,1)S(1)}, bf16[248,1408]{1,0:T(8,128)(2,1)S(1)}, u32[]{:S(2)}, u32[]{:S(2)}) collective-permute-start(bf16[248,1408]{1,0:T(8,128)(2,1)S(1)} %get-tuple-element.17), channel_id=1, source_target_pairs={{0,3},{1,0},{2,1},{3,2},{4,7},{5,4},{6,5},{7,6},{8,11},{9,8},{10,9... | collective-permute-start | bytes 2095112 | tf_op jit(solution)/shard_map/ppermute | solution.py:24
  92.1 34.6 %collective-permute-start.20 = (bf16[64,1408]{1,0:T(8,128)(2,1)S(1)}, bf16[64,1408]{1,0:T(8,128)(2,1)S(1)}, u32[]{:S(2)}, u32[]{:S(2)}) collective-permute-start(bf16[64,1408]{1,0:T(8,128)(2,1)S(1)} %slice.133), channel_id=1, source_target_pairs={{0,1},{1,2},{2,3},{3,0},{4,5},{5,6},{6,7},{7,4},{8,9},{9,10},{10,1... | collective-permute-start | bytes 540680 | tf_op jit(solution)/shard_map/ppermute | solution.py:24
  92.2 35.0 %collective-permute-start.21 = (bf16[56,1408]{1,0:T(8,128)(2,1)S(1)}, bf16[56,1408]{1,0:T(8,128)(2,1)S(1)}, u32[]{:S(2)}, u32[]{:S(2)}) collective-permute-start(bf16[56,1408]{1,0:T(8,128)(2,1)S(1)} %slice.134), channel_id=1, source_target_pairs={{0,3},{1,0},{2,1},{3,2},{4,7},{5,4},{6,5},{7,6},{8,11},{9,8},{10,9... | collective-permute-start | bytes 473096 | tf_op jit(solution)/shard_map/ppermute | solution.py:24
  96.1 54.8 %slice-start.2 = ((s8[5767168]{0:T(1024)(128)(4,1)}), s8[4194304]{0:T(1024)(128)(4,1)S(1)}, s32[]{:S(2)}) async-start(s8[5767168]{0:T(1024)(128)(4,1)} %bitcast.98), calls=%async_computation.4 | async-start | bytes 8388608
  127.2 23.7 %slice-start.3 = ((s8[5767168]{0:T(1024)(128)(4,1)}), s8[1572864]{0:T(1024)(128)(4,1)S(1)}, s32[]{:S(2)}) async-start(s8[5767168]{0:T(1024)(128)(4,1)} %bitcast.98), calls=%async_computation.5 | async-start | bytes 3145728
  131.0 23.6 %collective-permute-start.22 = (bf16[120,512]{1,0:T(8,128)(2,1)S(1)}, bf16[120,512]{1,0:T(8,128)(2,1)S(1)}, u32[]{:S(2)}, u32[]{:S(2)}) collective-permute-start(bf16[120,512]{1,0:T(8,128)(2,1)S(1)} %fusion.40), channel_id=1, source_target_pairs={{0,24},{4,28},{8,16},{12,20},{16,8},{20,12},{24,0},{28,4},{1,25},{... | collective-permute-start | bytes 368648 | tf_op jit(solution)/shard_map/ppermute | solution.py:28
  133.4 13.2 %collective-permute-start.13 = (bf16[128,1408]{1,0:T(8,128)(2,1)S(1)}, bf16[128,1408]{1,0:T(8,128)(2,1)S(1)}, u32[]{:S(2)}, u32[]{:S(2)}) collective-permute-start(bf16[128,1408]{1,0:T(8,128)(2,1)S(1)} %slice.126), channel_id=1, source_target_pairs={{0,1},{1,2},{2,3},{3,0},{4,5},{5,6},{6,7},{7,4},{8,9},{9,10},{10,1... | collective-permute-start | bytes 1081352 | tf_op jit(solution)/shard_map/ppermute | solution.py:24
  133.9 17.0 %collective-permute-start.14 = (bf16[120,1408]{1,0:T(8,128)(2,1)S(1)}, bf16[120,1408]{1,0:T(8,128)(2,1)S(1)}, u32[]{:S(2)}, u32[]{:S(2)}) collective-permute-start(bf16[120,1408]{1,0:T(8,128)(2,1)S(1)} %slice.127), channel_id=1, source_target_pairs={{0,3},{1,0},{2,1},{3,2},{4,7},{5,4},{6,5},{7,6},{8,11},{9,8},{10,9... | collective-permute-start | bytes 1013768 | tf_op jit(solution)/shard_map/ppermute | solution.py:24
  151.0 1.6 copy-start
  152.6 4.9 %collective-permute-start.15 = (bf16[120,512]{1,0:T(8,128)(2,1)S(1)}, bf16[120,512]{1,0:T(8,128)(2,1)S(1)}, u32[]{:S(2)}, u32[]{:S(2)}) collective-permute-start(bf16[120,512]{1,0:T(8,128)(2,1)S(1)} %get-tuple-element.22), channel_id=1, source_target_pairs={{0,8},{4,12},{8,0},{12,4},{16,24},{20,28},{24,16},{28,20},{1,9},{5... | collective-permute-start | bytes 368648 | tf_op jit(solution)/shard_map/ppermute | solution.py:28
  152.7 4.9 %collective-permute-start.16 = (bf16[120,512]{1,0:T(8,128)(2,1)S(1)}, bf16[120,512]{1,0:T(8,128)(2,1)S(1)}, u32[]{:S(2)}, u32[]{:S(2)}) collective-permute-start(bf16[120,512]{1,0:T(8,128)(2,1)S(1)} %get-tuple-element.21), channel_id=1, source_target_pairs={{0,16},{4,20},{8,24},{12,28},{16,0},{20,4},{24,8},{28,12},{1,17},{... | collective-permute-start | bytes 368648 | tf_op jit(solution)/shard_map/ppermute | solution.py:28
  157.7 1.6 collective-permute-start.23
  159.3 0.7 copy-start.7
Sparse Core Ops, SparseCore 0:
  9.2 27.0 all-gather.2
  38.2 33.2 all-gather.4

commit v2 on v1

v2 whole, which is shorter than its diff:
```python
import jax
import jax.numpy as jnp
from jax import lax
from jax.sharding import PartitionSpec as P

D = 2048
EXPERTS = 8
TOPK = 2
RANK = 16
CAP = 60
GAIN_ROWS = 16
SLOTS = 64
AHEAD = (0, 1, 0)


def contract_last(left, right):
    return lax.dot_general(
        left, right, (((1,), (1,)), ((), ())), preferred_element_type=jnp.float32
    )


def col_shift(value, by):
    size = lax.axis_size("col")
    return lax.ppermute(value, "col", [(i, (i + by) % size) for i in range(size)])


def row_xor(value, by):
    return lax.ppermute(value, "row", [(i, i ^ by) for i in range(lax.axis_size("row"))])


def along(value, pairs):
    return lax.ppermute(value, "col", pairs)


BESIDE = [(0, 1), (1, 0), (2, 3), (3, 2)]
MIRROR = [(0, 3), (1, 2), (2, 1), (3, 0)]
OVER = [(0, 2), (3, 1)]
OUTWARD = [(1, 0), (2, 3)]


def first_hops(value):
    return along(value, MIRROR), along(value, BESIDE), along(value, OVER)


def in_line(value, mirror, beside, over, passed):
    here = lax.axis_index("col")
    return side_by_side(
        value, [(here ^ 1, 0, beside), (here ^ 3, 0, mirror), (here ^ 2, 0, over + passed)]
    )


def ring_gather(value):
    size = lax.axis_size("col")
    here = lax.axis_index("col")
    rows = value.shape[0]
    half = -(-rows // 16) * 8
    found = []
    from_left, from_right = value, value
    for hop in range(1, (size + 1) // 2):
        from_left, from_right = col_shift(from_left, 1), col_shift(from_right, -1)
        found += [
            (lax.rem(here + size - hop, size), 0, from_left),
            (lax.rem(here + hop, size), 0, from_right),
        ]
    if size % 2 == 0:
        facing = lax.rem(here + size // 2, size)
        found += [
            (facing, 0, col_shift(from_left[:half], 1)),
            (facing, half, col_shift(from_right[half:], -1)),
        ]
    return found


def side_by_side(value, others):
    rows, width = value.shape
    whole = jnp.zeros((rows, lax.axis_size("col") * width), value.dtype)
    for sender, first, block in [(lax.axis_index("col"), 0, value)] + others:
        whole = lax.dynamic_update_slice(whole, block, (first, sender * width))
    return whole


def col_sum(value):
    size = lax.axis_size("col")
    total = value
    for by in range(1, size):
        total = total + lax.ppermute(value, "col", [(i, i ^ by) for i in range(size)])
    return total


def row_gather_chips(value):
    size = lax.axis_size("row")
    return jnp.stack([value] + [row_xor(value, by) for by in range(2, size, 2)])


def both_cores(stacked):
    both = jnp.stack([stacked, row_xor(stacked, 1)], axis=1)
    return both.reshape((lax.axis_size("row"),) + stacked.shape[1:])


def normalised(features, rows):
    widened = features[:rows].astype(jnp.float32)
    gain = jnp.sum(features[rows : rows + 3].astype(jnp.float32), axis=0)
    scale = lax.rsqrt(jnp.mean(widened * widened, axis=1, keepdims=True) + 1e-06)
    return (widened * scale * gain[None, :]).astype(jnp.bfloat16)


def after(value, *others):
    return lax.optimization_barrier((value,) + others)[0]


def split_float(value, parts):
    pieces = []
    for _ in range(parts):
        piece = lax.reduce_precision(value, 8, 7)
        pieces.append(piece.astype(jnp.bfloat16))
        value = value - piece
    return pieces


def body(
    tokens,
    norm_gain,
    lengths,
    request_adapter,
    routes,
    route_weights,
    gate_weight,
    up_weight,
    down_weight,
    adapter_down,
    adapter_up,
):
    tok_rows, width_part = tokens.shape
    rows_axis, cols_axis = lax.axis_size("row"), lax.axis_size("col")
    row_at, col_at = lax.axis_index("row"), lax.axis_index("col")
    splits = rows_axis // EXPERTS
    chips = rows_axis // 2
    unit_gate, unit_up, unit_down = gate_weight[0], up_weight[0], down_weight[0]
    hidden_part = unit_gate.shape[0]
    line = cols_axis == 4

    gain_parts = jnp.stack(split_float(norm_gain, 3))
    sent = jnp.concatenate(
        [tokens, jnp.pad(gain_parts, ((0, GAIN_ROWS - 3), (0, 0)))], axis=0
    )
    if line:
        mirror, beside, over = first_hops(sent)
        features = in_line(sent, mirror, beside, over, along(mirror, OUTWARD))
    else:
        features = side_by_side(sent, ring_gather(sent))
    normed = normalised(features, tok_rows)

    assigned = routes.reshape(-1)
    assign_count = assigned.shape[0]
    expert_hot = (assigned[:, None] == jnp.arange(EXPERTS, dtype=jnp.int32)[None, :]).astype(
        jnp.bfloat16
    )
    earlier = (
        jnp.arange(assign_count, dtype=jnp.int32)[:, None]
        > jnp.arange(assign_count, dtype=jnp.int32)[None, :]
    ).astype(jnp.bfloat16)
    before = jnp.dot(earlier, expert_hot, preferred_element_type=jnp.float32)
    slot_index = jnp.sum(before * expert_hot.astype(jnp.float32), axis=1).astype(jnp.int32)
    placed_at = assigned * SLOTS + slot_index

    def placing(core, slots):
        place = jnp.arange(chips * slots, dtype=jnp.int32)
        target = row_at ^ (place // slots * 2 + core)
        wanted = (target // splits) * SLOTS + place % slots
        return (wanted[:, None] == placed_at[None, :]).astype(jnp.bfloat16)

    def outgoing(core):
        of_token = jnp.sum(placing(core, SLOTS).reshape(-1, tok_rows, TOPK), axis=2)
        placed = jnp.dot(of_token, normed, preferred_element_type=jnp.float32)
        return placed.astype(jnp.bfloat16).reshape(chips, SLOTS, D)

    partner_half = row_xor(outgoing(1), 1)
    here_half = outgoing(0)

    local_adapters = adapter_down.shape[0]
    mine = jnp.concatenate([jnp.transpose(adapter_down, (0, 2, 1)), adapter_up], axis=0)
    mine = mine.reshape(2 * local_adapters * RANK, width_part)
    by_chip = row_gather_chips(mine)
    groups = [[0], list(range(1, chips - 1)), [chips - 1]]
    pairs = [
        jnp.concatenate([here_half[offset], partner_half[offset]], axis=0)
        for offset in range(chips)
    ]
    for offset in range(1, chips):
        pair = after(pairs[offset], pairs[1]) if offset == chips - 1 else pairs[offset]
        pairs[offset] = row_xor(pair, 2 * offset)

    def hidden_of(offsets, *earlier):
        arrived = jnp.concatenate(
            [
                pairs[offset][first : first + CAP]
                for offset in offsets
                for first in (0, SLOTS)
            ],
            axis=0,
        )
        arrived = after(arrived, *earlier)
        gate_sum = contract_last(arrived, unit_gate)
        up_sum = contract_last(arrived, unit_up)
        return (jax.nn.silu(gate_sum) * up_sum).astype(jnp.bfloat16)

    hidden, hops = [], []
    for offsets in groups:
        hidden.append(hidden_of(offsets))
        hops.append(first_hops(hidden[-1]) if line else ring_gather(hidden[-1]))

    factors = both_cores(after(by_chip, hidden[0]))
    factors = factors.reshape(rows_axis, 2, local_adapters * RANK, width_part)
    down_rows = factors[:, 0].reshape(-1, width_part)
    up_rows = factors[:, 1].reshape(-1, width_part)
    own = lax.dynamic_slice(after(normed, hidden[min(1, len(groups) - 1)]), (0, col_at * width_part), (tok_rows, width_part))
    req_ends = jnp.cumsum(lengths)
    position = row_at * tok_rows + jnp.arange(tok_rows, dtype=jnp.int32)
    request = jnp.sum((position[:, None] >= req_ends[None, :]).astype(jnp.int32), axis=1)
    request_hot = request[:, None] == jnp.arange(lengths.shape[0], dtype=jnp.int32)[None, :]
    adapter = jnp.sum(jnp.where(request_hot, request_adapter[None, :], 0), axis=1)
    adapter_count = local_adapters * rows_axis
    order = jnp.arange(adapter_count, dtype=jnp.int32)
    held = (row_at ^ (order // local_adapters)) * local_adapters + order % local_adapters
    select = (adapter[:, None] == held[None, :]).astype(jnp.float32)
    projected = contract_last(own, down_rows).reshape(tok_rows, adapter_count, RANK)
    partial_low = jnp.sum(projected * select[:, :, None], axis=1)

    low_sum = col_sum(partial_low)
    low_rank = low_sum.astype(jnp.bfloat16)
    expanded = (select.astype(jnp.bfloat16)[:, :, None] * low_rank[:, None, :]).reshape(
        tok_rows, adapter_count * RANK
    )
    branch = jnp.dot(expanded, up_rows, preferred_element_type=jnp.float32)

    def returns(numbers, whole):
        block_out = jnp.dot(whole, unit_down, preferred_element_type=jnp.float32).astype(
            jnp.bfloat16
        )
        offsets = [offset for number in numbers for offset in groups[number]]
        for index, offset in enumerate(offsets):
            piece = block_out[index * 2 * CAP : (index + 1) * 2 * CAP]
            returned[offset] = piece if offset == 0 else row_xor(piece, 2 * offset)
        return block_out

    returned = [None] * chips
    done = branch
    for number, value in enumerate(hidden):
        if line:
            mirror, beside, over = hops[number]
            passed = along(after(mirror, hidden[min(number + AHEAD[number], 2)]), OUTWARD)
            beside, over = after(beside, mirror), after(over, mirror)
            whole = in_line(value, mirror, beside, over, passed)
        else:
            whole = side_by_side(value, hops[number])
        done = returns([number], after(whole, done, hidden[-1]))
    back = jnp.stack(returned)
    taken = sum(
        lax.dot_general(
            placing(core, CAP),
            part.reshape(-1, width_part),
            (((0,), (0,)), ((), ())),
            preferred_element_type=jnp.float32,
        )
        for core, part in ((0, back[:, :CAP]), (1, row_xor(back[:, CAP:], 1)))
    ).reshape(tok_rows, TOPK, width_part)
    weighted = jnp.sum(taken * route_weights[:, :, None], axis=1)
    return (weighted + branch).astype(jnp.bfloat16)


def solution(mesh):
    in_specs = (
        P("row", "col"),
        P("col"),
        P(),
        P(),
        P("row", None),
        P("row", None),
        P("row", "col", None),
        P("row", "col", None),
        P("row", None, "col"),
        P("row", "col", None),
        P("row", None, "col"),
    )
    out_specs = P("row", "col")
    return jax.shard_map(body, mesh=mesh, in_specs=in_specs, out_specs=out_specs, check_vma=False)
```

time: 170 us -> 156 us (0.918)
  between operations: 14.2 us -> 0.85 us
  starting transfers between devices: 37.1 us -> 48.5 us
  matrix products: 29.7 us -> 18.6 us
  local copies, waits for them, and re-layouts: 12.1 us -> 5.05 us
  other arithmetic: 3.43 us -> 6.8 us
  waiting for transfers between devices: 73.1 us -> 75.5 us
    dot_general x7 -> x8, matrix products: 13.5 us -> 5.44 us  [the longest x3 3.43 us: returns(): jnp.dot(whole, unit_down, preferred_element_type=jnp.float32)]
    ppermute x8 -> x12, starting transfers between devices: 7.06 us -> 12.9 us  [row_xor(): lax.ppermute(value, 'row', [(i, i ^ by) for i in range(lax.axis_size('row...]
    ppermute x16 -> x19, starting transfers between devices: 30 us -> 35.6 us  [the longest x16 33.8 us: along(): return lax.ppermute(value, 'col', pairs)]
    ppermute x8 -> x12, waiting for transfers between devices: 10.6 us -> 14.3 us  [row_xor(): lax.ppermute(value, 'row', [(i, i ^ by) for i in range(lax.axis_size('row...]
    dot_general x6 -> x7, matrix products: 16 us -> 13 us  [contract_last(): lax.dot_general(left, right, (((1,), (1,)), ((), ())), preferred_element_...]
    unnamed x40 -> x22, local copies, waits for them, and re-layouts: 3.84 us -> 0.95 us
    slice x11 -> x9, local copies, waits for them, and re-layouts: 2.48 us -> 0.46 us  [the longest x1 0.17 us: body(): up_rows = factors[:, 1].reshape(-1, width_part)]
    squeeze x3 -> x1, local copies, waits for them, and re-layouts: 1.92 us -> 0.07 us  [body(): partner_half[offset]]
  transfers between devices with their start and end apart: 26 -> 31, of which waited for: 15 -> 16; matrix products, arithmetic and copies ran while one was open for 24% -> 12% of each run, Pallas kernels for 0% -> 0%
where the time goes in v2:
time: 156 us; the launch traced here: 155 us
  waiting for transfers between devices  75.5 us (48%)
  starting transfers between devices  48.5 us (31%)
  matrix products  18.6 us (12%)
  other arithmetic  6.8 us (4%)
  local copies, waits for them, and re-layouts  5.05 us (3%)
    ppermute x16, waiting for transfers between devices, along(): return lax.ppermute(value, 'col', pairs)  49.3 us
    ppermute x16, starting transfers between devices, along(): return lax.ppermute(value, 'col', pairs)  33.8 us
    ppermute x12, waiting for transfers between devices, row_xor(): lax.ppermute(value, 'row', [(i, i ^ by) for i in range(lax.axis_size('row...  14.3 us
    dot_general x7, matrix products, contract_last(): lax.dot_general(left, right, (((1,), (1,)), ((), ())), preferred_element_...  13 us
    ppermute x12, starting transfers between devices, row_xor(): lax.ppermute(value, 'row', [(i, i ^ by) for i in range(lax.axis_size('row...  12.9 us
    ppermute x3, waiting for transfers between devices, col_sum(): lax.ppermute(value, 'col', [(i, i ^ by) for i in range(size)])  11.9 us
    dot_general x3, matrix products, returns(): jnp.dot(whole, unit_down, preferred_element_type=jnp.float32)  3.43 us
  transfers between devices with their start and end apart: 31, of which 16 were waited for; matrix products, arithmetic and copies ran while one was open for 12% of the time, Pallas kernels for 0%

profile of v2, /device:TPU:0, one launch (start us, length us, event | category | flops | bytes accessed | tf_op | source)
XLA Modules:
  0.0 155.4 jit_solution(6613845003212188430)
XLA Ops:
  0.9 1.1 pad_maximum_fusion.10
  1.9 3.1 %collective-permute-start = (bf16[176,512]{1,0:T(8,128)(2,1)S(1)}, bf16[176,512]{1,0:T(8,128)(2,1)}, u32[]{:S(2)}, u32[]{:S(2)}) collective-permute-start(bf16[176,512]{1,0:T(8,128)(2,1)S(1)} %get-tuple-element.55), channel_id=1, source_target_pairs={{0,1},{1,0},{2,3},{3,2},{4,5},{5,4},{6,7},{7,6},{8,9},{9,8},{10,11... | collective-permute-start | bytes 540680 | tf_op jit(solution)/shard_map/ppermute | solution.py:32
  5.0 2.5 %collective-permute-start.1 = (bf16[176,512]{1,0:T(8,128)(2,1)S(1)}, bf16[176,512]{1,0:T(8,128)(2,1)}, u32[]{:S(2)}, u32[]{:S(2)}) collective-permute-start(bf16[176,512]{1,0:T(8,128)(2,1)S(1)} %get-tuple-element.55), channel_id=1, source_target_pairs={{0,3},{1,2},{2,1},{3,0},{4,7},{5,6},{6,5},{7,4},{8,11},{9,10},{10,... | collective-permute-start | bytes 540680 | tf_op jit(solution)/shard_map/ppermute | solution.py:32
  7.5 2.0 %collective-permute-start.2 = (bf16[176,512]{1,0:T(8,128)(2,1)S(1)}, bf16[176,512]{1,0:T(8,128)(2,1)S(1)}, u32[]{:S(2)}, u32[]{:S(2)}) collective-permute-start(bf16[176,512]{1,0:T(8,128)(2,1)S(1)} %get-tuple-element.55), channel_id=1, source_target_pairs={{0,2},{3,1},{4,6},{7,5},{8,10},{11,9},{12,14},{15,13},{16,18},{19,... | collective-permute-start | bytes 540680 | tf_op jit(solution)/shard_map/ppermute | solution.py:32
  9.5 1.0 pad_maximum_fusion.9
  10.5 2.5 %collective-permute-start.13 = (bf16[256,512]{1,0:T(8,128)(2,1)S(1)}, bf16[256,512]{1,0:T(8,128)(2,1)S(1)}, u32[]{:S(2)}, u32[]{:S(2)}) collective-permute-start(bf16[256,512]{1,0:T(8,128)(2,1)S(1)} %bitcast.104), channel_id=1, source_target_pairs={{0,24},{4,28},{8,16},{12,20},{16,8},{20,12},{24,0},{28,4},{1,25},{... | collective-permute-start | bytes 786440 | tf_op jit(solution)/shard_map/ppermute | solution.py:28
  17.0 1.3 collective-permute-start.3
  18.3 0.9 constant_dynamic-update-slice_fusion.10
  19.2 0.9 constant_dynamic-update-slice_fusion.9
  20.2 5.1 %collective-permute-done.3 = bf16[176,512]{1,0:T(8,128)(2,1)S(1)} collective-permute-done((bf16[176,512]{1,0:T(8,128)(2,1)}, bf16[176,512]{1,0:T(8,128)(2,1)S(1)}, u32[]{:S(2)}, u32[]{:S(2)}) %collective-permute-start.3) | collective-permute-done | bytes 180256 | tf_op jit(solution)/shard_map/ppermute | solution.py:32
  27.1 1.8 %collective-permute-done.4 = bf16[4,64,2048]{2,1,0:T(8,128)(2,1)S(1)} collective-permute-done((bf16[4,64,2048]{2,1,0:T(8,128)(2,1)S(1)}, bf16[4,64,2048]{2,1,0:T(8,128)(2,1)S(1)}, u32[]{:S(2)}, u32[]{:S(2)}) %collective-permute-start.4) | collective-permute-done | bytes 1048608 | tf_op jit(solution)/shard_map/ppermute | solution.py:28
  29.1 1.9 %fusion.16 = f32[120,1408]{1,0:T(8,128)S(1)} fusion(bf16[120,2048]{1,0:T(8,128)(2,1)S(1)} %pad_maximum_fusion.6, bf16[1,1408,2048]{2,1,0:T(8,128)(2,1)S(1)} %bitcast.94), kind=kOutput, calls=%fused_computation.16 | convolution fusion | flops 692060160 | bytes 6934528 | tf_op jit(solution)/shard_map/dot_general | solution.py:17
  31.2 2.0 %constant_dynamic-update-slice_fusion.8 = (bf16[120,5632]{1,0:T(8,128)(2,1)S(1)}, bf16[120,1408]{1,0:T(8,128)(2,1)S(1)}) fusion(bf16[120,5632]{1,0:T(8,128)(2,1)S(1)} %broadcast.405.clone.1, s32[]{:T(128)S(6)} %select_n.137, bf16[120,2048]{1,0:T(8,128)(2,1)S(1)} %pad_maximum_fusion.6, bf16[1,1408,2048]{2,1,0:T(8,128)(2,1)S(1)} %bitcast.118, ...), kind=kOutput, calls=%fused_computation.101 | convolution fusion | flops 693073920 | bytes 7610372 | tf_op jit(solution)/shard_map/dot_general | solution.py:17
  33.2 2.7 %collective-permute-start.6 = (bf16[120,1408]{1,0:T(8,128)(2,1)S(1)}, bf16[120,1408]{1,0:T(8,128)(2,1)S(1)}, u32[]{:S(2)}, u32[]{:S(2)}) collective-permute-start(bf16[120,1408]{1,0:T(8,128)(2,1)S(1)} %get-tuple-element.65), channel_id=1, source_target_pairs={{0,3},{1,2},{2,1},{3,0},{4,7},{5,6},{6,5},{7,4},{8,11},{9,10},{10,... | collective-permute-start | bytes 1013768 | tf_op jit(solution)/shard_map/ppermute | solution.py:32
  35.9 2.7 %collective-permute-start.7 = (bf16[120,1408]{1,0:T(8,128)(2,1)S(1)}, bf16[120,1408]{1,0:T(8,128)(2,1)S(1)}, u32[]{:S(2)}, u32[]{:S(2)}) collective-permute-start(bf16[120,1408]{1,0:T(8,128)(2,1)S(1)} %get-tuple-element.65), channel_id=1, source_target_pairs={{0,2},{3,1},{4,6},{7,5},{8,10},{11,9},{12,14},{15,13},{16,18},{19,... | collective-permute-start | bytes 1013768 | tf_op jit(solution)/shard_map/ppermute | solution.py:32
  38.8 1.6 %collective-permute-start.9 = (bf16[128,2048]{1,0:T(8,128)(2,1)S(1)}, bf16[128,2048]{1,0:T(8,128)(2,1)S(1)}, u32[]{:S(2)}, u32[]{:S(2)}) collective-permute-start(bf16[128,2048]{1,0:T(8,128)(2,1)S(1)} %pad_maximum_fusion.3), channel_id=1, source_target_pairs={{0,8},{4,12},{8,0},{12,4},{16,24},{20,28},{24,16},{28,20},{1,9},{5... | collective-permute-start | bytes 1572872 | tf_op jit(solution)/shard_map/ppermute | solution.py:28
  40.4 1.6 %collective-permute-start.10 = (bf16[128,2048]{1,0:T(8,128)(2,1)S(1)}, bf16[128,2048]{1,0:T(8,128)(2,1)S(1)}, u32[]{:S(2)}, u32[]{:S(2)}) collective-permute-start(bf16[128,2048]{1,0:T(8,128)(2,1)S(1)} %pad_maximum_fusion.4), channel_id=1, source_target_pairs={{0,16},{4,20},{8,24},{12,28},{16,0},{20,4},{24,8},{28,12},{1,17},{... | collective-permute-start | bytes 1572872 | tf_op jit(solution)/shard_map/ppermute | solution.py:28
  42.0 1.2 collective-permute-done.5
  43.2 8.7 %collective-permute-done.6 = bf16[120,1408]{1,0:T(8,128)(2,1)S(1)} collective-permute-done((bf16[120,1408]{1,0:T(8,128)(2,1)S(1)}, bf16[120,1408]{1,0:T(8,128)(2,1)S(1)}, u32[]{:S(2)}, u32[]{:S(2)}) %collective-permute-start.6) | collective-permute-done | bytes 337952 | tf_op jit(solution)/shard_map/ppermute | solution.py:32
  52.0 3.5 %collective-permute-done.7 = bf16[120,1408]{1,0:T(8,128)(2,1)S(1)} collective-permute-done((bf16[120,1408]{1,0:T(8,128)(2,1)S(1)}, bf16[120,1408]{1,0:T(8,128)(2,1)S(1)}, u32[]{:S(2)}, u32[]{:S(2)}) %collective-permute-start.7) | collective-permute-done | bytes 337952 | tf_op jit(solution)/shard_map/ppermute | solution.py:32
  55.5 1.5 collective-permute-start.8
  57.3 1.8 %fusion.14 = f32[240,1408]{1,0:T(8,128)S(1)} fusion(bf16[240,2048]{1,0:T(8,128)(2,1)S(1)} %pad_maximum_fusion.2, bf16[1,1408,2048]{2,1,0:T(8,128)(2,1)S(1)} %bitcast.94), kind=kOutput, calls=%fused_computation.14 | convolution fusion | flops 1384120320 | bytes 8101888 | tf_op jit(solution)/shard_map/dot_general | solution.py:17
  59.3 2.0 %constant_dynamic-update-slice_fusion.5 = (bf16[240,5632]{1,0:T(8,128)(2,1)S(1)}, bf16[240,1408]{1,0:T(8,128)(2,1)S(1)}) fusion(bf16[240,5632]{1,0:T(8,128)(2,1)S(1)} %broadcast_in_dim.15, s32[]{:T(128)S(6)} %select_n.137, bf16[240,2048]{1,0:T(8,128)(2,1)S(1)} %pad_maximum_fusion.2, bf16[1,1408,2048]{2,1,0:T(8,128)(2,1)S(1)} %bitcast.118, ...), kind=kOutput, calls=%fused_computation.97 | convolution fusion | flops 1386147840 | bytes 9453572 | tf_op jit(solution)/shard_map/dot_general | solution.py:17
  61.3 4.1 %collective-permute-start.19 = (bf16[240,1408]{1,0:T(8,128)(2,1)S(1)}, bf16[240,1408]{1,0:T(8,128)(2,1)S(1)}, u32[]{:S(2)}, u32[]{:S(2)}) collective-permute-start(bf16[240,1408]{1,0:T(8,128)(2,1)S(1)} %get-tuple-element.63), channel_id=1, source_target_pairs={{0,1},{1,0},{2,3},{3,2},{4,5},{5,4},{6,7},{7,6},{8,9},{9,8},{10,11... | collective-permute-start | bytes 2027528 | tf_op jit(solution)/shard_map/ppermute | solution.py:32
  65.4 2.6 %collective-permute-start.20 = (bf16[240,1408]{1,0:T(8,128)(2,1)S(1)}, bf16[240,1408]{1,0:T(8,128)(2,1)S(1)}, u32[]{:S(2)}, u32[]{:S(2)}) collective-permute-start(bf16[240,1408]{1,0:T(8,128)(2,1)S(1)} %get-tuple-element.63), channel_id=1, source_target_pairs={{0,3},{1,2},{2,1},{3,0},{4,7},{5,6},{6,5},{7,4},{8,11},{9,10},{10,... | collective-permute-start | bytes 2027528 | tf_op jit(solution)/shard_map/ppermute | solution.py:32
  68.0 2.5 %collective-permute-start.18 = (bf16[128,2048]{1,0:T(8,128)(2,1)S(1)}, bf16[128,2048]{1,0:T(8,128)(2,1)S(1)}, u32[]{:S(2)}, u32[]{:S(2)}) collective-permute-start(bf16[128,2048]{1,0:T(8,128)(2,1)S(1)} %pad_maximum_fusion.5), channel_id=1, source_target_pairs={{0,24},{4,28},{8,16},{12,20},{16,8},{20,12},{24,0},{28,4},{1,25},{... | collective-permute-start | bytes 1572872 | tf_op jit(solution)/shard_map/ppermute | solution.py:28
  71.0 1.3 fusion.39
  72.3 1.8 %collective-permute-start.17 = (f32[160,16]{0,1:T(8,128)S(1)}, f32[160,16]{0,1:T(8,128)S(1)}, u32[]{:S(2)}, u32[]{:S(2)}) collective-permute-start(f32[160,16]{0,1:T(8,128)S(1)} %fusion.39), channel_id=1, source_target_pairs={{0,3},{1,2},{2,1},{3,0},{4,7},{5,6},{6,5},{7,4},{8,11},{9,10},{10,... | collective-permute-start | bytes 30728 | tf_op jit(solution)/shard_map/ppermute | solution.py:86
  74.1 7.1 %collective-permute-done.18 = bf16[128,2048]{1,0:T(8,128)(2,1)S(1)} collective-permute-done((bf16[128,2048]{1,0:T(8,128)(2,1)S(1)}, bf16[128,2048]{1,0:T(8,128)(2,1)S(1)}, u32[]{:S(2)}, u32[]{:S(2)}) %collective-permute-start.18) | collective-permute-done | bytes 524320 | tf_op jit(solution)/shard_map/ppermute | solution.py:28
  81.3 1.9 %fusion.12 = f32[120,1408]{1,0:T(8,128)S(1)} fusion(bf16[120,2048]{1,0:T(8,128)(2,1)S(1)} %pad_maximum_fusion.7, bf16[1,1408,2048]{2,1,0:T(8,128)(2,1)S(1)} %bitcast.94), kind=kOutput, calls=%fused_computation.12 | convolution fusion | flops 692060160 | bytes 6934528 | tf_op jit(solution)/shard_map/dot_general | solution.py:17
  83.4 2.0 %constant_dynamic-update-slice_fusion.2 = (bf16[120,5632]{1,0:T(8,128)(2,1)S(1)}, bf16[120,1408]{1,0:T(8,128)(2,1)S(1)}) fusion(bf16[120,5632]{1,0:T(8,128)(2,1)S(1)} %broadcast.405.clone, s32[]{:T(128)S(6)} %select_n.137, bf16[120,2048]{1,0:T(8,128)(2,1)S(1)} %pad_maximum_fusion.7, bf16[1,1408,2048]{2,1,0:T(8,128)(2,1)S(1)} %bitcast.118, ...), kind=kOutput, calls=%fused_computation.94 | convolution fusion | flops 693073920 | bytes 7610372 | tf_op jit(solution)/shard_map/dot_general | solution.py:17
  85.4 11.9 %collective-permute-done.17 = f32[160,16]{0,1:T(8,128)S(1)} collective-permute-done((f32[160,16]{0,1:T(8,128)S(1)}, f32[160,16]{0,1:T(8,128)S(1)}, u32[]{:S(2)}, u32[]{:S(2)}) %collective-permute-start.17) | collective-permute-done | bytes 10272 | tf_op jit(solution)/shard_map/ppermute | solution.py:86
  97.3 3.0 %collective-permute-start.21 = (bf16[240,1408]{1,0:T(8,128)(2,1)S(1)}, bf16[240,1408]{1,0:T(8,128)(2,1)S(1)}, u32[]{:S(2)}, u32[]{:S(2)}) collective-permute-start(bf16[240,1408]{1,0:T(8,128)(2,1)S(1)} %get-tuple-element.63), channel_id=1, source_target_pairs={{0,2},{3,1},{4,6},{7,5},{8,10},{11,9},{12,14},{15,13},{16,18},{19,... | collective-permute-start | bytes 2027528 | tf_op jit(solution)/shard_map/ppermute | solution.py:32
  101.7 0.9 fusion.43
  102.7 4.6 %collective-permute-start.27 = (bf16[120,1408]{1,0:T(8,128)(2,1)S(1)}, bf16[120,1408]{1,0:T(8,128)(2,1)S(1)}, u32[]{:S(2)}, u32[]{:S(2)}) collective-permute-start(bf16[120,1408]{1,0:T(8,128)(2,1)S(1)} %get-tuple-element.67), channel_id=1, source_target_pairs={{0,2},{3,1},{4,6},{7,5},{8,10},{11,9},{12,14},{15,13},{16,18},{19,... | collective-permute-start | bytes 1013768 | tf_op jit(solution)/shard_map/ppermute | solution.py:32
  107.3 1.3 collective-permute-start.22
  108.8 7.1 %collective-permute-done.21 = bf16[240,1408]{1,0:T(8,128)(2,1)S(1)} collective-permute-done((bf16[240,1408]{1,0:T(8,128)(2,1)S(1)}, bf16[240,1408]{1,0:T(8,128)(2,1)S(1)}, u32[]{:S(2)}, u32[]{:S(2)}) %collective-permute-start.21) | collective-permute-done | bytes 675872 | tf_op jit(solution)/shard_map/ppermute | solution.py:32
  115.9 7.2 %collective-permute-done.25 = bf16[120,1408]{1,0:T(8,128)(2,1)S(1)} collective-permute-done((bf16[120,1408]{1,0:T(8,128)(2,1)S(1)}, bf16[120,1408]{1,0:T(8,128)(2,1)S(1)}, u32[]{:S(2)}, u32[]{:S(2)}) %collective-permute-start.25) | collective-permute-done | bytes 337952 | tf_op jit(solution)/shard_map/ppermute | solution.py:32
  123.2 8.2 %collective-permute-done.26 = bf16[120,1408]{1,0:T(8,128)(2,1)S(1)} collective-permute-done((bf16[120,1408]{1,0:T(8,128)(2,1)S(1)}, bf16[120,1408]{1,0:T(8,128)(2,1)S(1)}, u32[]{:S(2)}, u32[]{:S(2)}) %collective-permute-start.26) | collective-permute-done | bytes 337952 | tf_op jit(solution)/shard_map/ppermute | solution.py:32
  131.4 1.5 collective-permute-start.28
  133.0 7.5 %collective-permute-done.28 = bf16[120,1408]{1,0:T(8,128)(2,1)S(1)} collective-permute-done((bf16[120,1408]{1,0:T(8,128)(2,1)S(1)}, bf16[120,1408]{1,0:T(8,128)(2,1)S(1)}, u32[]{:S(2)}, u32[]{:S(2)}) %collective-permute-start.28) | collective-permute-done | bytes 337952 | tf_op jit(solution)/shard_map/ppermute | solution.py:32
  140.8 1.6 fusion.40
  142.4 0.9 fusion.46
  143.3 2.5 %collective-permute-start.29 = (bf16[120,512]{1,0:T(8,128)(2,1)S(1)}, bf16[120,512]{1,0:T(8,128)(2,1)S(1)}, u32[]{:S(2)}, u32[]{:S(2)}) collective-permute-start(bf16[120,512]{1,0:T(8,128)(2,1)S(1)} %fusion.46), channel_id=1, source_target_pairs={{0,24},{4,28},{8,16},{12,20},{16,8},{20,12},{24,0},{28,4},{1,25},{... | collective-permute-start | bytes 368648 | tf_op jit(solution)/shard_map/ppermute | solution.py:28
  147.0 2.1 %collective-permute-done.29 = bf16[120,512]{1,0:T(8,128)(2,1)S(1)} collective-permute-done((bf16[120,512]{1,0:T(8,128)(2,1)S(1)}, bf16[120,512]{1,0:T(8,128)(2,1)S(1)}, u32[]{:S(2)}, u32[]{:S(2)}) %collective-permute-start.29) | collective-permute-done | bytes 122912 | tf_op jit(solution)/shard_map/ppermute | solution.py:28
  149.2 1.6 collective-permute-done.24
  151.9 1.2 collective-permute-done.30
  153.8 0.9 multiply_reduce_fusion
  (125 shorter events, 13.9 us)
Async XLA Ops:
  0.0 14.9 %copy-start = (s32[160,2]{0,1:T(2,128)S(1)}, s32[160,2]{0,1:T(2,128)}, u32[]{:S(2)}) copy-start(s32[160,2]{0,1:T(2,128)} %param.15) | copy-start | bytes 3844
  0.0 15.0 %copy-start.2 = (s32[16]{0:T(128)S(1)}, s32[16]{0:T(128)}, u32[]{:S(2)}) copy-start(s32[16]{0:T(128)} %param.13) | copy-start | bytes 196
  0.0 15.3 %copy-start.3 = (s32[16]{0:T(128)S(1)}, s32[16]{0:T(128)}, u32[]{:S(2)}) copy-start(s32[16]{0:T(128)} %param.14) | copy-start | bytes 196
  0.8 28.3 %slice-start = ((s8[5767168]{0:T(1024)(128)(4,1)}), s8[1572864]{0:T(1024)(128)(4,1)S(1)}, s32[]{:S(2)}) async-start(s8[5767168]{0:T(1024)(128)(4,1)} %bitcast.93), calls=%async_computation | async-start | bytes 3145728
  1.9 13.6 %collective-permute-start = (bf16[176,512]{1,0:T(8,128)(2,1)S(1)}, bf16[176,512]{1,0:T(8,128)(2,1)}, u32[]{:S(2)}, u32[]{:S(2)}) collective-permute-start(bf16[176,512]{1,0:T(8,128)(2,1)S(1)} %get-tuple-element.55), channel_id=1, source_target_pairs={{0,1},{1,0},{2,3},{3,2},{4,5},{5,4},{6,7},{7,6},{8,9},{9,8},{10,11... | collective-permute-start | bytes 540680 | tf_op jit(solution)/shard_map/ppermute | solution.py:32
  5.0 12.0 %collective-permute-start.1 = (bf16[176,512]{1,0:T(8,128)(2,1)S(1)}, bf16[176,512]{1,0:T(8,128)(2,1)}, u32[]{:S(2)}, u32[]{:S(2)}) collective-permute-start(bf16[176,512]{1,0:T(8,128)(2,1)S(1)} %get-tuple-element.55), channel_id=1, source_target_pairs={{0,3},{1,2},{2,1},{3,0},{4,7},{5,6},{6,5},{7,4},{8,11},{9,10},{10,... | collective-permute-start | bytes 540680 | tf_op jit(solution)/shard_map/ppermute | solution.py:32
  7.5 12.7 %collective-permute-start.2 = (bf16[176,512]{1,0:T(8,128)(2,1)S(1)}, bf16[176,512]{1,0:T(8,128)(2,1)S(1)}, u32[]{:S(2)}, u32[]{:S(2)}) collective-permute-start(bf16[176,512]{1,0:T(8,128)(2,1)S(1)} %get-tuple-element.55), channel_id=1, source_target_pairs={{0,2},{3,1},{4,6},{7,5},{8,10},{11,9},{12,14},{15,13},{16,18},{19,... | collective-permute-start | bytes 540680 | tf_op jit(solution)/shard_map/ppermute | solution.py:32
  10.5 15.9 %collective-permute-start.13 = (bf16[256,512]{1,0:T(8,128)(2,1)S(1)}, bf16[256,512]{1,0:T(8,128)(2,1)S(1)}, u32[]{:S(2)}, u32[]{:S(2)}) collective-permute-start(bf16[256,512]{1,0:T(8,128)(2,1)S(1)} %bitcast.104), channel_id=1, source_target_pairs={{0,24},{4,28},{8,16},{12,20},{16,8},{20,12},{24,0},{28,4},{1,25},{... | collective-permute-start | bytes 786440 | tf_op jit(solution)/shard_map/ppermute | solution.py:28
  13.0 13.4 %collective-permute-start.12 = (bf16[256,512]{1,0:T(8,128)(2,1)S(1)}, bf16[256,512]{1,0:T(8,128)(2,1)S(1)}, u32[]{:S(2)}, u32[]{:S(2)}) collective-permute-start(bf16[256,512]{1,0:T(8,128)(2,1)S(1)} %bitcast.105), channel_id=1, source_target_pairs={{0,16},{4,20},{8,24},{12,28},{16,0},{20,4},{24,8},{28,12},{1,17},{... | collective-permute-start | bytes 786440 | tf_op jit(solution)/shard_map/ppermute | solution.py:28
  15.6 10.8 %collective-permute-start.11 = (bf16[256,512]{1,0:T(8,128)(2,1)S(1)}, bf16[256,512]{1,0:T(8,128)(2,1)S(1)}, u32[]{:S(2)}, u32[]{:S(2)}) collective-permute-start(bf16[256,512]{1,0:T(8,128)(2,1)S(1)} %bitcast.106), channel_id=1, source_target_pairs={{0,8},{4,12},{8,0},{12,4},{16,24},{20,28},{24,16},{28,20},{1,9},{5... | collective-permute-start | bytes 786440 | tf_op jit(solution)/shard_map/ppermute | solution.py:28
  17.0 8.2 %collective-permute-start.3 = (bf16[176,512]{1,0:T(8,128)(2,1)}, bf16[176,512]{1,0:T(8,128)(2,1)S(1)}, u32[]{:S(2)}, u32[]{:S(2)}) collective-permute-start(bf16[176,512]{1,0:T(8,128)(2,1)} %collective-permute-done.1), channel_id=1, source_target_pairs={{1,0},{2,3},{5,4},{6,7},{9,8},{10,11},{13,12},{14,15},{17,16},{18,... | collective-permute-start | bytes 540680 | tf_op jit(solution)/shard_map/ppermute | solution.py:32
  26.2 2.9 %slice-start.1 = ((s8[5767168]{0:T(1024)(128)(4,1)}), s8[4194304]{0:T(1024)(128)(4,1)S(1)}, s32[]{:S(2)}) async-start(s8[5767168]{0:T(1024)(128)(4,1)} %bitcast.93), calls=%async_computation.1 | async-start | bytes 8388608
  26.2 2.7 %collective-permute-start.4 = (bf16[4,64,2048]{2,1,0:T(8,128)(2,1)S(1)}, bf16[4,64,2048]{2,1,0:T(8,128)(2,1)S(1)}, u32[]{:S(2)}, u32[]{:S(2)}) collective-permute-start(bf16[4,64,2048]{2,1,0:T(8,128)(2,1)S(1)} %bitcast.101), channel_id=1, source_target_pairs={{0,4},{4,0},{8,12},{12,8},{16,20},{20,16},{24,28},{28,24},{1,5},{5... | collective-permute-start | bytes 3145736 | tf_op jit(solution)/shard_map/ppermute | solution.py:28
  27.1 4.1 %slice-start.4 = ((s8[5767168]{0:T(1024)(128)(4,1)}), s8[4194304]{0:T(1024)(128)(4,1)S(1)}, s32[]{:S(2)}) async-start(s8[5767168]{0:T(1024)(128)(4,1)} %bitcast.117), calls=%async_computation.4 | async-start | bytes 8388608
  29.1 2.1 %slice-start.5 = ((s8[5767168]{0:T(1024)(128)(4,1)}), s8[1572864]{0:T(1024)(128)(4,1)S(1)}, s32[]{:S(2)}) async-start(s8[5767168]{0:T(1024)(128)(4,1)} %bitcast.117), calls=%async_computation.5 | async-start | bytes 3145728
  33.2 10.0 %collective-permute-start.5 = (bf16[120,1408]{1,0:T(8,128)(2,1)S(1)}, bf16[120,1408]{1,0:T(8,128)(2,1)S(1)}, u32[]{:S(2)}, u32[]{:S(2)}) collective-permute-start(bf16[120,1408]{1,0:T(8,128)(2,1)S(1)} %get-tuple-element.65), channel_id=1, source_target_pairs={{0,1},{1,0},{2,3},{3,2},{4,5},{5,4},{6,7},{7,6},{8,9},{9,8},{10,11... | collective-permute-start | bytes 1013768 | tf_op jit(solution)/shard_map/ppermute | solution.py:32
  33.2 18.7 %collective-permute-start.6 = (bf16[120,1408]{1,0:T(8,128)(2,1)S(1)}, bf16[120,1408]{1,0:T(8,128)(2,1)S(1)}, u32[]{:S(2)}, u32[]{:S(2)}) collective-permute-start(bf16[120,1408]{1,0:T(8,128)(2,1)S(1)} %get-tuple-element.65), channel_id=1, source_target_pairs={{0,3},{1,2},{2,1},{3,0},{4,7},{5,6},{6,5},{7,4},{8,11},{9,10},{10,... | collective-permute-start | bytes 1013768 | tf_op jit(solution)/shard_map/ppermute | solution.py:32
  35.9 19.6 %collective-permute-start.7 = (bf16[120,1408]{1,0:T(8,128)(2,1)S(1)}, bf16[120,1408]{1,0:T(8,128)(2,1)S(1)}, u32[]{:S(2)}, u32[]{:S(2)}) collective-permute-start(bf16[120,1408]{1,0:T(8,128)(2,1)S(1)} %get-tuple-element.65), channel_id=1, source_target_pairs={{0,2},{3,1},{4,6},{7,5},{8,10},{11,9},{12,14},{15,13},{16,18},{19,... | collective-permute-start | bytes 1013768 | tf_op jit(solution)/shard_map/ppermute | solution.py:32
  38.8 18.3 %collective-permute-start.9 = (bf16[128,2048]{1,0:T(8,128)(2,1)S(1)}, bf16[128,2048]{1,0:T(8,128)(2,1)S(1)}, u32[]{:S(2)}, u32[]{:S(2)}) collective-permute-start(bf16[128,2048]{1,0:T(8,128)(2,1)S(1)} %pad_maximum_fusion.3), channel_id=1, source_target_pairs={{0,8},{4,12},{8,0},{12,4},{16,24},{20,28},{24,16},{28,20},{1,9},{5... | collective-permute-start | bytes 1572872 | tf_op jit(solution)/shard_map/ppermute | solution.py:28
  40.4 16.6 %collective-permute-start.10 = (bf16[128,2048]{1,0:T(8,128)(2,1)S(1)}, bf16[128,2048]{1,0:T(8,128)(2,1)S(1)}, u32[]{:S(2)}, u32[]{:S(2)}) collective-permute-start(bf16[128,2048]{1,0:T(8,128)(2,1)S(1)} %pad_maximum_fusion.4), channel_id=1, source_target_pairs={{0,16},{4,20},{8,24},{12,28},{16,0},{20,4},{24,8},{28,12},{1,17},{... | collective-permute-start | bytes 1572872 | tf_op jit(solution)/shard_map/ppermute | solution.py:28
  43.2 27.4 %collective-permute-start.14 = (bf16[4,256,512]{2,1,0:T(8,128)(2,1)S(1)}, bf16[4,256,512]{2,1,0:T(8,128)(2,1)S(1)}, u32[]{:S(2)}, u32[]{:S(2)}) collective-permute-start(bf16[4,256,512]{2,1,0:T(8,128)(2,1)S(1)} %pad_maximum_fusion.1), channel_id=1, source_target_pairs={{0,4},{4,0},{8,12},{12,8},{16,20},{20,16},{24,28},{28,24},{1,5},{5... | collective-permute-start | bytes 3145736 | tf_op jit(solution)/shard_map/ppermute | solution.py:28
  55.5 15.0 %collective-permute-start.8 = (bf16[120,1408]{1,0:T(8,128)(2,1)S(1)}, bf16[120,1408]{1,0:T(8,128)(2,1)S(1)}, u32[]{:S(2)}, u32[]{:S(2)}) collective-permute-start(bf16[120,1408]{1,0:T(8,128)(2,1)S(1)} %collective-permute-done.6), channel_id=1, source_target_pairs={{1,0},{2,3},{5,4},{6,7},{9,8},{10,11},{13,12},{14,15},{17,16},{18,... | collective-permute-start | bytes 1013768 | tf_op jit(solution)/shard_map/ppermute | solution.py:32
  61.3 41.4 %collective-permute-start.19 = (bf16[240,1408]{1,0:T(8,128)(2,1)S(1)}, bf16[240,1408]{1,0:T(8,128)(2,1)S(1)}, u32[]{:S(2)}, u32[]{:S(2)}) collective-permute-start(bf16[240,1408]{1,0:T(8,128)(2,1)S(1)} %get-tuple-element.63), channel_id=1, source_target_pairs={{0,1},{1,0},{2,3},{3,2},{4,5},{5,4},{6,7},{7,6},{8,9},{9,8},{10,11... | collective-permute-start | bytes 2027528 | tf_op jit(solution)/shard_map/ppermute | solution.py:32
  65.4 41.9 %collective-permute-start.20 = (bf16[240,1408]{1,0:T(8,128)(2,1)S(1)}, bf16[240,1408]{1,0:T(8,128)(2,1)S(1)}, u32[]{:S(2)}, u32[]{:S(2)}) collective-permute-start(bf16[240,1408]{1,0:T(8,128)(2,1)S(1)} %get-tuple-element.63), channel_id=1, source_target_pairs={{0,3},{1,2},{2,1},{3,0},{4,7},{5,6},{6,5},{7,4},{8,11},{9,10},{10,... | collective-permute-start | bytes 2027528 | tf_op jit(solution)/shard_map/ppermute | solution.py:32
  68.0 13.1 %collective-permute-start.18 = (bf16[128,2048]{1,0:T(8,128)(2,1)S(1)}, bf16[128,2048]{1,0:T(8,128)(2,1)S(1)}, u32[]{:S(2)}, u32[]{:S(2)}) collective-permute-start(bf16[128,2048]{1,0:T(8,128)(2,1)S(1)} %pad_maximum_fusion.5), channel_id=1, source_target_pairs={{0,24},{4,28},{8,16},{12,20},{16,8},{20,12},{24,0},{28,4},{1,25},{... | collective-permute-start | bytes 1572872 | tf_op jit(solution)/shard_map/ppermute | solution.py:28
  72.3 25.0 %collective-permute-start.17 = (f32[160,16]{0,1:T(8,128)S(1)}, f32[160,16]{0,1:T(8,128)S(1)}, u32[]{:S(2)}, u32[]{:S(2)}) collective-permute-start(f32[160,16]{0,1:T(8,128)S(1)} %fusion.39), channel_id=1, source_target_pairs={{0,3},{1,2},{2,1},{3,0},{4,7},{5,6},{6,5},{7,4},{8,11},{9,10},{10,... | collective-permute-start | bytes 30728 | tf_op jit(solution)/shard_map/ppermute | solution.py:86
  74.1 26.2 %collective-permute-start.16 = (f32[160,16]{0,1:T(8,128)S(1)}, f32[160,16]{0,1:T(8,128)S(1)}, u32[]{:S(2)}, u32[]{:S(2)}) collective-permute-start(f32[160,16]{0,1:T(8,128)S(1)} %fusion.39), channel_id=1, source_target_pairs={{0,2},{1,3},{2,0},{3,1},{4,6},{5,7},{6,4},{7,5},{8,10},{9,11},{10,... | collective-permute-start | bytes 30728 | tf_op jit(solution)/shard_map/ppermute | solution.py:86
  81.2 19.3 %collective-permute-start.15 = (f32[160,16]{0,1:T(8,128)S(1)}, f32[160,16]{0,1:T(8,128)S(1)}, u32[]{:S(2)}, u32[]{:S(2)}) collective-permute-start(f32[160,16]{0,1:T(8,128)S(1)} %fusion.39), channel_id=1, source_target_pairs={{0,1},{1,0},{2,3},{3,2},{4,5},{5,4},{6,7},{7,6},{8,9},{9,8},{10,11... | collective-permute-start | bytes 30728 | tf_op jit(solution)/shard_map/ppermute | solution.py:86
  83.3 18.4 %slice-start.2 = ((s8[5767168]{0:T(1024)(128)(4,1)}), s8[4194304]{0:T(1024)(128)(4,1)S(1)}, s32[]{:S(2)}) async-start(s8[5767168]{0:T(1024)(128)(4,1)} %bitcast.95), calls=%async_computation.2 | async-start | bytes 8388608
  83.4 18.3 %slice-start.3 = ((s8[5767168]{0:T(1024)(128)(4,1)}), s8[1572864]{0:T(1024)(128)(4,1)S(1)}, s32[]{:S(2)}) async-start(s8[5767168]{0:T(1024)(128)(4,1)} %bitcast.95), calls=%async_computation.3 | async-start | bytes 3145728
  97.3 18.6 %collective-permute-start.21 = (bf16[240,1408]{1,0:T(8,128)(2,1)S(1)}, bf16[240,1408]{1,0:T(8,128)(2,1)S(1)}, u32[]{:S(2)}, u32[]{:S(2)}) collective-permute-start(bf16[240,1408]{1,0:T(8,128)(2,1)S(1)} %get-tuple-element.63), channel_id=1, source_target_pairs={{0,2},{3,1},{4,6},{7,5},{8,10},{11,9},{12,14},{15,13},{16,18},{19,... | collective-permute-start | bytes 2027528 | tf_op jit(solution)/shard_map/ppermute | solution.py:32
  100.4 22.8 %collective-permute-start.25 = (bf16[120,1408]{1,0:T(8,128)(2,1)S(1)}, bf16[120,1408]{1,0:T(8,128)(2,1)S(1)}, u32[]{:S(2)}, u32[]{:S(2)}) collective-permute-start(bf16[120,1408]{1,0:T(8,128)(2,1)S(1)} %get-tuple-element.67), channel_id=1, source_target_pairs={{0,1},{1,0},{2,3},{3,2},{4,5},{5,4},{6,7},{7,6},{8,9},{9,8},{10,11... | collective-permute-start | bytes 1013768 | tf_op jit(solution)/shard_map/ppermute | solution.py:32
  100.5 30.9 %collective-permute-start.26 = (bf16[120,1408]{1,0:T(8,128)(2,1)S(1)}, bf16[120,1408]{1,0:T(8,128)(2,1)S(1)}, u32[]{:S(2)}, u32[]{:S(2)}) collective-permute-start(bf16[120,1408]{1,0:T(8,128)(2,1)S(1)} %get-tuple-element.67), channel_id=1, source_target_pairs={{0,3},{1,2},{2,1},{3,0},{4,7},{5,6},{6,5},{7,4},{8,11},{9,10},{10,... | collective-permute-start | bytes 1013768 | tf_op jit(solution)/shard_map/ppermute | solution.py:32
  102.7 30.2 %collective-permute-start.27 = (bf16[120,1408]{1,0:T(8,128)(2,1)S(1)}, bf16[120,1408]{1,0:T(8,128)(2,1)S(1)}, u32[]{:S(2)}, u32[]{:S(2)}) collective-permute-start(bf16[120,1408]{1,0:T(8,128)(2,1)S(1)} %get-tuple-element.67), channel_id=1, source_target_pairs={{0,2},{3,1},{4,6},{7,5},{8,10},{11,9},{12,14},{15,13},{16,18},{19,... | collective-permute-start | bytes 1013768 | tf_op jit(solution)/shard_map/ppermute | solution.py:32
  107.3 33.2 %collective-permute-start.22 = (bf16[240,1408]{1,0:T(8,128)(2,1)S(1)}, bf16[240,1408]{1,0:T(8,128)(2,1)S(1)}, u32[]{:S(2)}, u32[]{:S(2)}) collective-permute-start(bf16[240,1408]{1,0:T(8,128)(2,1)S(1)} %collective-permute-done.20), channel_id=1, source_target_pairs={{1,0},{2,3},{5,4},{6,7},{9,8},{10,11},{13,12},{14,15},{17,16},{18,... | collective-permute-start | bytes 2027528 | tf_op jit(solution)/shard_map/ppermute | solution.py:32
  131.4 9.1 %collective-permute-start.28 = (bf16[120,1408]{1,0:T(8,128)(2,1)S(1)}, bf16[120,1408]{1,0:T(8,128)(2,1)S(1)}, u32[]{:S(2)}, u32[]{:S(2)}) collective-permute-start(bf16[120,1408]{1,0:T(8,128)(2,1)S(1)} %collective-permute-done.26), channel_id=1, source_target_pairs={{1,0},{2,3},{5,4},{6,7},{9,8},{10,11},{13,12},{14,15},{17,16},{18,... | collective-permute-start | bytes 1013768 | tf_op jit(solution)/shard_map/ppermute | solution.py:32
  142.3 4.5 %copy-start.1 = (f32[160,2]{0,1:T(2,128)S(1)}, f32[160,2]{0,1:T(2,128)}, u32[]{:S(2)}) copy-start(f32[160,2]{0,1:T(2,128)} %param.16) | copy-start | bytes 3844
  143.3 5.8 %collective-permute-start.29 = (bf16[120,512]{1,0:T(8,128)(2,1)S(1)}, bf16[120,512]{1,0:T(8,128)(2,1)S(1)}, u32[]{:S(2)}, u32[]{:S(2)}) collective-permute-start(bf16[120,512]{1,0:T(8,128)(2,1)S(1)} %fusion.46), channel_id=1, source_target_pairs={{0,24},{4,28},{8,16},{12,20},{16,8},{20,12},{24,0},{28,4},{1,25},{... | collective-permute-start | bytes 368648 | tf_op jit(solution)/shard_map/ppermute | solution.py:28
  145.8 4.9 %collective-permute-start.24 = (bf16[120,512]{1,0:T(8,128)(2,1)S(1)}, bf16[120,512]{1,0:T(8,128)(2,1)S(1)}, u32[]{:S(2)}, u32[]{:S(2)}) collective-permute-start(bf16[120,512]{1,0:T(8,128)(2,1)S(1)} %get-tuple-element.54), channel_id=1, source_target_pairs={{0,16},{4,20},{8,24},{12,28},{16,0},{20,4},{24,8},{28,12},{1,17},{... | collective-permute-start | bytes 368648 | tf_op jit(solution)/shard_map/ppermute | solution.py:28
  146.3 4.9 %collective-permute-start.23 = (bf16[120,512]{1,0:T(8,128)(2,1)S(1)}, bf16[120,512]{1,0:T(8,128)(2,1)S(1)}, u32[]{:S(2)}, u32[]{:S(2)}) collective-permute-start(bf16[120,512]{1,0:T(8,128)(2,1)S(1)} %get-tuple-element.53), channel_id=1, source_target_pairs={{0,8},{4,12},{8,0},{12,4},{16,24},{20,28},{24,16},{28,20},{1,9},{5... | collective-permute-start | bytes 368648 | tf_op jit(solution)/shard_map/ppermute | solution.py:28
  151.4 1.6 %collective-permute-start.30 = (bf16[4,60,512]{2,1,0:T(8,128)(2,1)S(1)}, bf16[4,60,512]{2,1,0:T(8,128)(2,1)S(1)}, u32[]{:S(2)}, u32[]{:S(2)}) collective-permute-start(bf16[4,60,512]{2,1,0:T(8,128)(2,1)S(1)} %get-tuple-element.51), channel_id=1, source_target_pairs={{0,4},{4,0},{8,12},{12,8},{16,20},{20,16},{24,28},{28,24},{1,5},{5... | collective-permute-start | bytes 737288 | tf_op jit(solution)/shard_map/ppermute | solution.py:28

commit v3 on v2

v3 whole, which is shorter than its diff:
```python
import jax
import jax.numpy as jnp
from jax import lax
from jax.sharding import PartitionSpec as P

D = 2048
EXPERTS = 8
TOPK = 2
RANK = 16
CAP = 60
GAIN_ROWS = 8
LOW_STRIDE = 256
SLOTS = 64


def contract_last(left, right):
    return lax.dot_general(
        left, right, (((1,), (1,)), ((), ())), preferred_element_type=jnp.float32
    )


def col_shift(value, by):
    size = lax.axis_size("col")
    return lax.ppermute(value, "col", [(i, (i + by) % size) for i in range(size)])


def row_xor(value, by):
    return lax.ppermute(value, "row", [(i, i ^ by) for i in range(lax.axis_size("row"))])


def along(value, pairs):
    return lax.ppermute(value, "col", pairs)


BESIDE = [(0, 1), (1, 0), (2, 3), (3, 2)]
MIRROR = [(0, 3), (1, 2), (2, 1), (3, 0)]
OVER = [(0, 2), (3, 1)]
FACING = [(0, 2), (1, 3), (2, 0), (3, 1)]
OUTWARD = [(1, 0), (2, 3)]


def first_hops(value, whole):
    return (
        along(value, MIRROR),
        along(value, BESIDE),
        along(value, FACING if whole else OVER),
    )


def in_line(value, mirror, beside, facing):
    here = lax.axis_index("col")
    return side_by_side(
        value, [(here ^ 1, 0, beside), (here ^ 3, 0, mirror), (here ^ 2, 0, facing)]
    )


def ring_gather(value):
    size = lax.axis_size("col")
    here = lax.axis_index("col")
    rows = value.shape[0]
    half = -(-rows // 16) * 8
    found = []
    from_left, from_right = value, value
    for hop in range(1, (size + 1) // 2):
        from_left, from_right = col_shift(from_left, 1), col_shift(from_right, -1)
        found += [
            (lax.rem(here + size - hop, size), 0, from_left),
            (lax.rem(here + hop, size), 0, from_right),
        ]
    if size % 2 == 0:
        facing = lax.rem(here + size // 2, size)
        found += [
            (facing, 0, col_shift(from_left[:half], 1)),
            (facing, half, col_shift(from_right[half:], -1)),
        ]
    return found


def side_by_side(value, others):
    rows, width = value.shape
    whole = jnp.zeros((rows, lax.axis_size("col") * width), value.dtype)
    for sender, first, block in [(lax.axis_index("col"), 0, value)] + others:
        whole = lax.dynamic_update_slice(whole, block, (first, sender * width))
    return whole


def col_sum(value):
    size = lax.axis_size("col")
    total = value
    for by in range(1, size):
        total = total + lax.ppermute(value, "col", [(i, i ^ by) for i in range(size)])
    return total


def both_cores(stacked):
    both = jnp.stack([stacked, row_xor(stacked, 1)], axis=1)
    return both.reshape((lax.axis_size("row"),) + stacked.shape[1:])


def normalised(features, rows):
    widened = features[:rows].astype(jnp.float32)
    gain = jnp.sum(features[rows : rows + 3].astype(jnp.float32), axis=0)
    scale = lax.rsqrt(jnp.mean(widened * widened, axis=1, keepdims=True) + 1e-06)
    return (widened * scale * gain[None, :]).astype(jnp.bfloat16)


def tie(*values):
    return lax.optimization_barrier(values)


def split_float(value, parts):
    pieces = []
    for _ in range(parts):
        piece = lax.reduce_precision(value, 8, 7)
        pieces.append(piece.astype(jnp.bfloat16))
        value = value - piece
    return pieces


def body(
    tokens,
    norm_gain,
    lengths,
    request_adapter,
    routes,
    route_weights,
    gate_weight,
    up_weight,
    down_weight,
    adapter_down,
    adapter_up,
):
    tok_rows, width_part = tokens.shape
    rows_axis, cols_axis = lax.axis_size("row"), lax.axis_size("col")
    row_at, col_at = lax.axis_index("row"), lax.axis_index("col")
    splits = rows_axis // EXPERTS
    chips = rows_axis // 2
    unit_gate, unit_up, unit_down = gate_weight[0], up_weight[0], down_weight[0]
    hidden_part = unit_gate.shape[0]
    line = cols_axis == 4

    gain_parts = jnp.stack(split_float(norm_gain, 3))
    sent = jnp.concatenate(
        [tokens, jnp.pad(gain_parts, ((0, GAIN_ROWS - 3), (0, 0)))], axis=0
    )
    hops = first_hops(sent, True) if line else ring_gather(sent)

    local_adapters = adapter_down.shape[0]
    mine = jnp.concatenate([jnp.transpose(adapter_down, (0, 2, 1)), adapter_up], axis=0)
    mine = mine.reshape(2 * local_adapters * RANK, width_part)
    by_chip = [mine] + [row_xor(mine, by) for by in range(2, rows_axis, 2)]
    assigned = routes.reshape(-1)
    assign_count = assigned.shape[0]
    expert_hot = (assigned[:, None] == jnp.arange(EXPERTS, dtype=jnp.int32)[None, :]).astype(
        jnp.bfloat16
    )
    earlier = (
        jnp.arange(assign_count, dtype=jnp.int32)[:, None]
        > jnp.arange(assign_count, dtype=jnp.int32)[None, :]
    ).astype(jnp.bfloat16)
    before = jnp.dot(earlier, expert_hot, preferred_element_type=jnp.float32)
    slot_index = jnp.sum(before * expert_hot.astype(jnp.float32), axis=1).astype(jnp.int32)
    placed_at = assigned * SLOTS + slot_index

    def placing(core, slots):
        place = jnp.arange(chips * slots, dtype=jnp.int32)
        target = row_at ^ (place // slots * 2 + core)
        wanted = (target // splits) * SLOTS + place % slots
        return (wanted[:, None] == placed_at[None, :]).astype(jnp.bfloat16)

    of_token = [
        jnp.sum(placing(core, SLOTS).reshape(-1, tok_rows, TOPK), axis=2) for core in (0, 1)
    ]
    if line:
        hops, of_token = tie(hops, of_token)
    features = in_line(sent, *hops) if line else side_by_side(sent, hops)
    normed, *by_chip = tie(normalised(features, tok_rows), *by_chip)

    def outgoing(core):
        placed = jnp.dot(of_token[core], normed, preferred_element_type=jnp.float32)
        return placed.astype(jnp.bfloat16).reshape(chips, SLOTS, D)

    partner_half = row_xor(outgoing(1), 1)
    here_half = outgoing(0)

    groups = [[0], list(range(1, chips - 1)), [chips - 1]]
    pairs = [
        jnp.concatenate([here_half[offset], partner_half[offset]], axis=0)
        for offset in range(chips)
    ]
    for offset in range(1, chips):
        if offset == chips - 1:
            pairs[1:] = tie(*pairs[1:])
        pairs[offset] = row_xor(pairs[offset], 2 * offset)

    def hidden_of(offsets, earlier):
        arrived = jnp.concatenate(
            [
                pairs[offset][first : first + CAP]
                for offset in offsets
                for first in (0, SLOTS)
            ],
            axis=0,
        )
        arrived, *earlier = tie(arrived, *earlier)
        gate_sum = contract_last(arrived, unit_gate)
        up_sum = contract_last(arrived, unit_up)
        value = (jax.nn.silu(gate_sum) * up_sum).astype(jnp.bfloat16)
        return value, earlier

    def first_of(value, whole):
        return list(first_hops(value, whole)) if line else ring_gather(value)

    value, _ = hidden_of(groups[0], [])
    hidden, hops = [value], [first_of(value, False)]

    hidden[0], pairs[1:-1], by_chip = tie(hidden[0], pairs[1:-1], by_chip)
    factors = both_cores(jnp.stack(by_chip))
    factors = factors.reshape(rows_axis, 2, local_adapters * RANK, width_part)
    down_rows = factors[:, 0].reshape(-1, width_part)
    up_rows = factors[:, 1].reshape(-1, width_part)
    normed, pairs[1:-1] = tie(normed, pairs[1:-1])
    own = lax.dynamic_slice(normed, (0, col_at * width_part), (tok_rows, width_part))
    req_ends = jnp.cumsum(lengths)
    position = row_at * tok_rows + jnp.arange(tok_rows, dtype=jnp.int32)
    request = jnp.sum((position[None, :] >= req_ends[:, None]).astype(jnp.int32), axis=0)
    request_hot = request[None, :] == jnp.arange(lengths.shape[0], dtype=jnp.int32)[:, None]
    adapter = jnp.sum(jnp.where(request_hot, request_adapter[:, None], 0), axis=0)
    adapter_count = local_adapters * rows_axis
    order = jnp.arange(adapter_count, dtype=jnp.int32)
    held = (row_at ^ (order // local_adapters)) * local_adapters + order % local_adapters
    select = held[:, None] == adapter[None, :]
    projected = contract_last(down_rows, own).reshape(adapter_count, RANK, tok_rows)
    partial_low = jnp.sum(jnp.where(select[:, None, :], projected, 0.0), axis=0)
    extra = jnp.zeros((0, hidden_part), jnp.bfloat16)
    if line:
        pieces = [piece[at : at + 8] for piece in split_float(partial_low, 2) for at in (0, 8)]
        spare = (0, LOW_STRIDE - tok_rows)
        extra = jnp.concatenate([jnp.pad(piece, ((0, 0), spare)) for piece in pieces], axis=1)
        extra = jnp.pad(extra, ((0, 0), (0, hidden_part - extra.shape[1])))

    passed = along(hops[0][0], OUTWARD) if line else None
    value, (extra, *hops[0][:1]) = hidden_of(groups[1], [extra] + hops[0][:1])
    hidden.append(jnp.concatenate([value, extra], axis=0))
    hops.append(first_of(hidden[1], False))
    earlier = hops[0][1:] + [passed] if line else []
    pairs[-1], hidden[1] = tie(pairs[-1], hidden[1])
    value, (hidden[1], *earlier) = hidden_of(groups[2], [hidden[1]] + earlier)
    hidden.append(value)
    hops.append(first_of(value, True))
    if line:
        beside, over, passed = earlier
        hops[0] = [hops[0][0], beside, over + passed]

    def whole_of(number):
        return (in_line if line else side_by_side)(
            hidden[number], *(hops[number] if line else [hops[number]])
        )

    def block_sum(whole):
        return jnp.dot(whole, unit_down, preferred_element_type=jnp.float32)

    late_weights, hidden[2] = tie(route_weights, hidden[2])

    def weights_at(core):
        place = jnp.arange(chips * CAP, dtype=jnp.int32)
        target = row_at ^ (place // CAP * 2 + core)
        wanted = (target // splits) * SLOTS + place % CAP
        at = wanted[:, None, None] == placed_at.reshape(1, tok_rows, TOPK)
        return split_float(jnp.sum(jnp.where(at, late_weights[None], 0.0), axis=2), 2)

    place_weights = [weights_at(core) for core in (0, 1)]

    def weighted(core_blocks):
        return sum(
            lax.dot_general(
                part[first : first + rows.shape[0]],
                rows,
                (((0,), (0,)), ((), ())),
                preferred_element_type=jnp.float32,
            )
            for parts, (first, rows) in zip(place_weights, core_blocks)
            for part in parts
        )

    out = block_sum(whole_of(0)).astype(jnp.bfloat16)
    returned = [out]
    if line:
        mirror, beside, over = hops[1]
        mirror, hidden[2], returned[0], late_down = tie(mirror, hidden[2], out, unit_down)
        passed = along(mirror, OUTWARD)
        beside, over, mirror = tie(beside, over, mirror)
        hops[1] = [mirror, beside, over + passed]
    whole = whole_of(1)
    count = len(groups[1]) * 2 * CAP
    out = block_sum(whole[:count]).astype(jnp.bfloat16)
    if line:
        out, *hops[2][:2] = tie(out, *hops[2][:2])
    for index, offset in enumerate(groups[1]):
        returned.append(row_xor(out[index * 2 * CAP : (index + 1) * 2 * CAP], 2 * offset))
    if line:
        rest = whole[count:].reshape(8, cols_axis, hidden_part)[:, :, : 4 * LOW_STRIDE]
        rest = jnp.sum(rest.astype(jnp.float32), axis=1)
        rest = jnp.sum(rest.reshape(8, 2, 2, LOW_STRIDE), axis=1)[:, :, :tok_rows]
        low_sum = jnp.concatenate([rest[:, 0], rest[:, 1]], axis=0)
    else:
        low_sum = col_sum(partial_low)
    low_rank = low_sum.astype(jnp.bfloat16)
    expanded = jnp.where(select[:, None, :], low_rank[None], 0).reshape(
        adapter_count * RANK, tok_rows
    )
    branch = lax.dot_general(
        expanded, up_rows, (((0,), (0,)), ((), ())), preferred_element_type=jnp.float32
    )
    near = jnp.stack(returned)
    near_others = row_xor(near[:, CAP:], 1)
    if line:
        mirror, beside, facing = hops[2]
        part = block_sum(in_line(hidden[2], mirror, beside, jnp.zeros_like(mirror)))
        facing_down = lax.dynamic_slice(
            late_down, ((col_at ^ 2) * hidden_part, 0), (hidden_part, width_part)
        )
        facing, near, branch, part, facing_down, place_weights = tie(
            facing, near, branch, part, facing_down, place_weights
        )
        out = part + jnp.dot(facing, facing_down, preferred_element_type=jnp.float32)
    else:
        out = block_sum(whole_of(2))
    out = out.astype(jnp.bfloat16)
    far = [row_xor(out[:CAP], 2 * chips - 2), row_xor(out[CAP:], 2 * chips - 1)]
    near, out = tie(near, out)
    near = [near[:, :CAP].reshape(-1, width_part), near_others.reshape(-1, width_part)]
    mixed = branch + weighted([(0, rows) for rows in near])
    mixed = mixed + weighted([((chips - 1) * CAP, rows) for rows in far])
    return mixed.astype(jnp.bfloat16)


def solution(mesh):
    in_specs = (
        P("row", "col"),
        P("col"),
        P(),
        P(),
        P("row", None),
        P("row", None),
        P("row", "col", None),
        P("row", "col", None),
        P("row", None, "col"),
        P("row", "col", None),
        P("row", None, "col"),
    )
    out_specs = P("row", "col")
    return jax.shard_map(body, mesh=mesh, in_specs=in_specs, out_specs=out_specs, check_vma=False)
```

time: 156 us -> 145 us (0.929)
  waiting for transfers between devices: 75.5 us -> 57.6 us
  matrix products: 18.6 us -> 22.3 us
  starting transfers between devices: 48.5 us -> 51.9 us
    ppermute x3 -> x0, waiting for transfers between devices: 11.9 us -> none  [col_sum(): lax.ppermute(value, 'col', [(i, i ^ by) for i in range(size)])]
    ppermute x16 -> x14, waiting for transfers between devices: 49.3 us -> 42.6 us  [along(): return lax.ppermute(value, 'col', pairs)]
    ppermute x16 -> x14, starting transfers between devices: 33.8 us -> 39.4 us  [along(): return lax.ppermute(value, 'col', pairs)]
    dot_general x8 -> x15, matrix products: 5.44 us -> 9.14 us  [the longest x3 4.13 us: block_sum(): return jnp.dot(whole, unit_down, preferred_element_type=jnp.float32)]
    ppermute x3 -> x0, starting transfers between devices: 1.83 us -> none  [col_sum(): lax.ppermute(value, 'col', [(i, i ^ by) for i in range(size)])]
    dynamic_update_slice x8 -> x13, local copies, waits for them, and re-layouts: 2.2 us -> 3.39 us  [side_by_side(): whole = lax.dynamic_update_slice(whole, block, (first, sender * width))]
    ppermute x12 -> x13, waiting for transfers between devices: 14.3 us -> 14.9 us  [row_xor(): lax.ppermute(value, 'row', [(i, i ^ by) for i in range(lax.axis_size('row...]
    ppermute x12 -> x13, starting transfers between devices: 12.9 us -> 12.6 us  [row_xor(): lax.ppermute(value, 'row', [(i, i ^ by) for i in range(lax.axis_size('row...]
  transfers between devices with their start and end apart: 31 -> 27, of which waited for: 16 -> 13; matrix products, arithmetic and copies ran while one was open for 12% -> 20% of each run, Pallas kernels for 0% -> 0%
where the time goes in v3:
time: 145 us
  waiting for transfers between devices  57.6 us (40%)
  starting transfers between devices  51.9 us (36%)
  matrix products  22.3 us (15%)
  local copies, waits for them, and re-layouts  6.47 us (4%)
  other arithmetic  5.34 us (4%)
    ppermute x14, waiting for transfers between devices, along(): return lax.ppermute(value, 'col', pairs)  42.6 us
    ppermute x14, starting transfers between devices, along(): return lax.ppermute(value, 'col', pairs)  39.4 us
    ppermute x13, waiting for transfers between devices, row_xor(): lax.ppermute(value, 'row', [(i, i ^ by) for i in range(lax.axis_size('row...  14.9 us
    dot_general x7, matrix products, contract_last(): lax.dot_general(left, right, (((1,), (1,)), ((), ())), preferred_element_...  12.9 us
    ppermute x13, starting transfers between devices, row_xor(): lax.ppermute(value, 'row', [(i, i ^ by) for i in range(lax.axis_size('row...  12.6 us
    dot_general x3, matrix products, block_sum(): return jnp.dot(whole, unit_down, preferred_element_type=jnp.float32)  4.13 us
    dynamic_update_slice x13, local copies, waits for them, and re-layouts, side_by_side(): whole = lax.dynamic_update_slice(whole, block, (first, sender * width))  3.39 us
  transfers between devices with their start and end apart: 27, of which 13 were waited for; matrix products, arithmetic and copies ran while one was open for 20% of the time, Pallas kernels for 0%

profile of v3, /device:TPU:0, one launch (start us, length us, event | category | flops | bytes accessed | tf_op | source)
XLA Modules:
  0.0 144.5 jit_solution(8676133999216688558)
XLA Ops:
  0.0 0.7 reduce-precision_convert_fusion.4
  0.9 0.9 constant_dynamic-update-slice_fusion.12
  1.8 5.1 %collective-permute-start = (bf16[168,512]{1,0:T(8,128)(2,1)S(1)}, bf16[168,512]{1,0:T(8,128)(2,1)S(1)}, u32[]{:S(2)}, u32[]{:S(2)}) collective-permute-start(bf16[168,512]{1,0:T(8,128)(2,1)S(1)} %get-tuple-element.138), channel_id=1, source_target_pairs={{0,3},{1,2},{2,1},{3,0},{4,7},{5,6},{6,5},{7,4},{8,11},{9,10},{10,... | collective-permute-start | bytes 516104 | tf_op jit(solution)/shard_map/ppermute | solution.py:32
  7.6 1.0 pad_maximum_fusion.10
  8.6 1.7 %collective-permute-start.3 = (bf16[256,512]{1,0:T(8,128)(2,1)S(1)}, bf16[256,512]{1,0:T(8,128)(2,1)S(1)}, u32[]{:S(2)}, u32[]{:S(2)}) collective-permute-start(bf16[256,512]{1,0:T(8,128)(2,1)S(1)} %bitcast.100), channel_id=1, source_target_pairs={{0,8},{4,12},{8,0},{12,4},{16,24},{20,28},{24,16},{28,20},{1,9},{5... | collective-permute-start | bytes 786440 | tf_op jit(solution)/shard_map/ppermute | solution.py:28
  10.3 1.5 %collective-permute-start.4 = (bf16[256,512]{1,0:T(8,128)(2,1)S(1)}, bf16[256,512]{1,0:T(8,128)(2,1)S(1)}, u32[]{:S(2)}, u32[]{:S(2)}) collective-permute-start(bf16[256,512]{1,0:T(8,128)(2,1)S(1)} %bitcast.101), channel_id=1, source_target_pairs={{0,16},{4,20},{8,24},{12,28},{16,0},{20,4},{24,8},{28,12},{1,17},{... | collective-permute-start | bytes 786440 | tf_op jit(solution)/shard_map/ppermute | solution.py:28
  11.8 0.9 copy.29
  13.9 0.9 collective-permute-start.5
  14.8 1.4 collective-permute-done.1
  16.2 5.4 %collective-permute-done.2 = bf16[168,512]{1,0:T(8,128)(2,1)} collective-permute-done((bf16[168,512]{1,0:T(8,128)(2,1)S(1)}, bf16[168,512]{1,0:T(8,128)(2,1)}, u32[]{:S(2)}, u32[]{:S(2)}) %collective-permute-start.2) | collective-permute-done | bytes 172064 | tf_op jit(solution)/shard_map/ppermute | solution.py:32
  21.6 0.9 constant_dynamic-update-slice_fusion.11
  22.6 0.9 constant_dynamic-update-slice_fusion.9
  25.3 2.0 %collective-permute-done.6 = bf16[4,64,2048]{2,1,0:T(8,128)(2,1)S(1)} collective-permute-done((bf16[4,64,2048]{2,1,0:T(8,128)(2,1)S(1)}, bf16[4,64,2048]{2,1,0:T(8,128)(2,1)S(1)}, u32[]{:S(2)}, u32[]{:S(2)}) %collective-permute-start.6) | collective-permute-done | bytes 1048608 | tf_op jit(solution)/shard_map/ppermute | solution.py:28
  27.4 1.6 %collective-permute-start.8 = (bf16[128,2048]{1,0:T(8,128)(2,1)S(1)}, bf16[128,2048]{1,0:T(8,128)(2,1)S(1)}, u32[]{:S(2)}, u32[]{:S(2)}) collective-permute-start(bf16[128,2048]{1,0:T(8,128)(2,1)S(1)} %pad_maximum_fusion.5), channel_id=1, source_target_pairs={{0,16},{4,20},{8,24},{12,28},{16,0},{20,4},{24,8},{28,12},{1,17},{... | collective-permute-start | bytes 1572872 | tf_op jit(solution)/shard_map/ppermute | solution.py:28
  29.1 1.6 %collective-permute-start.7 = (bf16[128,2048]{1,0:T(8,128)(2,1)S(1)}, bf16[128,2048]{1,0:T(8,128)(2,1)S(1)}, u32[]{:S(2)}, u32[]{:S(2)}) collective-permute-start(bf16[128,2048]{1,0:T(8,128)(2,1)S(1)} %pad_maximum_fusion.4), channel_id=1, source_target_pairs={{0,8},{4,12},{8,0},{12,4},{16,24},{20,28},{24,16},{28,20},{1,9},{5... | collective-permute-start | bytes 1572872 | tf_op jit(solution)/shard_map/ppermute | solution.py:28
  30.6 1.9 %fusion.10 = f32[120,1408]{1,0:T(8,128)S(1)} fusion(bf16[120,2048]{1,0:T(8,128)(2,1)S(1)} %pad_maximum_fusion.7, bf16[1,1408,2048]{2,1,0:T(8,128)(2,1)S(1)} %bitcast.95), kind=kOutput, calls=%fused_computation.10 | convolution fusion | flops 692060160 | bytes 6934528 | tf_op jit(solution)/shard_map/dot_general | solution.py:17
  32.6 2.0 %fusion.17 = bf16[120,1408]{1,0:T(8,128)(2,1)S(1)} fusion(bf16[120,2048]{1,0:T(8,128)(2,1)S(1)} %pad_maximum_fusion.7, bf16[1,1408,2048]{2,1,0:T(8,128)(2,1)S(1)} %bitcast.117, f32[120,1408]{1,0:T(8,128)S(1)} %fusion.10), kind=kOutput, calls=%fused_computation.17 | convolution fusion | flops 693073920 | bytes 7272448 | tf_op jit(solution)/shard_map/dot_general | solution.py:17
  34.6 2.5 %collective-permute-start.11 = (bf16[120,1408]{1,0:T(8,128)(2,1)S(1)}, bf16[120,1408]{1,0:T(8,128)(2,1)S(1)}, u32[]{:S(2)}, u32[]{:S(2)}) collective-permute-start(bf16[120,1408]{1,0:T(8,128)(2,1)S(1)} %fusion.17), channel_id=1, source_target_pairs={{0,3},{1,2},{2,1},{3,0},{4,7},{5,6},{6,5},{7,4},{8,11},{9,10},{10,... | collective-permute-start | bytes 1013768 | tf_op jit(solution)/shard_map/ppermute | solution.py:32
  37.2 3.8 %collective-permute-start.13 = (bf16[120,1408]{1,0:T(8,128)(2,1)S(1)}, bf16[120,1408]{1,0:T(8,128)(2,1)S(1)}, u32[]{:S(2)}, u32[]{:S(2)}) collective-permute-start(bf16[120,1408]{1,0:T(8,128)(2,1)S(1)} %fusion.17), channel_id=1, source_target_pairs={{0,2},{3,1},{4,6},{7,5},{8,10},{11,9},{12,14},{15,13},{16,18},{19,... | collective-permute-start | bytes 1013768 | tf_op jit(solution)/shard_map/ppermute | solution.py:32
  41.1 6.3 %collective-permute-done.11 = bf16[120,1408]{1,0:T(8,128)(2,1)S(1)} collective-permute-done((bf16[120,1408]{1,0:T(8,128)(2,1)S(1)}, bf16[120,1408]{1,0:T(8,128)(2,1)S(1)}, u32[]{:S(2)}, u32[]{:S(2)}) %collective-permute-start.11) | collective-permute-done | bytes 337952 | tf_op jit(solution)/shard_map/ppermute | solution.py:32
  47.3 1.3 collective-permute-start.14
  49.9 1.7 %collective-permute-done.10 = bf16[4,256,512]{2,1,0:T(8,128)(2,1)S(1)} collective-permute-done((bf16[4,256,512]{2,1,0:T(8,128)(2,1)S(1)}, bf16[4,256,512]{2,1,0:T(8,128)(2,1)S(1)}, u32[]{:S(2)}, u32[]{:S(2)}) %collective-permute-start.10) | collective-permute-done | bytes 1048608 | tf_op jit(solution)/shard_map/ppermute | solution.py:28
  52.5 2.0 %fusion.8 = f32[240,1408]{1,0:T(8,128)S(1)} fusion(bf16[240,2048]{1,0:T(8,128)(2,1)S(1)} %pad_maximum_fusion.2, bf16[1,1408,2048]{2,1,0:T(8,128)(2,1)S(1)} %bitcast.95), kind=kOutput, calls=%fused_computation.8 | convolution fusion | flops 1384120320 | bytes 8101888 | tf_op jit(solution)/shard_map/dot_general | solution.py:17
  54.4 2.0 %multiply_convert_fusion = bf16[240,1408]{1,0:T(8,128)(2,1)S(1)} fusion(f32[240,1408]{1,0:T(8,128)S(1)} %fusion.8, bf16[240,2048]{1,0:T(8,128)(2,1)S(1)} %pad_maximum_fusion.2, bf16[1,1408,2048]{2,1,0:T(8,128)(2,1)S(1)} %bitcast.117), kind=kOutput, calls=%fused_computation.22 | convolution fusion | flops 1386147840 | bytes 8777728 | tf_op jit(solution)/shard_map/dot_general | solution.py:17
  56.5 2.5 %collective-permute-start.16 = (bf16[248,1408]{1,0:T(8,128)(2,1)S(1)}, bf16[248,1408]{1,0:T(8,128)(2,1)S(1)}, u32[]{:S(2)}, u32[]{:S(2)}) collective-permute-start(bf16[248,1408]{1,0:T(8,128)(2,1)S(1)} %pad_maximum_fusion.3), channel_id=1, source_target_pairs={{0,3},{1,2},{2,1},{3,0},{4,7},{5,6},{6,5},{7,4},{8,11},{9,10},{10,... | collective-permute-start | bytes 2095112 | tf_op jit(solution)/shard_map/ppermute | solution.py:32
  59.0 5.3 %collective-permute-done.9 = bf16[128,2048]{1,0:T(8,128)(2,1)S(1)} collective-permute-done((bf16[128,2048]{1,0:T(8,128)(2,1)S(1)}, bf16[128,2048]{1,0:T(8,128)(2,1)S(1)}, u32[]{:S(2)}, u32[]{:S(2)}) %collective-permute-start.9) | collective-permute-done | bytes 524320 | tf_op jit(solution)/shard_map/ppermute | solution.py:28
  64.2 3.9 %collective-permute-start.17 = (bf16[248,1408]{1,0:T(8,128)(2,1)S(1)}, bf16[248,1408]{1,0:T(8,128)(2,1)S(1)}, u32[]{:S(2)}, u32[]{:S(2)}) collective-permute-start(bf16[248,1408]{1,0:T(8,128)(2,1)S(1)} %pad_maximum_fusion.3), channel_id=1, source_target_pairs={{0,1},{1,0},{2,3},{3,2},{4,5},{5,4},{6,7},{7,6},{8,9},{9,8},{10,11... | collective-permute-start | bytes 2095112 | tf_op jit(solution)/shard_map/ppermute | solution.py:32
  68.3 2.6 %collective-permute-start.18 = (bf16[248,1408]{1,0:T(8,128)(2,1)S(1)}, bf16[248,1408]{1,0:T(8,128)(2,1)S(1)}, u32[]{:S(2)}, u32[]{:S(2)}) collective-permute-start(bf16[248,1408]{1,0:T(8,128)(2,1)S(1)} %pad_maximum_fusion.3), channel_id=1, source_target_pairs={{0,2},{3,1},{4,6},{7,5},{8,10},{11,9},{12,14},{15,13},{16,18},{19,... | collective-permute-start | bytes 2095112 | tf_op jit(solution)/shard_map/ppermute | solution.py:32
  70.9 1.9 %fusion.6 = f32[120,1408]{1,0:T(8,128)S(1)} fusion(bf16[120,2048]{1,0:T(8,128)(2,1)S(1)} %pad_maximum_fusion.8, bf16[1,1408,2048]{2,1,0:T(8,128)(2,1)S(1)} %bitcast.95), kind=kOutput, calls=%fused_computation.6 | convolution fusion | flops 692060160 | bytes 6934528 | tf_op jit(solution)/shard_map/dot_general | solution.py:17
  72.8 2.7 %multiply_convert_fusion.1 = bf16[120,1408]{1,0:T(8,128)(2,1)} fusion(f32[120,1408]{1,0:T(8,128)S(1)} %fusion.6, bf16[120,2048]{1,0:T(8,128)(2,1)S(1)} %pad_maximum_fusion.8, bf16[1,1408,2048]{2,1,0:T(8,128)(2,1)S(1)} %bitcast.117), kind=kOutput, calls=%fused_computation.41 | convolution fusion | flops 693073920 | bytes 7272448 | tf_op jit(solution)/shard_map/dot_general | solution.py:17
  75.6 1.9 %collective-permute-start.20 = (bf16[120,1408]{1,0:T(8,128)(2,1)}, bf16[120,1408]{1,0:T(8,128)(2,1)S(1)}, u32[]{:S(2)}, u32[]{:S(2)}) collective-permute-start(bf16[120,1408]{1,0:T(8,128)(2,1)} %multiply_convert_fusion.1), channel_id=1, source_target_pairs={{0,3},{1,2},{2,1},{3,0},{4,7},{5,6},{6,5},{7,4},{8,11},{9,10},{10,... | collective-permute-start | bytes 1013768 | tf_op jit(solution)/shard_map/ppermute | solution.py:32
  78.7 0.9 convolution_convert_fusion.2
  79.7 13.7 %collective-permute-start.15 = (bf16[120,1408]{1,0:T(8,128)(2,1)}, bf16[120,1408]{1,0:T(8,128)(2,1)}, u32[]{:S(2)}, u32[]{:S(2)}) collective-permute-start(bf16[120,1408]{1,0:T(8,128)(2,1)} %multiply_convert_fusion.1), channel_id=1, source_target_pairs={{0,2},{1,3},{2,0},{3,1},{4,6},{5,7},{6,4},{7,5},{8,10},{9,11},{10,... | collective-permute-start | bytes 1013768 | tf_op jit(solution)/shard_map/ppermute | solution.py:32
  93.4 1.3 collective-permute-start.19
  94.7 10.4 %collective-permute-done.18 = bf16[248,1408]{1,0:T(8,128)(2,1)S(1)} collective-permute-done((bf16[248,1408]{1,0:T(8,128)(2,1)S(1)}, bf16[248,1408]{1,0:T(8,128)(2,1)S(1)}, u32[]{:S(2)}, u32[]{:S(2)}) %collective-permute-start.18) | collective-permute-done | bytes 698400 | tf_op jit(solution)/shard_map/ppermute | solution.py:32
  105.3 1.0 constant_dynamic-update-slice_fusion.2
  106.5 14.1 %collective-permute-done.19 = bf16[248,1408]{1,0:T(8,128)(2,1)S(1)} collective-permute-done((bf16[248,1408]{1,0:T(8,128)(2,1)S(1)}, bf16[248,1408]{1,0:T(8,128)(2,1)S(1)}, u32[]{:S(2)}, u32[]{:S(2)}) %collective-permute-start.19) | collective-permute-done | bytes 698400 | tf_op jit(solution)/shard_map/ppermute | solution.py:32
  120.8 2.3 %fusion.24 = bf16[240,512]{1,0:T(8,128)(2,1)} fusion(bf16[248,5632]{1,0:T(8,128)(2,1)S(1)} %add_dynamic-update-slice_fusion, bf16[1,5632,512]{2,1,0:T(8,128)(2,1)S(1)} %bitcast.92), kind=kOutput, calls=%fused_computation.27 | convolution fusion | flops 1384243200 | bytes 8716288 | tf_op jit(solution)/shard_map/dot_general | solution.py:261
  123.2 0.9 fusion.84
  125.0 0.8 collective-permute-start.23
  126.2 3.1 %collective-permute-done.22 = bf16[120,512]{1,0:T(8,128)(2,1)S(1)} collective-permute-done((bf16[120,512]{1,0:T(8,128)(2,1)S(1)}, bf16[120,512]{1,0:T(8,128)(2,1)S(1)}, u32[]{:S(2)}, u32[]{:S(2)}) %collective-permute-start.22) | collective-permute-done | bytes 122912 | tf_op jit(solution)/shard_map/ppermute | solution.py:28
  129.9 5.1 %collective-permute-done.15 = bf16[120,1408]{1,0:T(8,128)(2,1)} collective-permute-done((bf16[120,1408]{1,0:T(8,128)(2,1)}, bf16[120,1408]{1,0:T(8,128)(2,1)}, u32[]{:S(2)}, u32[]{:S(2)}) %collective-permute-start.15) | collective-permute-done | bytes 337952 | tf_op jit(solution)/shard_map/ppermute | solution.py:32
  135.0 1.3 fusion.99
  136.5 0.9 collective-permute-start.25
  137.4 1.5 %collective-permute-start.26 = (bf16[60,512]{1,0:T(8,128)(2,1)S(1)}, bf16[60,512]{1,0:T(8,128)(2,1)S(1)}, u32[]{:S(2)}, u32[]{:S(2)}) collective-permute-start(bf16[60,512]{1,0:T(8,128)(2,1)S(1)} %get-tuple-element.144), channel_id=1, source_target_pairs={{0,28},{4,24},{8,20},{12,16},{16,12},{20,8},{24,4},{28,0},{1,29},{... | collective-permute-start | bytes 184328 | tf_op jit(solution)/shard_map/ppermute | solution.py:28
  138.9 0.8 collective-permute-start.24
  140.1 2.1 %collective-permute-done.25 = bf16[60,512]{1,0:T(8,128)(2,1)S(1)} collective-permute-done((bf16[60,512]{1,0:T(8,128)(2,1)S(1)}, bf16[60,512]{1,0:T(8,128)(2,1)S(1)}, u32[]{:S(2)}, u32[]{:S(2)}) %collective-permute-start.25) | collective-permute-done | bytes 61472 | tf_op jit(solution)/shard_map/ppermute | solution.py:28
  143.6 0.9 add_convert_fusion
  (141 shorter events, 11.7 us)
Async XLA Ops:
  0.0 13.3 %copy-start.1 = (s32[160,2]{0,1:T(2,128)S(1)}, s32[160,2]{0,1:T(2,128)}, u32[]{:S(2)}) copy-start(s32[160,2]{0,1:T(2,128)} %param.15) | copy-start | bytes 3844
  0.0 13.3 %copy-start.3 = (s32[16]{0:T(128)S(1)}, s32[16]{0:T(128)}, u32[]{:S(2)}) copy-start(s32[16]{0:T(128)} %param.13) | copy-start | bytes 196
  0.0 13.6 %copy-start.4 = (s32[16]{0:T(128)S(1)}, s32[16]{0:T(128)}, u32[]{:S(2)}) copy-start(s32[16]{0:T(128)} %param.14) | copy-start | bytes 196
  1.8 12.1 %collective-permute-start = (bf16[168,512]{1,0:T(8,128)(2,1)S(1)}, bf16[168,512]{1,0:T(8,128)(2,1)S(1)}, u32[]{:S(2)}, u32[]{:S(2)}) collective-permute-start(bf16[168,512]{1,0:T(8,128)(2,1)S(1)} %get-tuple-element.138), channel_id=1, source_target_pairs={{0,3},{1,2},{2,1},{3,0},{4,7},{5,6},{6,5},{7,4},{8,11},{9,10},{10,... | collective-permute-start | bytes 516104 | tf_op jit(solution)/shard_map/ppermute | solution.py:32
  6.9 9.3 %collective-permute-start.1 = (bf16[168,512]{1,0:T(8,128)(2,1)S(1)}, bf16[168,512]{1,0:T(8,128)(2,1)}, u32[]{:S(2)}, u32[]{:S(2)}) collective-permute-start(bf16[168,512]{1,0:T(8,128)(2,1)S(1)} %get-tuple-element.138), channel_id=1, source_target_pairs={{0,1},{1,0},{2,3},{3,2},{4,5},{5,4},{6,7},{7,6},{8,9},{9,8},{10,11... | collective-permute-start | bytes 516104 | tf_op jit(solution)/shard_map/ppermute | solution.py:32
  6.9 14.7 %collective-permute-start.2 = (bf16[168,512]{1,0:T(8,128)(2,1)S(1)}, bf16[168,512]{1,0:T(8,128)(2,1)}, u32[]{:S(2)}, u32[]{:S(2)}) collective-permute-start(bf16[168,512]{1,0:T(8,128)(2,1)S(1)} %get-tuple-element.138), channel_id=1, source_target_pairs={{0,2},{1,3},{2,0},{3,1},{4,6},{5,7},{6,4},{7,5},{8,10},{9,11},{10,... | collective-permute-start | bytes 516104 | tf_op jit(solution)/shard_map/ppermute | solution.py:32
  8.6 15.4 %collective-permute-start.3 = (bf16[256,512]{1,0:T(8,128)(2,1)S(1)}, bf16[256,512]{1,0:T(8,128)(2,1)S(1)}, u32[]{:S(2)}, u32[]{:S(2)}) collective-permute-start(bf16[256,512]{1,0:T(8,128)(2,1)S(1)} %bitcast.100), channel_id=1, source_target_pairs={{0,8},{4,12},{8,0},{12,4},{16,24},{20,28},{24,16},{28,20},{1,9},{5... | collective-permute-start | bytes 786440 | tf_op jit(solution)/shard_map/ppermute | solution.py:28
  10.3 13.8 %collective-permute-start.4 = (bf16[256,512]{1,0:T(8,128)(2,1)S(1)}, bf16[256,512]{1,0:T(8,128)(2,1)S(1)}, u32[]{:S(2)}, u32[]{:S(2)}) collective-permute-start(bf16[256,512]{1,0:T(8,128)(2,1)S(1)} %bitcast.101), channel_id=1, source_target_pairs={{0,16},{4,20},{8,24},{12,28},{16,0},{20,4},{24,8},{28,12},{1,17},{... | collective-permute-start | bytes 786440 | tf_op jit(solution)/shard_map/ppermute | solution.py:28
  11.8 18.8 %slice-start.2 = ((s8[5767168]{0:T(1024)(128)(4,1)}), s8[1572864]{0:T(1024)(128)(4,1)S(1)}, s32[]{:S(2)}) async-start(s8[5767168]{0:T(1024)(128)(4,1)} %bitcast.94), calls=%async_computation.2 | async-start | bytes 3145728
  13.9 10.1 %collective-permute-start.5 = (bf16[256,512]{1,0:T(8,128)(2,1)S(1)}, bf16[256,512]{1,0:T(8,128)(2,1)S(1)}, u32[]{:S(2)}, u32[]{:S(2)}) collective-permute-start(bf16[256,512]{1,0:T(8,128)(2,1)S(1)} %bitcast.102), channel_id=1, source_target_pairs={{0,24},{4,28},{8,16},{12,20},{16,8},{20,12},{24,0},{28,4},{1,25},{... | collective-permute-start | bytes 786440 | tf_op jit(solution)/shard_map/ppermute | solution.py:28
  24.5 2.7 %collective-permute-start.6 = (bf16[4,64,2048]{2,1,0:T(8,128)(2,1)S(1)}, bf16[4,64,2048]{2,1,0:T(8,128)(2,1)S(1)}, u32[]{:S(2)}, u32[]{:S(2)}) collective-permute-start(bf16[4,64,2048]{2,1,0:T(8,128)(2,1)S(1)} %bitcast.99), channel_id=1, source_target_pairs={{0,4},{4,0},{8,12},{12,8},{16,20},{20,16},{24,28},{28,24},{1,5},{5... | collective-permute-start | bytes 3145736 | tf_op jit(solution)/shard_map/ppermute | solution.py:28
  24.7 6.0 %slice-start.3 = ((s8[5767168]{0:T(1024)(128)(4,1)}), s8[4194304]{0:T(1024)(128)(4,1)S(1)}, s32[]{:S(2)}) async-start(s8[5767168]{0:T(1024)(128)(4,1)} %bitcast.94), calls=%async_computation.3 | async-start | bytes 8388608
  25.1 7.4 %slice-start.4 = ((s8[5767168]{0:T(1024)(128)(4,1)}), s8[4194304]{0:T(1024)(128)(4,1)S(1)}, s32[]{:S(2)}) async-start(s8[5767168]{0:T(1024)(128)(4,1)} %bitcast.116), calls=%async_computation.4 | async-start | bytes 8388608
  27.4 21.2 %collective-permute-start.8 = (bf16[128,2048]{1,0:T(8,128)(2,1)S(1)}, bf16[128,2048]{1,0:T(8,128)(2,1)S(1)}, u32[]{:S(2)}, u32[]{:S(2)}) collective-permute-start(bf16[128,2048]{1,0:T(8,128)(2,1)S(1)} %pad_maximum_fusion.5), channel_id=1, source_target_pairs={{0,16},{4,20},{8,24},{12,28},{16,0},{20,4},{24,8},{28,12},{1,17},{... | collective-permute-start | bytes 1572872 | tf_op jit(solution)/shard_map/ppermute | solution.py:28
  29.0 3.5 %slice-start.5 = ((s8[5767168]{0:T(1024)(128)(4,1)}), s8[1572864]{0:T(1024)(128)(4,1)S(1)}, s32[]{:S(2)}) async-start(s8[5767168]{0:T(1024)(128)(4,1)} %bitcast.116), calls=%async_computation.5 | async-start | bytes 3145728
  29.1 19.6 %collective-permute-start.7 = (bf16[128,2048]{1,0:T(8,128)(2,1)S(1)}, bf16[128,2048]{1,0:T(8,128)(2,1)S(1)}, u32[]{:S(2)}, u32[]{:S(2)}) collective-permute-start(bf16[128,2048]{1,0:T(8,128)(2,1)S(1)} %pad_maximum_fusion.4), channel_id=1, source_target_pairs={{0,8},{4,12},{8,0},{12,4},{16,24},{20,28},{24,16},{28,20},{1,9},{5... | collective-permute-start | bytes 1572872 | tf_op jit(solution)/shard_map/ppermute | solution.py:28
  34.6 12.8 %collective-permute-start.11 = (bf16[120,1408]{1,0:T(8,128)(2,1)S(1)}, bf16[120,1408]{1,0:T(8,128)(2,1)S(1)}, u32[]{:S(2)}, u32[]{:S(2)}) collective-permute-start(bf16[120,1408]{1,0:T(8,128)(2,1)S(1)} %fusion.17), channel_id=1, source_target_pairs={{0,3},{1,2},{2,1},{3,0},{4,7},{5,6},{6,5},{7,4},{8,11},{9,10},{10,... | collective-permute-start | bytes 1013768 | tf_op jit(solution)/shard_map/ppermute | solution.py:32
  37.1 31.1 %collective-permute-start.12 = (bf16[120,1408]{1,0:T(8,128)(2,1)S(1)}, bf16[120,1408]{1,0:T(8,128)(2,1)S(1)}, u32[]{:S(2)}, u32[]{:S(2)}) collective-permute-start(bf16[120,1408]{1,0:T(8,128)(2,1)S(1)} %fusion.17), channel_id=1, source_target_pairs={{0,1},{1,0},{2,3},{3,2},{4,5},{5,4},{6,7},{7,6},{8,9},{9,8},{10,11... | collective-permute-start | bytes 1013768 | tf_op jit(solution)/shard_map/ppermute | solution.py:32
  37.2 33.7 %collective-permute-start.13 = (bf16[120,1408]{1,0:T(8,128)(2,1)S(1)}, bf16[120,1408]{1,0:T(8,128)(2,1)S(1)}, u32[]{:S(2)}, u32[]{:S(2)}) collective-permute-start(bf16[120,1408]{1,0:T(8,128)(2,1)S(1)} %fusion.17), channel_id=1, source_target_pairs={{0,2},{3,1},{4,6},{7,5},{8,10},{11,9},{12,14},{15,13},{16,18},{19,... | collective-permute-start | bytes 1013768 | tf_op jit(solution)/shard_map/ppermute | solution.py:32
  47.3 23.5 %collective-permute-start.14 = (bf16[120,1408]{1,0:T(8,128)(2,1)S(1)}, bf16[120,1408]{1,0:T(8,128)(2,1)S(1)}, u32[]{:S(2)}, u32[]{:S(2)}) collective-permute-start(bf16[120,1408]{1,0:T(8,128)(2,1)S(1)} %collective-permute-done.11), channel_id=1, source_target_pairs={{1,0},{2,3},{5,4},{6,7},{9,8},{10,11},{13,12},{14,15},{17,16},{18,... | collective-permute-start | bytes 1013768 | tf_op jit(solution)/shard_map/ppermute | solution.py:32
  48.8 2.7 %collective-permute-start.10 = (bf16[4,256,512]{2,1,0:T(8,128)(2,1)S(1)}, bf16[4,256,512]{2,1,0:T(8,128)(2,1)S(1)}, u32[]{:S(2)}, u32[]{:S(2)}) collective-permute-start(bf16[4,256,512]{2,1,0:T(8,128)(2,1)S(1)} %get-tuple-element.122), channel_id=1, source_target_pairs={{0,4},{4,0},{8,12},{12,8},{16,20},{20,16},{24,28},{28,24},{1,5},{5... | collective-permute-start | bytes 3145736 | tf_op jit(solution)/shard_map/ppermute | solution.py:28
  49.0 15.3 %collective-permute-start.9 = (bf16[128,2048]{1,0:T(8,128)(2,1)S(1)}, bf16[128,2048]{1,0:T(8,128)(2,1)S(1)}, u32[]{:S(2)}, u32[]{:S(2)}) collective-permute-start(bf16[128,2048]{1,0:T(8,128)(2,1)S(1)} %pad_maximum_fusion.6), channel_id=1, source_target_pairs={{0,24},{4,28},{8,16},{12,20},{16,8},{20,12},{24,0},{28,4},{1,25},{... | collective-permute-start | bytes 1572872 | tf_op jit(solution)/shard_map/ppermute | solution.py:28
  56.5 23.2 %collective-permute-start.16 = (bf16[248,1408]{1,0:T(8,128)(2,1)S(1)}, bf16[248,1408]{1,0:T(8,128)(2,1)S(1)}, u32[]{:S(2)}, u32[]{:S(2)}) collective-permute-start(bf16[248,1408]{1,0:T(8,128)(2,1)S(1)} %pad_maximum_fusion.3), channel_id=1, source_target_pairs={{0,3},{1,2},{2,1},{3,0},{4,7},{5,6},{6,5},{7,4},{8,11},{9,10},{10,... | collective-permute-start | bytes 2095112 | tf_op jit(solution)/shard_map/ppermute | solution.py:32
  64.2 29.2 %collective-permute-start.17 = (bf16[248,1408]{1,0:T(8,128)(2,1)S(1)}, bf16[248,1408]{1,0:T(8,128)(2,1)S(1)}, u32[]{:S(2)}, u32[]{:S(2)}) collective-permute-start(bf16[248,1408]{1,0:T(8,128)(2,1)S(1)} %pad_maximum_fusion.3), channel_id=1, source_target_pairs={{0,1},{1,0},{2,3},{3,2},{4,5},{5,4},{6,7},{7,6},{8,9},{9,8},{10,11... | collective-permute-start | bytes 2095112 | tf_op jit(solution)/shard_map/ppermute | solution.py:32
  68.3 36.8 %collective-permute-start.18 = (bf16[248,1408]{1,0:T(8,128)(2,1)S(1)}, bf16[248,1408]{1,0:T(8,128)(2,1)S(1)}, u32[]{:S(2)}, u32[]{:S(2)}) collective-permute-start(bf16[248,1408]{1,0:T(8,128)(2,1)S(1)} %pad_maximum_fusion.3), channel_id=1, source_target_pairs={{0,2},{3,1},{4,6},{7,5},{8,10},{11,9},{12,14},{15,13},{16,18},{19,... | collective-permute-start | bytes 2095112 | tf_op jit(solution)/shard_map/ppermute | solution.py:32
  70.9 7.8 %slice-start = ((s8[5767168]{0:T(1024)(128)(4,1)}), s8[4194304]{0:T(1024)(128)(4,1)S(1)}, s32[]{:S(2)}) async-start(s8[5767168]{0:T(1024)(128)(4,1)} %bitcast.91), calls=%async_computation | async-start | bytes 8388608
  72.8 5.9 %slice-start.1 = ((s8[5767168]{0:T(1024)(128)(4,1)}), s8[1572864]{0:T(1024)(128)(4,1)S(1)}, s32[]{:S(2)}) async-start(s8[5767168]{0:T(1024)(128)(4,1)} %bitcast.91), calls=%async_computation.1 | async-start | bytes 3145728
  75.6 47.5 %collective-permute-start.20 = (bf16[120,1408]{1,0:T(8,128)(2,1)}, bf16[120,1408]{1,0:T(8,128)(2,1)S(1)}, u32[]{:S(2)}, u32[]{:S(2)}) collective-permute-start(bf16[120,1408]{1,0:T(8,128)(2,1)} %multiply_convert_fusion.1), channel_id=1, source_target_pairs={{0,3},{1,2},{2,1},{3,0},{4,7},{5,6},{6,5},{7,4},{8,11},{9,10},{10,... | collective-permute-start | bytes 1013768 | tf_op jit(solution)/shard_map/ppermute | solution.py:32
  77.5 45.6 %collective-permute-start.21 = (bf16[120,1408]{1,0:T(8,128)(2,1)}, bf16[120,1408]{1,0:T(8,128)(2,1)S(1)}, u32[]{:S(2)}, u32[]{:S(2)}) collective-permute-start(bf16[120,1408]{1,0:T(8,128)(2,1)} %multiply_convert_fusion.1), channel_id=1, source_target_pairs={{0,1},{1,0},{2,3},{3,2},{4,5},{5,4},{6,7},{7,6},{8,9},{9,8},{10,11... | collective-permute-start | bytes 1013768 | tf_op jit(solution)/shard_map/ppermute | solution.py:32
  77.7 0.7 copy-start.2
  79.7 55.3 %collective-permute-start.15 = (bf16[120,1408]{1,0:T(8,128)(2,1)}, bf16[120,1408]{1,0:T(8,128)(2,1)}, u32[]{:S(2)}, u32[]{:S(2)}) collective-permute-start(bf16[120,1408]{1,0:T(8,128)(2,1)} %multiply_convert_fusion.1), channel_id=1, source_target_pairs={{0,2},{1,3},{2,0},{3,1},{4,6},{5,7},{6,4},{7,5},{8,10},{9,11},{10,... | collective-permute-start | bytes 1013768 | tf_op jit(solution)/shard_map/ppermute | solution.py:32
  93.4 27.1 %collective-permute-start.19 = (bf16[248,1408]{1,0:T(8,128)(2,1)S(1)}, bf16[248,1408]{1,0:T(8,128)(2,1)S(1)}, u32[]{:S(2)}, u32[]{:S(2)}) collective-permute-start(bf16[248,1408]{1,0:T(8,128)(2,1)S(1)} %collective-permute-done.16), channel_id=1, source_target_pairs={{1,0},{2,3},{5,4},{6,7},{9,8},{10,11},{13,12},{14,15},{17,16},{18,... | collective-permute-start | bytes 2095112 | tf_op jit(solution)/shard_map/ppermute | solution.py:32
  123.2 1.1 copy-start
  124.3 4.9 %collective-permute-start.22 = (bf16[120,512]{1,0:T(8,128)(2,1)S(1)}, bf16[120,512]{1,0:T(8,128)(2,1)S(1)}, u32[]{:S(2)}, u32[]{:S(2)}) collective-permute-start(bf16[120,512]{1,0:T(8,128)(2,1)S(1)} %get-tuple-element.135), channel_id=1, source_target_pairs={{0,8},{4,12},{8,0},{12,4},{16,24},{20,28},{24,16},{28,20},{1,9},{5... | collective-permute-start | bytes 368648 | tf_op jit(solution)/shard_map/ppermute | solution.py:28
  125.0 4.9 %collective-permute-start.23 = (bf16[120,512]{1,0:T(8,128)(2,1)S(1)}, bf16[120,512]{1,0:T(8,128)(2,1)S(1)}, u32[]{:S(2)}, u32[]{:S(2)}) collective-permute-start(bf16[120,512]{1,0:T(8,128)(2,1)S(1)} %get-tuple-element.136), channel_id=1, source_target_pairs={{0,16},{4,20},{8,24},{12,28},{16,0},{20,4},{24,8},{28,12},{1,17},{... | collective-permute-start | bytes 368648 | tf_op jit(solution)/shard_map/ppermute | solution.py:28
  136.5 5.7 %collective-permute-start.25 = (bf16[60,512]{1,0:T(8,128)(2,1)S(1)}, bf16[60,512]{1,0:T(8,128)(2,1)S(1)}, u32[]{:S(2)}, u32[]{:S(2)}) collective-permute-start(bf16[60,512]{1,0:T(8,128)(2,1)S(1)} %get-tuple-element.143), channel_id=1, source_target_pairs={{0,24},{4,28},{8,16},{12,20},{16,8},{20,12},{24,0},{28,4},{1,25},{... | collective-permute-start | bytes 184328 | tf_op jit(solution)/shard_map/ppermute | solution.py:28
  137.4 5.3 %collective-permute-start.26 = (bf16[60,512]{1,0:T(8,128)(2,1)S(1)}, bf16[60,512]{1,0:T(8,128)(2,1)S(1)}, u32[]{:S(2)}, u32[]{:S(2)}) collective-permute-start(bf16[60,512]{1,0:T(8,128)(2,1)S(1)} %get-tuple-element.144), channel_id=1, source_target_pairs={{0,28},{4,24},{8,20},{12,16},{16,12},{20,8},{24,4},{28,0},{1,29},{... | collective-permute-start | bytes 184328 | tf_op jit(solution)/shard_map/ppermute | solution.py:28
  138.9 4.3 %collective-permute-start.24 = (bf16[3,60,512]{2,1,0:T(8,128)(2,1)S(1)}, bf16[3,60,512]{2,1,0:T(8,128)(2,1)S(1)}, u32[]{:S(2)}, u32[]{:S(2)}) collective-permute-start(bf16[3,60,512]{2,1,0:T(8,128)(2,1)S(1)} %slice.203), channel_id=1, source_target_pairs={{0,4},{4,0},{8,12},{12,8},{16,20},{20,16},{24,28},{28,24},{1,5},{5... | collective-permute-start | bytes 552968 | tf_op jit(solution)/shard_map/ppermute | solution.py:28

commit v4 on v3

--- a/solution.py
+++ b/solution.py
@@ -37,14 +37,11 @@
 OVER = [(0, 2), (3, 1)]
 FACING = [(0, 2), (1, 3), (2, 0), (3, 1)]
 OUTWARD = [(1, 0), (2, 3)]
-
-
-def first_hops(value, whole):
-    return (
-        along(value, MIRROR),
-        along(value, BESIDE),
-        along(value, FACING if whole else OVER),
-    )
+ACROSS = [(1, 2), (2, 1)]
+
+
+def first_hops(value, mirror, facing):
+    return along(value, mirror), along(value, BESIDE), along(value, facing)
 
 
 def in_line(value, mirror, beside, facing):
@@ -143,7 +140,7 @@
     sent = jnp.concatenate(
         [tokens, jnp.pad(gain_parts, ((0, GAIN_ROWS - 3), (0, 0)))], axis=0
     )
-    hops = first_hops(sent, True) if line else ring_gather(sent)
+    hops = first_hops(sent, MIRROR, FACING) if line else ring_gather(sent)
 
     local_adapters = adapter_down.shape[0]
     mine = jnp.concatenate([jnp.transpose(adapter_down, (0, 2, 1)), adapter_up], axis=0)
@@ -180,7 +177,9 @@
         placed = jnp.dot(of_token[core], normed, preferred_element_type=jnp.float32)
         return placed.astype(jnp.bfloat16).reshape(chips, SLOTS, D)
 
-    partner_half = row_xor(outgoing(1), 1)
+    there_half = outgoing(1)
+    partner_own = row_xor(there_half[0], 1)
+    partner_half = [partner_own] + list(row_xor(there_half[1:], 1))
     here_half = outgoing(0)
 
     groups = [[0], list(range(1, chips - 1)), [chips - 1]]
@@ -208,11 +207,11 @@
         value = (jax.nn.silu(gate_sum) * up_sum).astype(jnp.bfloat16)
         return value, earlier
 
-    def first_of(value, whole):
-        return list(first_hops(value, whole)) if line else ring_gather(value)
+    def first_of(value, *pairs_of):
+        return list(first_hops(value, *pairs_of)) if line else ring_gather(value)
 
     value, _ = hidden_of(groups[0], [])
-    hidden, hops = [value], [first_of(value, False)]
+    hidden, hops = [value], [first_of(value, MIRROR, OVER)]
 
     hidden[0], pairs[1:-1], by_chip = tie(hidden[0], pairs[1:-1], by_chip)
     factors = both_cores(jnp.stack(by_chip))
@@ -239,15 +238,17 @@
         extra = jnp.concatenate([jnp.pad(piece, ((0, 0), spare)) for piece in pieces], axis=1)
         extra = jnp.pad(extra, ((0, 0), (0, hidden_part - extra.shape[1])))
 
+    if line:
+        hops[0][0], extra = tie(hops[0][0], extra)
     passed = along(hops[0][0], OUTWARD) if line else None
     value, (extra, *hops[0][:1]) = hidden_of(groups[1], [extra] + hops[0][:1])
     hidden.append(jnp.concatenate([value, extra], axis=0))
-    hops.append(first_of(hidden[1], False))
+    hops.append(first_of(hidden[1], ACROSS, OVER))
     earlier = hops[0][1:] + [passed] if line else []
     pairs[-1], hidden[1] = tie(pairs[-1], hidden[1])
     value, (hidden[1], *earlier) = hidden_of(groups[2], [hidden[1]] + earlier)
     hidden.append(value)
-    hops.append(first_of(value, True))
+    hops.append(first_of(value, MIRROR, OVER))
     if line:
         beside, over, passed = earlier
         hops[0] = [hops[0][0], beside, over + passed]
@@ -288,14 +289,16 @@
     if line:
         mirror, beside, over = hops[1]
         mirror, hidden[2], returned[0], late_down = tie(mirror, hidden[2], out, unit_down)
-        passed = along(mirror, OUTWARD)
-        beside, over, mirror = tie(beside, over, mirror)
-        hops[1] = [mirror, beside, over + passed]
+        near = along(mirror, OUTWARD)
+        beside, mirror = tie(beside, mirror)
+        over, beside = tie(over, beside)
+        hops[1] = [mirror + along(over, OUTWARD), beside, over + near]
+        hops[2][0], over = tie(hops[2][0], over)
+        hops[1][2] = over + near
+        passed = along(hops[2][0], OUTWARD)
     whole = whole_of(1)
     count = len(groups[1]) * 2 * CAP
     out = block_sum(whole[:count]).astype(jnp.bfloat16)
-    if line:
-        out, *hops[2][:2] = tie(out, *hops[2][:2])
     for index, offset in enumerate(groups[1]):
         returned.append(row_xor(out[index * 2 * CAP : (index + 1) * 2 * CAP], 2 * offset))
     if line:
@@ -312,26 +315,24 @@
     branch = lax.dot_general(
         expanded, up_rows, (((0,), (0,)), ((), ())), preferred_element_type=jnp.float32
     )
-    near = jnp.stack(returned)
-    near_others = row_xor(near[:, CAP:], 1)
     if line:
         mirror, beside, facing = hops[2]
         part = block_sum(in_line(hidden[2], mirror, beside, jnp.zeros_like(mirror)))
         facing_down = lax.dynamic_slice(
             late_down, ((col_at ^ 2) * hidden_part, 0), (hidden_part, width_part)
         )
-        facing, near, branch, part, facing_down, place_weights = tie(
-            facing, near, branch, part, facing_down, place_weights
-        )
-        out = part + jnp.dot(facing, facing_down, preferred_element_type=jnp.float32)
+        facing, passed, branch, part, facing_down, place_weights = tie(
+            facing, passed, branch, part, facing_down, place_weights
+        )
+        out = part + jnp.dot(facing + passed, facing_down, preferred_element_type=jnp.float32)
     else:
         out = block_sum(whole_of(2))
     out = out.astype(jnp.bfloat16)
-    far = [row_xor(out[:CAP], 2 * chips - 2), row_xor(out[CAP:], 2 * chips - 1)]
-    near, out = tie(near, out)
+    returned.append(row_xor(out, 2 * chips - 2))
+    near = jnp.stack(returned)
+    near_others = row_xor(near[:, CAP:], 1)
     near = [near[:, :CAP].reshape(-1, width_part), near_others.reshape(-1, width_part)]
     mixed = branch + weighted([(0, rows) for rows in near])
-    mixed = mixed + weighted([((chips - 1) * CAP, rows) for rows in far])
     return mixed.astype(jnp.bfloat16)
 
 

time: 145 us -> 141 us (0.972)
  starting transfers between devices: 51.9 us -> 44.8 us
  waiting for transfers between devices: 57.6 us -> 60.6 us
  other arithmetic: 5.34 us -> 7.66 us
    ppermute x14 -> x16, starting transfers between devices: 39.4 us -> 31 us  [along(): return lax.ppermute(value, 'col', pairs)]
    ppermute x14 -> x16, waiting for transfers between devices: 42.6 us -> 44.5 us  [along(): return lax.ppermute(value, 'col', pairs)]
    dot_general x8 -> x4, matrix products: 2.4 us -> 0.78 us  [weighted(): lax.dot_general(part[first:first + rows.shape[0]], rows, (((0,), (0,)), (...]
    dynamic_update_slice x13 -> x12, local copies, waits for them, and re-layouts: 3.39 us -> 4.29 us  [side_by_side(): whole = lax.dynamic_update_slice(whole, block, (first, sender * width))]
  transfers between devices with their start and end apart: 27 -> 29, of which waited for: 13 -> 15; matrix products, arithmetic and copies ran while one was open for 20% -> 20% of each run, Pallas kernels for 0% -> 0%
where the time goes in v4:
time: 141 us
  waiting for transfers between devices  60.6 us (43%)
  starting transfers between devices  44.8 us (32%)
  matrix products  20.9 us (15%)
  other arithmetic  7.66 us (5%)
  local copies, waits for them, and re-layouts  6.2 us (4%)
    ppermute x16, waiting for transfers between devices, along(): return lax.ppermute(value, 'col', pairs)  44.5 us
    ppermute x16, starting transfers between devices, along(): return lax.ppermute(value, 'col', pairs)  31 us
    ppermute x13, waiting for transfers between devices, row_xor(): lax.ppermute(value, 'row', [(i, i ^ by) for i in range(lax.axis_size('row...  16.2 us
    ppermute x13, starting transfers between devices, row_xor(): lax.ppermute(value, 'row', [(i, i ^ by) for i in range(lax.axis_size('row...  13.8 us
    dot_general x7, matrix products, contract_last(): lax.dot_general(left, right, (((1,), (1,)), ((), ())), preferred_element_...  13 us
    dynamic_update_slice x12, local copies, waits for them, and re-layouts, side_by_side(): whole = lax.dynamic_update_slice(whole, block, (first, sender * width))  4.29 us
    dot_general x3, matrix products, block_sum(): return jnp.dot(whole, unit_down, preferred_element_type=jnp.float32)  4.15 us
  transfers between devices with their start and end apart: 29, of which 15 were waited for; matrix products, arithmetic and copies ran while one was open for 20% of the time, Pallas kernels for 0%

profile of v4, /device:TPU:0, one launch (start us, length us, event | category | flops | bytes accessed | tf_op | source)
XLA Modules:
  0.0 141.0 jit_solution(15711908171092995106)
XLA Ops:
  0.9 1.1 constant_dynamic-update-slice_fusion.11
  1.9 5.1 %collective-permute-start = (bf16[168,512]{1,0:T(8,128)(2,1)S(1)}, bf16[168,512]{1,0:T(8,128)(2,1)S(1)}, u32[]{:S(2)}, u32[]{:S(2)}) collective-permute-start(bf16[168,512]{1,0:T(8,128)(2,1)S(1)} %get-tuple-element.142), channel_id=1, source_target_pairs={{0,3},{1,2},{2,1},{3,0},{4,7},{5,6},{6,5},{7,4},{8,11},{9,10},{10,... | collective-permute-start | bytes 516104 | tf_op jit(solution)/shard_map/ppermute | solution.py:32
  7.7 1.0 pad_maximum_fusion.10
  8.7 1.7 %collective-permute-start.3 = (bf16[256,512]{1,0:T(8,128)(2,1)S(1)}, bf16[256,512]{1,0:T(8,128)(2,1)S(1)}, u32[]{:S(2)}, u32[]{:S(2)}) collective-permute-start(bf16[256,512]{1,0:T(8,128)(2,1)S(1)} %bitcast.100), channel_id=1, source_target_pairs={{0,8},{4,12},{8,0},{12,4},{16,24},{20,28},{24,16},{28,20},{1,9},{5... | collective-permute-start | bytes 786440 | tf_op jit(solution)/shard_map/ppermute | solution.py:28
  10.4 1.5 %collective-permute-start.4 = (bf16[256,512]{1,0:T(8,128)(2,1)S(1)}, bf16[256,512]{1,0:T(8,128)(2,1)S(1)}, u32[]{:S(2)}, u32[]{:S(2)}) collective-permute-start(bf16[256,512]{1,0:T(8,128)(2,1)S(1)} %bitcast.101), channel_id=1, source_target_pairs={{0,16},{4,20},{8,24},{12,28},{16,0},{20,4},{24,8},{28,12},{1,17},{... | collective-permute-start | bytes 786440 | tf_op jit(solution)/shard_map/ppermute | solution.py:28
  13.4 1.6 %collective-permute-start.5 = (bf16[256,512]{1,0:T(8,128)(2,1)S(1)}, bf16[256,512]{1,0:T(8,128)(2,1)S(1)}, u32[]{:S(2)}, u32[]{:S(2)}) collective-permute-start(bf16[256,512]{1,0:T(8,128)(2,1)S(1)} %bitcast.102), channel_id=1, source_target_pairs={{0,24},{4,28},{8,16},{12,20},{16,8},{20,12},{24,0},{28,4},{1,25},{... | collective-permute-start | bytes 786440 | tf_op jit(solution)/shard_map/ppermute | solution.py:28
  14.9 1.4 collective-permute-done.1
  16.3 5.4 %collective-permute-done.2 = bf16[168,512]{1,0:T(8,128)(2,1)} collective-permute-done((bf16[168,512]{1,0:T(8,128)(2,1)S(1)}, bf16[168,512]{1,0:T(8,128)(2,1)}, u32[]{:S(2)}, u32[]{:S(2)}) %collective-permute-start.2) | collective-permute-done | bytes 172064 | tf_op jit(solution)/shard_map/ppermute | solution.py:32
  21.7 0.9 constant_dynamic-update-slice_fusion.10
  22.7 0.9 constant_dynamic-update-slice_fusion.8
  25.9 0.9 collective-permute-done.10
  26.9 1.9 %fusion.10 = f32[120,1408]{1,0:T(8,128)S(1)} fusion(bf16[120,2048]{1,0:T(8,128)(2,1)S(1)} %pad_maximum_fusion.7, bf16[1,1408,2048]{2,1,0:T(8,128)(2,1)S(1)} %bitcast.96), kind=kOutput, calls=%fused_computation.10 | convolution fusion | flops 692060160 | bytes 6934528 | tf_op jit(solution)/shard_map/dot_general | solution.py:17
  29.0 1.6 %collective-permute-start.8 = (bf16[128,2048]{1,0:T(8,128)(2,1)S(1)}, bf16[128,2048]{1,0:T(8,128)(2,1)S(1)}, u32[]{:S(2)}, u32[]{:S(2)}) collective-permute-start(bf16[128,2048]{1,0:T(8,128)(2,1)S(1)} %pad_maximum_fusion.5), channel_id=1, source_target_pairs={{0,16},{4,20},{8,24},{12,28},{16,0},{20,4},{24,8},{28,12},{1,17},{... | collective-permute-start | bytes 1572872 | tf_op jit(solution)/shard_map/ppermute | solution.py:28
  30.6 1.6 %collective-permute-start.7 = (bf16[128,2048]{1,0:T(8,128)(2,1)S(1)}, bf16[128,2048]{1,0:T(8,128)(2,1)S(1)}, u32[]{:S(2)}, u32[]{:S(2)}) collective-permute-start(bf16[128,2048]{1,0:T(8,128)(2,1)S(1)} %pad_maximum_fusion.4), channel_id=1, source_target_pairs={{0,8},{4,12},{8,0},{12,4},{16,24},{20,28},{24,16},{28,20},{1,9},{5... | collective-permute-start | bytes 1572872 | tf_op jit(solution)/shard_map/ppermute | solution.py:28
  32.2 2.0 %fusion.23 = bf16[120,1408]{1,0:T(8,128)(2,1)S(1)} fusion(bf16[120,2048]{1,0:T(8,128)(2,1)S(1)} %pad_maximum_fusion.7, bf16[1,1408,2048]{2,1,0:T(8,128)(2,1)S(1)} %bitcast.120, f32[120,1408]{1,0:T(8,128)S(1)} %fusion.10), kind=kOutput, calls=%fused_computation.19 | convolution fusion | flops 693073920 | bytes 7272448 | tf_op jit(solution)/shard_map/dot_general | solution.py:17
  34.1 2.5 %collective-permute-start.11 = (bf16[120,1408]{1,0:T(8,128)(2,1)S(1)}, bf16[120,1408]{1,0:T(8,128)(2,1)S(1)}, u32[]{:S(2)}, u32[]{:S(2)}) collective-permute-start(bf16[120,1408]{1,0:T(8,128)(2,1)S(1)} %fusion.23), channel_id=1, source_target_pairs={{0,3},{1,2},{2,1},{3,0},{4,7},{5,6},{6,5},{7,4},{8,11},{9,10},{10,... | collective-permute-start | bytes 1013768 | tf_op jit(solution)/shard_map/ppermute | solution.py:32
  36.7 3.8 %collective-permute-start.14 = (bf16[120,1408]{1,0:T(8,128)(2,1)S(1)}, bf16[120,1408]{1,0:T(8,128)(2,1)S(1)}, u32[]{:S(2)}, u32[]{:S(2)}) collective-permute-start(bf16[120,1408]{1,0:T(8,128)(2,1)S(1)} %fusion.23), channel_id=1, source_target_pairs={{0,2},{3,1},{4,6},{7,5},{8,10},{11,9},{12,14},{15,13},{16,18},{19,... | collective-permute-start | bytes 1013768 | tf_op jit(solution)/shard_map/ppermute | solution.py:32
  40.6 2.4 %collective-permute-done.8 = bf16[128,2048]{1,0:T(8,128)(2,1)S(1)} collective-permute-done((bf16[128,2048]{1,0:T(8,128)(2,1)S(1)}, bf16[128,2048]{1,0:T(8,128)(2,1)S(1)}, u32[]{:S(2)}, u32[]{:S(2)}) %collective-permute-start.8) | collective-permute-done | bytes 524320 | tf_op jit(solution)/shard_map/ppermute | solution.py:28
  43.0 1.4 collective-permute-done.7
  44.6 1.5 %collective-permute-start.9 = (bf16[128,2048]{1,0:T(8,128)(2,1)S(1)}, bf16[128,2048]{1,0:T(8,128)(2,1)S(1)}, u32[]{:S(2)}, u32[]{:S(2)}) collective-permute-start(bf16[128,2048]{1,0:T(8,128)(2,1)S(1)} %pad_maximum_fusion.6), channel_id=1, source_target_pairs={{0,24},{4,28},{8,16},{12,20},{16,8},{20,12},{24,0},{28,4},{1,25},{... | collective-permute-start | bytes 1572872 | tf_op jit(solution)/shard_map/ppermute | solution.py:28
  46.5 0.7 collective-permute-done.12
  48.2 1.3 collective-permute-start.15
  49.5 2.0 %fusion.8 = f32[240,1408]{1,0:T(8,128)S(1)} fusion(bf16[240,2048]{1,0:T(8,128)(2,1)S(1)} %pad_maximum_fusion.2, bf16[1,1408,2048]{2,1,0:T(8,128)(2,1)S(1)} %bitcast.96), kind=kOutput, calls=%fused_computation.8 | convolution fusion | flops 1384120320 | bytes 8101888 | tf_op jit(solution)/shard_map/dot_general | solution.py:17
  51.4 2.0 %fusion.17 = bf16[240,1408]{1,0:T(8,128)(2,1)S(1)} fusion(bf16[240,2048]{1,0:T(8,128)(2,1)S(1)} %pad_maximum_fusion.2, bf16[1,1408,2048]{2,1,0:T(8,128)(2,1)S(1)} %bitcast.120, f32[240,1408]{1,0:T(8,128)S(1)} %fusion.8), kind=kOutput, calls=%fused_computation.17 | convolution fusion | flops 1386147840 | bytes 8777728 | tf_op jit(solution)/shard_map/dot_general | solution.py:17
  54.2 5.7 %collective-permute-done.9 = bf16[128,2048]{1,0:T(8,128)(2,1)S(1)} collective-permute-done((bf16[128,2048]{1,0:T(8,128)(2,1)S(1)}, bf16[128,2048]{1,0:T(8,128)(2,1)S(1)}, u32[]{:S(2)}, u32[]{:S(2)}) %collective-permute-start.9) | collective-permute-done | bytes 524320 | tf_op jit(solution)/shard_map/ppermute | solution.py:28
  60.3 4.9 %collective-permute-start.18 = (bf16[248,1408]{1,0:T(8,128)(2,1)S(1)}, bf16[248,1408]{1,0:T(8,128)(2,1)S(1)}, u32[]{:S(2)}, u32[]{:S(2)}) collective-permute-start(bf16[248,1408]{1,0:T(8,128)(2,1)S(1)} %pad_maximum_fusion.3), channel_id=1, source_target_pairs={{0,2},{3,1},{4,6},{7,5},{8,10},{11,9},{12,14},{15,13},{16,18},{19,... | collective-permute-start | bytes 2095112 | tf_op jit(solution)/shard_map/ppermute | solution.py:32
  65.3 1.9 %fusion.6 = f32[120,1408]{1,0:T(8,128)S(1)} fusion(bf16[120,2048]{1,0:T(8,128)(2,1)S(1)} %pad_maximum_fusion.8, bf16[1,1408,2048]{2,1,0:T(8,128)(2,1)S(1)} %bitcast.96), kind=kOutput, calls=%fused_computation.6 | convolution fusion | flops 692060160 | bytes 6934528 | tf_op jit(solution)/shard_map/dot_general | solution.py:17
  67.2 2.7 %multiply_convert_fusion = bf16[120,1408]{1,0:T(8,128)(2,1)} fusion(f32[120,1408]{1,0:T(8,128)S(1)} %fusion.6, bf16[120,2048]{1,0:T(8,128)(2,1)S(1)} %pad_maximum_fusion.8, bf16[1,1408,2048]{2,1,0:T(8,128)(2,1)S(1)} %bitcast.120), kind=kOutput, calls=%fused_computation.40 | convolution fusion | flops 693073920 | bytes 7272448 | tf_op jit(solution)/shard_map/dot_general | solution.py:17
  70.0 1.3 collective-permute-start.17
  71.5 0.9 convolution_convert_fusion.2
  74.3 6.5 %collective-permute-start.16 = (bf16[120,1408]{1,0:T(8,128)(2,1)}, bf16[120,1408]{1,0:T(8,128)(2,1)}, u32[]{:S(2)}, u32[]{:S(2)}) collective-permute-start(bf16[120,1408]{1,0:T(8,128)(2,1)} %multiply_convert_fusion), channel_id=1, source_target_pairs={{0,2},{3,1},{4,6},{7,5},{8,10},{11,9},{12,14},{15,13},{16,18},{19,... | collective-permute-start | bytes 1013768 | tf_op jit(solution)/shard_map/ppermute | solution.py:32
  80.8 1.3 collective-permute-start.23
  82.1 9.2 %collective-permute-done.18 = bf16[248,1408]{1,0:T(8,128)(2,1)S(1)} collective-permute-done((bf16[248,1408]{1,0:T(8,128)(2,1)S(1)}, bf16[248,1408]{1,0:T(8,128)(2,1)S(1)}, u32[]{:S(2)}, u32[]{:S(2)}) %collective-permute-start.18) | collective-permute-done | bytes 698400 | tf_op jit(solution)/shard_map/ppermute | solution.py:32
  91.3 1.3 collective-permute-start.22
  92.6 16.1 %collective-permute-done.17 = bf16[120,1408]{1,0:T(8,128)(2,1)} collective-permute-done((bf16[120,1408]{1,0:T(8,128)(2,1)}, bf16[120,1408]{1,0:T(8,128)(2,1)}, u32[]{:S(2)}, u32[]{:S(2)}) %collective-permute-start.17) | collective-permute-done | bytes 337952 | tf_op jit(solution)/shard_map/ppermute | solution.py:32
  108.7 1.3 collective-permute-start.21
  110.1 1.0 constant_dynamic-update-slice_fusion.2
  111.2 1.0 constant_dynamic-update-slice_fusion
  112.4 0.9 fusion.77
  113.4 10.1 %collective-permute-done.22 = bf16[248,1408]{1,0:T(8,128)(2,1)S(1)} collective-permute-done((bf16[248,1408]{1,0:T(8,128)(2,1)S(1)}, bf16[248,1408]{1,0:T(8,128)(2,1)S(1)}, u32[]{:S(2)}, u32[]{:S(2)}) %collective-permute-start.22) | collective-permute-done | bytes 698400 | tf_op jit(solution)/shard_map/ppermute | solution.py:32
  123.9 2.3 %fusion.30 = bf16[240,512]{1,0:T(8,128)(2,1)} fusion(bf16[248,5632]{1,0:T(8,128)(2,1)S(1)} %add_dynamic-update-slice_fusion, bf16[1,5632,512]{2,1,0:T(8,128)(2,1)S(1)} %bitcast.93), kind=kOutput, calls=%fused_computation.28 | convolution fusion | flops 1384243200 | bytes 8716288 | tf_op jit(solution)/shard_map/dot_general | solution.py:262
  126.7 2.2 %collective-permute-done.21 = bf16[120,1408]{1,0:T(8,128)(2,1)} collective-permute-done((bf16[120,1408]{1,0:T(8,128)(2,1)}, bf16[120,1408]{1,0:T(8,128)(2,1)}, u32[]{:S(2)}, u32[]{:S(2)}) %collective-permute-start.21) | collective-permute-done | bytes 337952 | tf_op jit(solution)/shard_map/ppermute | solution.py:32
  129.0 1.5 %fusion.36 = f32[120,512]{1,0:T(8,128)S(1)} fusion(bf16[1408,512]{1,0:T(8,128)(2,1)S(1)} %constant_dynamic-slice_fusion, bf16[120,1408]{1,0:T(8,128)(2,1)} %collective-permute-done.16, bf16[120,1408]{1,0:T(8,128)(2,1)} %collective-permute-done.21), kind=kOutput, calls=%fused_computation.49 | convolution fusion | flops 173184000 | bytes 2363392 | tf_op jit(solution)/shard_map/dot_general | solution.py:327
  130.5 1.5 %collective-permute-start.27 = (bf16[120,512]{1,0:T(8,128)(2,1)S(1)}, bf16[120,512]{1,0:T(8,128)(2,1)S(1)}, u32[]{:S(2)}, u32[]{:S(2)}) collective-permute-start(bf16[120,512]{1,0:T(8,128)(2,1)S(1)} %add_convert_fusion.1), channel_id=1, source_target_pairs={{0,24},{4,28},{8,16},{12,20},{16,8},{20,12},{24,0},{28,4},{1,25},{... | collective-permute-start | bytes 368648 | tf_op jit(solution)/shard_map/ppermute | solution.py:28
  132.6 1.5 %collective-permute-start.26 = (bf16[120,512]{1,0:T(8,128)(2,1)S(1)}, bf16[120,512]{1,0:T(8,128)(2,1)S(1)}, u32[]{:S(2)}, u32[]{:S(2)}) collective-permute-start(bf16[120,512]{1,0:T(8,128)(2,1)S(1)} %get-tuple-element.140), channel_id=1, source_target_pairs={{0,16},{4,20},{8,24},{12,28},{16,0},{20,4},{24,8},{28,12},{1,17},{... | collective-permute-start | bytes 368648 | tf_op jit(solution)/shard_map/ppermute | solution.py:28
  134.2 2.5 %collective-permute-done.27 = bf16[120,512]{1,0:T(8,128)(2,1)S(1)} collective-permute-done((bf16[120,512]{1,0:T(8,128)(2,1)S(1)}, bf16[120,512]{1,0:T(8,128)(2,1)S(1)}, u32[]{:S(2)}, u32[]{:S(2)}) %collective-permute-start.27) | collective-permute-done | bytes 122912 | tf_op jit(solution)/shard_map/ppermute | solution.py:28
  137.0 0.9 collective-permute-done.26
  138.4 1.3 collective-permute-done.28
  (145 shorter events, 14.0 us)
Async XLA Ops:
  0.0 11.9 %copy-start.3 = (s32[160,2]{0,1:T(2,128)S(1)}, s32[160,2]{0,1:T(2,128)}, u32[]{:S(2)}) copy-start(s32[160,2]{0,1:T(2,128)} %param.15) | copy-start | bytes 3844
  0.0 12.6 %copy-start.5 = (s32[16]{0:T(128)S(1)}, s32[16]{0:T(128)}, u32[]{:S(2)}) copy-start(s32[16]{0:T(128)} %param.13) | copy-start | bytes 196
  0.0 13.0 %copy-start.6 = (s32[16]{0:T(128)S(1)}, s32[16]{0:T(128)}, u32[]{:S(2)}) copy-start(s32[16]{0:T(128)} %param.14) | copy-start | bytes 196
  0.8 26.1 %slice-start.2 = ((s8[5767168]{0:T(1024)(128)(4,1)}), s8[1572864]{0:T(1024)(128)(4,1)S(1)}, s32[]{:S(2)}) async-start(s8[5767168]{0:T(1024)(128)(4,1)} %bitcast.95), calls=%async_computation.2 | async-start | bytes 3145728
  1.9 11.4 %collective-permute-start = (bf16[168,512]{1,0:T(8,128)(2,1)S(1)}, bf16[168,512]{1,0:T(8,128)(2,1)S(1)}, u32[]{:S(2)}, u32[]{:S(2)}) collective-permute-start(bf16[168,512]{1,0:T(8,128)(2,1)S(1)} %get-tuple-element.142), channel_id=1, source_target_pairs={{0,3},{1,2},{2,1},{3,0},{4,7},{5,6},{6,5},{7,4},{8,11},{9,10},{10,... | collective-permute-start | bytes 516104 | tf_op jit(solution)/shard_map/ppermute | solution.py:32
  7.0 9.3 %collective-permute-start.1 = (bf16[168,512]{1,0:T(8,128)(2,1)S(1)}, bf16[168,512]{1,0:T(8,128)(2,1)}, u32[]{:S(2)}, u32[]{:S(2)}) collective-permute-start(bf16[168,512]{1,0:T(8,128)(2,1)S(1)} %get-tuple-element.142), channel_id=1, source_target_pairs={{0,1},{1,0},{2,3},{3,2},{4,5},{5,4},{6,7},{7,6},{8,9},{9,8},{10,11... | collective-permute-start | bytes 516104 | tf_op jit(solution)/shard_map/ppermute | solution.py:32
  7.0 14.7 %collective-permute-start.2 = (bf16[168,512]{1,0:T(8,128)(2,1)S(1)}, bf16[168,512]{1,0:T(8,128)(2,1)}, u32[]{:S(2)}, u32[]{:S(2)}) collective-permute-start(bf16[168,512]{1,0:T(8,128)(2,1)S(1)} %get-tuple-element.142), channel_id=1, source_target_pairs={{0,2},{1,3},{2,0},{3,1},{4,6},{5,7},{6,4},{7,5},{8,10},{9,11},{10,... | collective-permute-start | bytes 516104 | tf_op jit(solution)/shard_map/ppermute | solution.py:32
  8.7 15.5 %collective-permute-start.3 = (bf16[256,512]{1,0:T(8,128)(2,1)S(1)}, bf16[256,512]{1,0:T(8,128)(2,1)S(1)}, u32[]{:S(2)}, u32[]{:S(2)}) collective-permute-start(bf16[256,512]{1,0:T(8,128)(2,1)S(1)} %bitcast.100), channel_id=1, source_target_pairs={{0,8},{4,12},{8,0},{12,4},{16,24},{20,28},{24,16},{28,20},{1,9},{5... | collective-permute-start | bytes 786440 | tf_op jit(solution)/shard_map/ppermute | solution.py:28
  10.4 13.8 %collective-permute-start.4 = (bf16[256,512]{1,0:T(8,128)(2,1)S(1)}, bf16[256,512]{1,0:T(8,128)(2,1)S(1)}, u32[]{:S(2)}, u32[]{:S(2)}) collective-permute-start(bf16[256,512]{1,0:T(8,128)(2,1)S(1)} %bitcast.101), channel_id=1, source_target_pairs={{0,16},{4,20},{8,24},{12,28},{16,0},{20,4},{24,8},{28,12},{1,17},{... | collective-permute-start | bytes 786440 | tf_op jit(solution)/shard_map/ppermute | solution.py:28
  13.4 10.8 %collective-permute-start.5 = (bf16[256,512]{1,0:T(8,128)(2,1)S(1)}, bf16[256,512]{1,0:T(8,128)(2,1)S(1)}, u32[]{:S(2)}, u32[]{:S(2)}) collective-permute-start(bf16[256,512]{1,0:T(8,128)(2,1)S(1)} %bitcast.102), channel_id=1, source_target_pairs={{0,24},{4,28},{8,16},{12,20},{16,8},{20,12},{24,0},{28,4},{1,25},{... | collective-permute-start | bytes 786440 | tf_op jit(solution)/shard_map/ppermute | solution.py:28
  24.1 2.8 %slice-start.3 = ((s8[5767168]{0:T(1024)(128)(4,1)}), s8[4194304]{0:T(1024)(128)(4,1)S(1)}, s32[]{:S(2)}) async-start(s8[5767168]{0:T(1024)(128)(4,1)} %bitcast.95), calls=%async_computation.3 | async-start | bytes 8388608
  25.2 1.6 %collective-permute-start.10 = (bf16[64,2048]{1,0:T(8,128)(2,1)S(1)}, bf16[64,2048]{1,0:T(8,128)(2,1)S(1)}, u32[]{:S(2)}, u32[]{:S(2)}) collective-permute-start(bf16[64,2048]{1,0:T(8,128)(2,1)S(1)} %slice.144), channel_id=1, source_target_pairs={{0,4},{4,0},{8,12},{12,8},{16,20},{20,16},{24,28},{28,24},{1,5},{5... | collective-permute-start | bytes 786440 | tf_op jit(solution)/shard_map/ppermute | solution.py:28
  25.3 3.6 %collective-permute-start.6 = (bf16[3,64,2048]{2,1,0:T(8,128)(2,1)S(1)}, bf16[3,64,2048]{2,1,0:T(8,128)(2,1)S(1)}, u32[]{:S(2)}, u32[]{:S(2)}) collective-permute-start(bf16[3,64,2048]{2,1,0:T(8,128)(2,1)S(1)} %bitcast.106), channel_id=1, source_target_pairs={{0,4},{4,0},{8,12},{12,8},{16,20},{20,16},{24,28},{28,24},{1,5},{5... | collective-permute-start | bytes 2359304 | tf_op jit(solution)/shard_map/ppermute | solution.py:28
  26.8 5.4 %slice-start.4 = ((s8[5767168]{0:T(1024)(128)(4,1)}), s8[4194304]{0:T(1024)(128)(4,1)S(1)}, s32[]{:S(2)}) async-start(s8[5767168]{0:T(1024)(128)(4,1)} %bitcast.119), calls=%async_computation.4 | async-start | bytes 8388608
  26.9 5.3 %slice-start.5 = ((s8[5767168]{0:T(1024)(128)(4,1)}), s8[1572864]{0:T(1024)(128)(4,1)S(1)}, s32[]{:S(2)}) async-start(s8[5767168]{0:T(1024)(128)(4,1)} %bitcast.119), calls=%async_computation.5 | async-start | bytes 3145728
  29.0 14.0 %collective-permute-start.8 = (bf16[128,2048]{1,0:T(8,128)(2,1)S(1)}, bf16[128,2048]{1,0:T(8,128)(2,1)S(1)}, u32[]{:S(2)}, u32[]{:S(2)}) collective-permute-start(bf16[128,2048]{1,0:T(8,128)(2,1)S(1)} %pad_maximum_fusion.5), channel_id=1, source_target_pairs={{0,16},{4,20},{8,24},{12,28},{16,0},{20,4},{24,8},{28,12},{1,17},{... | collective-permute-start | bytes 1572872 | tf_op jit(solution)/shard_map/ppermute | solution.py:28
  30.6 13.7 %collective-permute-start.7 = (bf16[128,2048]{1,0:T(8,128)(2,1)S(1)}, bf16[128,2048]{1,0:T(8,128)(2,1)S(1)}, u32[]{:S(2)}, u32[]{:S(2)}) collective-permute-start(bf16[128,2048]{1,0:T(8,128)(2,1)S(1)} %pad_maximum_fusion.4), channel_id=1, source_target_pairs={{0,8},{4,12},{8,0},{12,4},{16,24},{20,28},{24,16},{28,20},{1,9},{5... | collective-permute-start | bytes 1572872 | tf_op jit(solution)/shard_map/ppermute | solution.py:28
  34.1 14.0 %collective-permute-start.11 = (bf16[120,1408]{1,0:T(8,128)(2,1)S(1)}, bf16[120,1408]{1,0:T(8,128)(2,1)S(1)}, u32[]{:S(2)}, u32[]{:S(2)}) collective-permute-start(bf16[120,1408]{1,0:T(8,128)(2,1)S(1)} %fusion.23), channel_id=1, source_target_pairs={{0,3},{1,2},{2,1},{3,0},{4,7},{5,6},{6,5},{7,4},{8,11},{9,10},{10,... | collective-permute-start | bytes 1013768 | tf_op jit(solution)/shard_map/ppermute | solution.py:32
  36.7 23.7 %collective-permute-start.13 = (bf16[120,1408]{1,0:T(8,128)(2,1)S(1)}, bf16[120,1408]{1,0:T(8,128)(2,1)S(1)}, u32[]{:S(2)}, u32[]{:S(2)}) collective-permute-start(bf16[120,1408]{1,0:T(8,128)(2,1)S(1)} %fusion.23), channel_id=1, source_target_pairs={{0,1},{1,0},{2,3},{3,2},{4,5},{5,4},{6,7},{7,6},{8,9},{9,8},{10,11... | collective-permute-start | bytes 1013768 | tf_op jit(solution)/shard_map/ppermute | solution.py:32
  36.7 28.6 %collective-permute-start.14 = (bf16[120,1408]{1,0:T(8,128)(2,1)S(1)}, bf16[120,1408]{1,0:T(8,128)(2,1)S(1)}, u32[]{:S(2)}, u32[]{:S(2)}) collective-permute-start(bf16[120,1408]{1,0:T(8,128)(2,1)S(1)} %fusion.23), channel_id=1, source_target_pairs={{0,2},{3,1},{4,6},{7,5},{8,10},{11,9},{12,14},{15,13},{16,18},{19,... | collective-permute-start | bytes 1013768 | tf_op jit(solution)/shard_map/ppermute | solution.py:32
  44.5 2.7 %collective-permute-start.12 = (bf16[4,256,512]{2,1,0:T(8,128)(2,1)S(1)}, bf16[4,256,512]{2,1,0:T(8,128)(2,1)S(1)}, u32[]{:S(2)}, u32[]{:S(2)}) collective-permute-start(bf16[4,256,512]{2,1,0:T(8,128)(2,1)S(1)} %get-tuple-element.124), channel_id=1, source_target_pairs={{0,4},{4,0},{8,12},{12,8},{16,20},{20,16},{24,28},{28,24},{1,5},{5... | collective-permute-start | bytes 3145736 | tf_op jit(solution)/shard_map/ppermute | solution.py:28
  44.6 15.3 %collective-permute-start.9 = (bf16[128,2048]{1,0:T(8,128)(2,1)S(1)}, bf16[128,2048]{1,0:T(8,128)(2,1)S(1)}, u32[]{:S(2)}, u32[]{:S(2)}) collective-permute-start(bf16[128,2048]{1,0:T(8,128)(2,1)S(1)} %pad_maximum_fusion.6), channel_id=1, source_target_pairs={{0,24},{4,28},{8,16},{12,20},{16,8},{20,12},{24,0},{28,4},{1,25},{... | collective-permute-start | bytes 1572872 | tf_op jit(solution)/shard_map/ppermute | solution.py:28
  48.2 17.1 %collective-permute-start.15 = (bf16[120,1408]{1,0:T(8,128)(2,1)S(1)}, bf16[120,1408]{1,0:T(8,128)(2,1)S(1)}, u32[]{:S(2)}, u32[]{:S(2)}) collective-permute-start(bf16[120,1408]{1,0:T(8,128)(2,1)S(1)} %collective-permute-done.11), channel_id=1, source_target_pairs={{1,0},{2,3},{5,4},{6,7},{9,8},{10,11},{13,12},{14,15},{17,16},{18,... | collective-permute-start | bytes 1013768 | tf_op jit(solution)/shard_map/ppermute | solution.py:32
  53.5 20.7 %collective-permute-start.20 = (bf16[248,1408]{1,0:T(8,128)(2,1)S(1)}, bf16[248,1408]{1,0:T(8,128)(2,1)S(1)}, u32[]{:S(2)}, u32[]{:S(2)}) collective-permute-start(bf16[248,1408]{1,0:T(8,128)(2,1)S(1)} %pad_maximum_fusion.3), channel_id=1, source_target_pairs={{1,2},{2,1},{5,6},{6,5},{9,10},{10,9},{13,14},{14,13},{17,18},{18,... | collective-permute-start | bytes 2095112 | tf_op jit(solution)/shard_map/ppermute | solution.py:32
  59.9 20.9 %collective-permute-start.19 = (bf16[248,1408]{1,0:T(8,128)(2,1)S(1)}, bf16[248,1408]{1,0:T(8,128)(2,1)S(1)}, u32[]{:S(2)}, u32[]{:S(2)}) collective-permute-start(bf16[248,1408]{1,0:T(8,128)(2,1)S(1)} %pad_maximum_fusion.3), channel_id=1, source_target_pairs={{0,1},{1,0},{2,3},{3,2},{4,5},{5,4},{6,7},{7,6},{8,9},{9,8},{10,11... | collective-permute-start | bytes 2095112 | tf_op jit(solution)/shard_map/ppermute | solution.py:32
  60.3 31.0 %collective-permute-start.18 = (bf16[248,1408]{1,0:T(8,128)(2,1)S(1)}, bf16[248,1408]{1,0:T(8,128)(2,1)S(1)}, u32[]{:S(2)}, u32[]{:S(2)}) collective-permute-start(bf16[248,1408]{1,0:T(8,128)(2,1)S(1)} %pad_maximum_fusion.3), channel_id=1, source_target_pairs={{0,2},{3,1},{4,6},{7,5},{8,10},{11,9},{12,14},{15,13},{16,18},{19,... | collective-permute-start | bytes 2095112 | tf_op jit(solution)/shard_map/ppermute | solution.py:32
  65.3 6.2 %slice-start = ((s8[5767168]{0:T(1024)(128)(4,1)}), s8[4194304]{0:T(1024)(128)(4,1)S(1)}, s32[]{:S(2)}) async-start(s8[5767168]{0:T(1024)(128)(4,1)} %bitcast.92), calls=%async_computation | async-start | bytes 8388608
  67.2 4.3 %slice-start.1 = ((s8[5767168]{0:T(1024)(128)(4,1)}), s8[1572864]{0:T(1024)(128)(4,1)S(1)}, s32[]{:S(2)}) async-start(s8[5767168]{0:T(1024)(128)(4,1)} %bitcast.92), calls=%async_computation.1 | async-start | bytes 3145728
  69.9 41.2 %collective-permute-start.24 = (bf16[120,1408]{1,0:T(8,128)(2,1)}, bf16[120,1408]{1,0:T(8,128)(2,1)S(1)}, u32[]{:S(2)}, u32[]{:S(2)}) collective-permute-start(bf16[120,1408]{1,0:T(8,128)(2,1)} %multiply_convert_fusion), channel_id=1, source_target_pairs={{0,1},{1,0},{2,3},{3,2},{4,5},{5,4},{6,7},{7,6},{8,9},{9,8},{10,11... | collective-permute-start | bytes 1013768 | tf_op jit(solution)/shard_map/ppermute | solution.py:32
  70.0 38.8 %collective-permute-start.17 = (bf16[120,1408]{1,0:T(8,128)(2,1)}, bf16[120,1408]{1,0:T(8,128)(2,1)}, u32[]{:S(2)}, u32[]{:S(2)}) collective-permute-start(bf16[120,1408]{1,0:T(8,128)(2,1)} %multiply_convert_fusion), channel_id=1, source_target_pairs={{0,3},{1,2},{2,1},{3,0},{4,7},{5,6},{6,5},{7,4},{8,11},{9,10},{10,... | collective-permute-start | bytes 1013768 | tf_op jit(solution)/shard_map/ppermute | solution.py:32
  71.5 1.0 copy-start.4
  74.3 52.5 %collective-permute-start.16 = (bf16[120,1408]{1,0:T(8,128)(2,1)}, bf16[120,1408]{1,0:T(8,128)(2,1)}, u32[]{:S(2)}, u32[]{:S(2)}) collective-permute-start(bf16[120,1408]{1,0:T(8,128)(2,1)} %multiply_convert_fusion), channel_id=1, source_target_pairs={{0,2},{3,1},{4,6},{7,5},{8,10},{11,9},{12,14},{15,13},{16,18},{19,... | collective-permute-start | bytes 1013768 | tf_op jit(solution)/shard_map/ppermute | solution.py:32
  80.8 42.9 %collective-permute-start.23 = (bf16[248,1408]{1,0:T(8,128)(2,1)S(1)}, bf16[248,1408]{1,0:T(8,128)(2,1)S(1)}, u32[]{:S(2)}, u32[]{:S(2)}) collective-permute-start(bf16[248,1408]{1,0:T(8,128)(2,1)S(1)} %collective-permute-done.20), channel_id=1, source_target_pairs={{1,0},{2,3},{5,4},{6,7},{9,8},{10,11},{13,12},{14,15},{17,16},{18,... | collective-permute-start | bytes 2095112 | tf_op jit(solution)/shard_map/ppermute | solution.py:32
  91.3 32.2 %collective-permute-start.22 = (bf16[248,1408]{1,0:T(8,128)(2,1)S(1)}, bf16[248,1408]{1,0:T(8,128)(2,1)S(1)}, u32[]{:S(2)}, u32[]{:S(2)}) collective-permute-start(bf16[248,1408]{1,0:T(8,128)(2,1)S(1)} %collective-permute-done.18), channel_id=1, source_target_pairs={{1,0},{2,3},{5,4},{6,7},{9,8},{10,11},{13,12},{14,15},{17,16},{18,... | collective-permute-start | bytes 2095112 | tf_op jit(solution)/shard_map/ppermute | solution.py:32
  108.7 20.2 %collective-permute-start.21 = (bf16[120,1408]{1,0:T(8,128)(2,1)}, bf16[120,1408]{1,0:T(8,128)(2,1)}, u32[]{:S(2)}, u32[]{:S(2)}) collective-permute-start(bf16[120,1408]{1,0:T(8,128)(2,1)} %collective-permute-done.17), channel_id=1, source_target_pairs={{1,0},{2,3},{5,4},{6,7},{9,8},{10,11},{13,12},{14,15},{17,16},{18,... | collective-permute-start | bytes 1013768 | tf_op jit(solution)/shard_map/ppermute | solution.py:32
  129.0 3.0 %copy-start.2 = (bf16[240,512]{1,0:T(8,128)(2,1)S(1)}, bf16[240,512]{1,0:T(8,128)(2,1)}, u32[]{:S(2)}) copy-start(bf16[240,512]{1,0:T(8,128)(2,1)} %fusion.30) | copy-start | bytes 737284
  130.5 7.7 %copy-start.1 = (bf16[240,160]{0,1:T(8,128)(2,1)S(1)}, bf16[240,160]{0,1:T(8,128)(2,1)}, u32[]{:S(2)}) copy-start(bf16[240,160]{0,1:T(8,128)(2,1)} %get-tuple-element.114) | copy-start | bytes 230404
  130.5 6.1 %collective-permute-start.27 = (bf16[120,512]{1,0:T(8,128)(2,1)S(1)}, bf16[120,512]{1,0:T(8,128)(2,1)S(1)}, u32[]{:S(2)}, u32[]{:S(2)}) collective-permute-start(bf16[120,512]{1,0:T(8,128)(2,1)S(1)} %add_convert_fusion.1), channel_id=1, source_target_pairs={{0,24},{4,28},{8,16},{12,20},{16,8},{20,12},{24,0},{28,4},{1,25},{... | collective-permute-start | bytes 368648 | tf_op jit(solution)/shard_map/ppermute | solution.py:28
  132.0 4.9 %collective-permute-start.25 = (bf16[120,512]{1,0:T(8,128)(2,1)S(1)}, bf16[120,512]{1,0:T(8,128)(2,1)S(1)}, u32[]{:S(2)}, u32[]{:S(2)}) collective-permute-start(bf16[120,512]{1,0:T(8,128)(2,1)S(1)} %get-tuple-element.139), channel_id=1, source_target_pairs={{0,8},{4,12},{8,0},{12,4},{16,24},{20,28},{24,16},{28,20},{1,9},{5... | collective-permute-start | bytes 368648 | tf_op jit(solution)/shard_map/ppermute | solution.py:28
  132.6 5.3 %collective-permute-start.26 = (bf16[120,512]{1,0:T(8,128)(2,1)S(1)}, bf16[120,512]{1,0:T(8,128)(2,1)S(1)}, u32[]{:S(2)}, u32[]{:S(2)}) collective-permute-start(bf16[120,512]{1,0:T(8,128)(2,1)S(1)} %get-tuple-element.140), channel_id=1, source_target_pairs={{0,16},{4,20},{8,24},{12,28},{16,0},{20,4},{24,8},{28,12},{1,17},{... | collective-permute-start | bytes 368648 | tf_op jit(solution)/shard_map/ppermute | solution.py:28
  138.0 1.7 %copy-start = (bf16[240,160]{0,1:T(8,128)(2,1)S(1)}, bf16[240,160]{0,1:T(8,128)(2,1)}, u32[]{:S(2)}) copy-start(bf16[240,160]{0,1:T(8,128)(2,1)} %get-tuple-element.115) | copy-start | bytes 230404
  138.0 1.6 %collective-permute-start.28 = (bf16[4,60,512]{2,1,0:T(8,128)(2,1)S(1)}, bf16[4,60,512]{2,1,0:T(8,128)(2,1)S(1)}, u32[]{:S(2)}, u32[]{:S(2)}) collective-permute-start(bf16[4,60,512]{2,1,0:T(8,128)(2,1)S(1)} %get-tuple-element.138), channel_id=1, source_target_pairs={{0,4},{4,0},{8,12},{12,8},{16,20},{20,16},{24,28},{28,24},{1,5},{5... | collective-permute-start | bytes 737288 | tf_op jit(solution)/shard_map/ppermute | solution.py:28

commit v5 on v4

--- a/solution.py
+++ b/solution.py
@@ -1,6 +1,8 @@
 import jax
 import jax.numpy as jnp
 from jax import lax
+from jax.experimental import pallas as pl
+from jax.experimental.pallas import tpu as pltpu
 from jax.sharding import PartitionSpec as P
 
 D = 2048
@@ -99,6 +101,33 @@
     gain = jnp.sum(features[rows : rows + 3].astype(jnp.float32), axis=0)
     scale = lax.rsqrt(jnp.mean(widened * widened, axis=1, keepdims=True) + 1e-06)
     return (widened * scale * gain[None, :]).astype(jnp.bfloat16)
+
+
+def line_normalised(value, mirror, beside, facing, rows):
+    width = value.shape[1]
+
+    def kernel(at_ref, *refs):
+        *block_refs, out_ref = refs
+        at = at_ref[0]
+        blocks = [ref[...].astype(jnp.float32) for ref in block_refs]
+        squares = sum(jnp.sum(block[:rows] * block[:rows], axis=1, keepdims=True) for block in blocks)
+        scale = lax.rsqrt(squares / (4 * width) + 1e-06)
+        for block, away in zip(blocks, (0, 3, 1, 2)):
+            gain = jnp.sum(block[rows:], axis=0, keepdims=True)
+            where = pl.ds(pl.multiple_of((at ^ away) * width, width), width)
+            out_ref[:, where] = (block[:rows] * scale * gain).astype(out_ref.dtype)
+
+    return pl.pallas_call(
+        kernel,
+        out_shape=jax.ShapeDtypeStruct((rows, 4 * width), jnp.bfloat16),
+        in_specs=[pl.BlockSpec(memory_space=pltpu.SMEM)]
+        + [pl.BlockSpec(memory_space=pltpu.VMEM)] * 4,
+        out_specs=pl.BlockSpec(memory_space=pltpu.VMEM),
+        compiler_params=pltpu.CompilerParams(vmem_limit_bytes=16 * 1024 * 1024),
+        cost_estimate=pl.CostEstimate(
+            flops=16 * rows * width, bytes_accessed=16 * rows * width, transcendentals=rows
+        ),
+    )(lax.axis_index("col")[None], value, mirror, beside, facing)
 
 
 def tie(*values):
@@ -140,12 +169,15 @@
     sent = jnp.concatenate(
         [tokens, jnp.pad(gain_parts, ((0, GAIN_ROWS - 3), (0, 0)))], axis=0
     )
-    hops = first_hops(sent, MIRROR, FACING) if line else ring_gather(sent)
+    hops = list(first_hops(sent, MIRROR, FACING)) if line else ring_gather(sent)
 
     local_adapters = adapter_down.shape[0]
     mine = jnp.concatenate([jnp.transpose(adapter_down, (0, 2, 1)), adapter_up], axis=0)
     mine = mine.reshape(2 * local_adapters * RANK, width_part)
-    by_chip = [mine] + [row_xor(mine, by) for by in range(2, rows_axis, 2)]
+    by_chip = [mine] + [row_xor(mine, by) for by in range(2, rows_axis - 2, 2)]
+    if line:
+        hops[0], mine = tie(hops[0], mine)
+    by_chip.append(row_xor(mine, rows_axis - 2))
     assigned = routes.reshape(-1)
     assign_count = assigned.shape[0]
     expert_hot = (assigned[:, None] == jnp.arange(EXPERTS, dtype=jnp.int32)[None, :]).astype(
@@ -170,8 +202,11 @@
     ]
     if line:
         hops, of_token = tie(hops, of_token)
-    features = in_line(sent, *hops) if line else side_by_side(sent, hops)
-    normed, *by_chip = tie(normalised(features, tok_rows), *by_chip)
+    if line:
+        normed = line_normalised(sent, *hops, tok_rows)
+    else:
+        normed = normalised(side_by_side(sent, hops), tok_rows)
+    normed, *by_chip[:-1] = tie(normed, *by_chip[:-1])
 
     def outgoing(core):
         placed = jnp.dot(of_token[core], normed, preferred_element_type=jnp.float32)
@@ -187,6 +222,8 @@
         jnp.concatenate([here_half[offset], partner_half[offset]], axis=0)
         for offset in range(chips)
     ]
+    if line:
+        pairs[1], by_chip[-1] = tie(pairs[1], by_chip[-1])
     for offset in range(1, chips):
         if offset == chips - 1:
             pairs[1:] = tie(*pairs[1:])
@@ -241,7 +278,7 @@
     if line:
         hops[0][0], extra = tie(hops[0][0], extra)
     passed = along(hops[0][0], OUTWARD) if line else None
-    value, (extra, *hops[0][:1]) = hidden_of(groups[1], [extra] + hops[0][:1])
+    value, (extra, *hops[0][:2]) = hidden_of(groups[1], [extra] + hops[0][:2])
     hidden.append(jnp.concatenate([value, extra], axis=0))
     hops.append(first_of(hidden[1], ACROSS, OVER))
     earlier = hops[0][1:] + [passed] if line else []

time: 141 us -> 140 us (level)
  waiting for transfers between devices: 60.6 us -> 42.6 us
  starting transfers between devices: 44.8 us -> 62.4 us
    ppermute x16, starting transfers between devices: 31 us -> 49.2 us  [along(): return lax.ppermute(value, 'col', pairs)]
    ppermute x16, waiting for transfers between devices: 44.5 us -> 31.5 us  [along(): return lax.ppermute(value, 'col', pairs)]
    ppermute x13, waiting for transfers between devices: 16.2 us -> 11.1 us  [row_xor(): lax.ppermute(value, 'row', [(i, i ^ by) for i in range(lax.axis_size('row...]
    dynamic_update_slice x12 -> x9, local copies, waits for them, and re-layouts: 4.29 us -> 1.42 us  [side_by_side(): whole = lax.dynamic_update_slice(whole, block, (first, sender * width))]
  transfers between devices with their start and end apart: 29 -> 29, of which waited for: 15 -> 14; matrix products, arithmetic and copies ran while one was open for 20% -> 20% of each run, Pallas kernels for 0% -> 0%
where the time goes in v5:
time: 140 us
  starting transfers between devices  62.4 us (45%)
  waiting for transfers between devices  42.6 us (30%)
  matrix products  19.9 us (14%)
  other arithmetic  8.45 us (6%)
  local copies, waits for them, and re-layouts  4.92 us (4%)
    ppermute x16, starting transfers between devices, along(): return lax.ppermute(value, 'col', pairs)  49.2 us
    ppermute x16, waiting for transfers between devices, along(): return lax.ppermute(value, 'col', pairs)  31.5 us
    ppermute x13, starting transfers between devices, row_xor(): lax.ppermute(value, 'row', [(i, i ^ by) for i in range(lax.axis_size('row...  13.2 us
    dot_general x7, matrix products, contract_last(): lax.dot_general(left, right, (((1,), (1,)), ((), ())), preferred_element_...  12.1 us
    ppermute x13, waiting for transfers between devices, row_xor(): lax.ppermute(value, 'row', [(i, i ^ by) for i in range(lax.axis_size('row...  11.1 us
    dot_general x3, matrix products, block_sum(): return jnp.dot(whole, unit_down, preferred_element_type=jnp.float32)  4.12 us
  transfers between devices with their start and end apart: 29, of which 14 were waited for; matrix products, arithmetic and copies ran while one was open for 20% of the time, Pallas kernels for 0%

profile of v5, /device:TPU:0, one launch (start us, length us, event | category | flops | bytes accessed | tf_op | source)
XLA Modules:
  0.0 139.5 jit_solution(4026972441448711931)
XLA Ops:
  0.7 0.9 pad_maximum_fusion.11.refs_0_
  1.7 5.1 %collective-permute-start = (bf16[168,512]{1,0:T(8,128)(2,1)S(1)}, bf16[168,512]{1,0:T(8,128)(2,1)S(1)}, u32[]{:S(2)}, u32[]{:S(2)}) collective-permute-start(bf16[168,512]{1,0:T(8,128)(2,1)S(1)} %pad_maximum_fusion.11.refs_0_), channel_id=1, source_target_pairs={{0,3},{1,2},{2,1},{3,0},{4,7},{5,6},{6,5},{7,4},{8,11},{9,10},{10,... | collective-permute-start | bytes 516104 | tf_op jit(solution)/shard_map/ppermute | solution.py:34
  7.4 1.0 pad_maximum_fusion.10
  8.4 1.7 %collective-permute-start.3 = (bf16[256,512]{1,0:T(8,128)(2,1)S(1)}, bf16[256,512]{1,0:T(8,128)(2,1)S(1)}, u32[]{:S(2)}, u32[]{:S(2)}) collective-permute-start(bf16[256,512]{1,0:T(8,128)(2,1)S(1)} %bitcast.97), channel_id=1, source_target_pairs={{0,8},{4,12},{8,0},{12,4},{16,24},{20,28},{24,16},{28,20},{1,9},{5... | collective-permute-start | bytes 786440 | tf_op jit(solution)/shard_map/ppermute | solution.py:30
  10.1 1.5 %collective-permute-start.4 = (bf16[256,512]{1,0:T(8,128)(2,1)S(1)}, bf16[256,512]{1,0:T(8,128)(2,1)S(1)}, u32[]{:S(2)}, u32[]{:S(2)}) collective-permute-start(bf16[256,512]{1,0:T(8,128)(2,1)S(1)} %bitcast.98), channel_id=1, source_target_pairs={{0,16},{4,20},{8,24},{12,28},{16,0},{20,4},{24,8},{28,12},{1,17},{... | collective-permute-start | bytes 786440 | tf_op jit(solution)/shard_map/ppermute | solution.py:30
  11.6 0.8 copy.29
  13.0 0.7 multiply_add_fusion
  13.7 0.7 copy.31
  14.7 0.7 select_reduce_fusion.2
  15.9 5.4 %collective-permute-done.2.refs_3_ = bf16[168,512]{1,0:T(8,128)(2,1)S(1)} collective-permute-done((bf16[168,512]{1,0:T(8,128)(2,1)S(1)}, bf16[168,512]{1,0:T(8,128)(2,1)S(1)}, u32[]{:S(2)}, u32[]{:S(2)}) %collective-permute-start.2) | collective-permute-done | bytes 172064 | tf_op jit(solution)/shard_map/ppermute | solution.py:34
  21.4 2.4 %collective-permute-start.6 = (bf16[256,512]{1,0:T(8,128)(2,1)S(1)}, bf16[256,512]{1,0:T(8,128)(2,1)S(1)}, u32[]{:S(2)}, u32[]{:S(2)}) collective-permute-start(bf16[256,512]{1,0:T(8,128)(2,1)S(1)} %bitcast.99), channel_id=1, source_target_pairs={{0,24},{4,28},{8,16},{12,20},{16,8},{20,12},{24,0},{28,4},{1,25},{... | collective-permute-start | bytes 786440 | tf_op jit(solution)/shard_map/ppermute | solution.py:30
  25.9 0.9 collective-permute-done.10
  27.3 1.9 %fusion.10 = f32[120,1408]{1,0:T(8,128)S(1)} fusion(bf16[120,2048]{1,0:T(8,128)(2,1)S(1)} %pad_maximum_fusion.7, bf16[1,1408,2048]{2,1,0:T(8,128)(2,1)S(1)} %copy-done), kind=kOutput, calls=%fused_computation.10 | convolution fusion | flops 692060160 | bytes 6934528 | tf_op jit(solution)/shard_map/dot_general | solution.py:19
  30.0 1.1 collective-permute-start.7
  31.1 2.0 %fusion.17 = bf16[120,1408]{1,0:T(8,128)(2,1)S(1)} fusion(bf16[120,2048]{1,0:T(8,128)(2,1)S(1)} %pad_maximum_fusion.7, bf16[1,1408,2048]{2,1,0:T(8,128)(2,1)S(1)} %bitcast.117, f32[120,1408]{1,0:T(8,128)S(1)} %fusion.10), kind=kOutput, calls=%fused_computation.17 | convolution fusion | flops 693073920 | bytes 7272448 | tf_op jit(solution)/shard_map/dot_general | solution.py:19
  33.1 2.3 %collective-permute-start.11 = (bf16[120,1408]{1,0:T(8,128)(2,1)S(1)}, bf16[120,1408]{1,0:T(8,128)(2,1)S(1)}, u32[]{:S(2)}, u32[]{:S(2)}) collective-permute-start(bf16[120,1408]{1,0:T(8,128)(2,1)S(1)} %fusion.17), channel_id=1, source_target_pairs={{0,3},{1,2},{2,1},{3,0},{4,7},{5,6},{6,5},{7,4},{8,11},{9,10},{10,... | collective-permute-start | bytes 1013768 | tf_op jit(solution)/shard_map/ppermute | solution.py:34
  35.5 4.0 %collective-permute-start.14 = (bf16[120,1408]{1,0:T(8,128)(2,1)S(1)}, bf16[120,1408]{1,0:T(8,128)(2,1)S(1)}, u32[]{:S(2)}, u32[]{:S(2)}) collective-permute-start(bf16[120,1408]{1,0:T(8,128)(2,1)S(1)} %fusion.17), channel_id=1, source_target_pairs={{0,2},{3,1},{4,6},{7,5},{8,10},{11,9},{12,14},{15,13},{16,18},{19,... | collective-permute-start | bytes 1013768 | tf_op jit(solution)/shard_map/ppermute | solution.py:34
  39.5 3.5 %collective-permute-done.8 = bf16[128,2048]{1,0:T(8,128)(2,1)S(1)} collective-permute-done((bf16[128,2048]{1,0:T(8,128)(2,1)S(1)}, bf16[128,2048]{1,0:T(8,128)(2,1)S(1)}, u32[]{:S(2)}, u32[]{:S(2)}) %collective-permute-start.8) | collective-permute-done | bytes 524320 | tf_op jit(solution)/shard_map/ppermute | solution.py:30
  43.7 1.5 %collective-permute-start.9 = (bf16[128,2048]{1,0:T(8,128)(2,1)S(1)}, bf16[128,2048]{1,0:T(8,128)(2,1)S(1)}, u32[]{:S(2)}, u32[]{:S(2)}) collective-permute-start(bf16[128,2048]{1,0:T(8,128)(2,1)S(1)} %pad_maximum_fusion.6), channel_id=1, source_target_pairs={{0,24},{4,28},{8,16},{12,20},{16,8},{20,12},{24,0},{28,4},{1,25},{... | collective-permute-start | bytes 1572872 | tf_op jit(solution)/shard_map/ppermute | solution.py:30
  45.6 0.7 collective-permute-done.12
  47.2 1.3 collective-permute-start.15
  48.5 2.6 %collective-permute-done.13 = bf16[120,1408]{1,0:T(8,128)(2,1)S(1)} collective-permute-done((bf16[120,1408]{1,0:T(8,128)(2,1)S(1)}, bf16[120,1408]{1,0:T(8,128)(2,1)S(1)}, u32[]{:S(2)}, u32[]{:S(2)}) %collective-permute-start.13) | collective-permute-done | bytes 337952 | tf_op jit(solution)/shard_map/ppermute | solution.py:34
  51.1 1.8 %fusion.8 = f32[240,1408]{1,0:T(8,128)S(1)} fusion(bf16[240,2048]{1,0:T(8,128)(2,1)S(1)} %pad_maximum_fusion.2, bf16[1,1408,2048]{2,1,0:T(8,128)(2,1)S(1)} %copy-done), kind=kOutput, calls=%fused_computation.8 | convolution fusion | flops 1384120320 | bytes 8101888 | tf_op jit(solution)/shard_map/dot_general | solution.py:19
  52.9 2.0 %multiply_convert_fusion = bf16[240,1408]{1,0:T(8,128)(2,1)S(1)} fusion(f32[240,1408]{1,0:T(8,128)S(1)} %fusion.8, bf16[240,2048]{1,0:T(8,128)(2,1)S(1)} %pad_maximum_fusion.2, bf16[1,1408,2048]{2,1,0:T(8,128)(2,1)S(1)} %bitcast.117), kind=kOutput, calls=%fused_computation.20 | convolution fusion | flops 1386147840 | bytes 8777728 | tf_op jit(solution)/shard_map/dot_general | solution.py:19
  55.0 0.7 collective-permute-start.20
  55.7 4.4 %collective-permute-start.19 = (bf16[248,1408]{1,0:T(8,128)(2,1)S(1)}, bf16[248,1408]{1,0:T(8,128)(2,1)S(1)}, u32[]{:S(2)}, u32[]{:S(2)}) collective-permute-start(bf16[248,1408]{1,0:T(8,128)(2,1)S(1)} %pad_maximum_fusion.3), channel_id=1, source_target_pairs={{0,1},{1,0},{2,3},{3,2},{4,5},{5,4},{6,7},{7,6},{8,9},{9,8},{10,11... | collective-permute-start | bytes 2095112 | tf_op jit(solution)/shard_map/ppermute | solution.py:34
  60.1 2.9 %collective-permute-start.18 = (bf16[248,1408]{1,0:T(8,128)(2,1)S(1)}, bf16[248,1408]{1,0:T(8,128)(2,1)S(1)}, u32[]{:S(2)}, u32[]{:S(2)}) collective-permute-start(bf16[248,1408]{1,0:T(8,128)(2,1)S(1)} %pad_maximum_fusion.3), channel_id=1, source_target_pairs={{0,2},{3,1},{4,6},{7,5},{8,10},{11,9},{12,14},{15,13},{16,18},{19,... | collective-permute-start | bytes 2095112 | tf_op jit(solution)/shard_map/ppermute | solution.py:34
  63.2 1.9 %fusion.6 = f32[120,1408]{1,0:T(8,128)S(1)} fusion(bf16[120,2048]{1,0:T(8,128)(2,1)S(1)} %pad_maximum_fusion.8, bf16[1,1408,2048]{2,1,0:T(8,128)(2,1)S(1)} %copy-done), kind=kOutput, calls=%fused_computation.6 | convolution fusion | flops 692060160 | bytes 6934528 | tf_op jit(solution)/shard_map/dot_general | solution.py:19
  65.2 2.0 %multiply_convert_fusion.1 = bf16[120,1408]{1,0:T(8,128)(2,1)S(1)} fusion(f32[120,1408]{1,0:T(8,128)S(1)} %fusion.6, bf16[120,2048]{1,0:T(8,128)(2,1)S(1)} %pad_maximum_fusion.8, bf16[1,1408,2048]{2,1,0:T(8,128)(2,1)S(1)} %bitcast.117), kind=kOutput, calls=%fused_computation.34 | convolution fusion | flops 693073920 | bytes 7272448 | tf_op jit(solution)/shard_map/dot_general | solution.py:19
  67.2 1.6 %collective-permute-start.17 = (bf16[120,1408]{1,0:T(8,128)(2,1)S(1)}, bf16[120,1408]{1,0:T(8,128)(2,1)}, u32[]{:S(2)}, u32[]{:S(2)}) collective-permute-start(bf16[120,1408]{1,0:T(8,128)(2,1)S(1)} %multiply_convert_fusion.1), channel_id=1, source_target_pairs={{0,3},{1,2},{2,1},{3,0},{4,7},{5,6},{6,5},{7,4},{8,11},{9,10},{10,... | collective-permute-start | bytes 1013768 | tf_op jit(solution)/shard_map/ppermute | solution.py:34
  69.1 0.9 convolution_convert_fusion.2
  71.9 22.2 %collective-permute-start.16 = (bf16[120,1408]{1,0:T(8,128)(2,1)S(1)}, bf16[120,1408]{1,0:T(8,128)(2,1)}, u32[]{:S(2)}, u32[]{:S(2)}) collective-permute-start(bf16[120,1408]{1,0:T(8,128)(2,1)S(1)} %multiply_convert_fusion.1), channel_id=1, source_target_pairs={{0,2},{3,1},{4,6},{7,5},{8,10},{11,9},{12,14},{15,13},{16,18},{19,... | collective-permute-start | bytes 1013768 | tf_op jit(solution)/shard_map/ppermute | solution.py:34
  94.0 1.3 collective-permute-start.23
  95.3 1.3 collective-permute-start.22
  96.6 11.7 %collective-permute-done.17 = bf16[120,1408]{1,0:T(8,128)(2,1)} collective-permute-done((bf16[120,1408]{1,0:T(8,128)(2,1)S(1)}, bf16[120,1408]{1,0:T(8,128)(2,1)}, u32[]{:S(2)}, u32[]{:S(2)}) %collective-permute-start.17) | collective-permute-done | bytes 337952 | tf_op jit(solution)/shard_map/ppermute | solution.py:34
  108.4 1.3 collective-permute-start.21
  109.8 1.0 constant_dynamic-update-slice_fusion
  111.0 0.9 fusion.68
  112.1 11.1 %collective-permute-done.22 = bf16[248,1408]{1,0:T(8,128)(2,1)S(1)} collective-permute-done((bf16[248,1408]{1,0:T(8,128)(2,1)S(1)}, bf16[248,1408]{1,0:T(8,128)(2,1)S(1)}, u32[]{:S(2)}, u32[]{:S(2)}) %collective-permute-start.22) | collective-permute-done | bytes 698400 | tf_op jit(solution)/shard_map/ppermute | solution.py:34
  123.6 2.2 %fusion.21 = bf16[240,512]{1,0:T(8,128)(2,1)} fusion(bf16[248,5632]{1,0:T(8,128)(2,1)S(1)} %add_dynamic-update-slice_fusion, bf16[1,5632,512]{2,1,0:T(8,128)(2,1)S(1)} %bitcast.92), kind=kOutput, calls=%fused_computation.22 | convolution fusion | flops 1384243200 | bytes 8716288 | tf_op jit(solution)/shard_map/dot_general | solution.py:299
  126.8 1.4 %fusion.27 = f32[120,512]{1,0:T(8,128)S(1)} fusion(bf16[1408,512]{1,0:T(8,128)(2,1)S(1)} %constant_dynamic-slice_fusion, bf16[120,1408]{1,0:T(8,128)(2,1)} %collective-permute-done.16, bf16[120,1408]{1,0:T(8,128)(2,1)} %collective-permute-done.21), kind=kOutput, calls=%fused_computation.43 | convolution fusion | flops 173184000 | bytes 2363392 | tf_op jit(solution)/shard_map/dot_general | solution.py:364
  128.3 1.1 collective-permute-start.27
  129.5 2.0 %collective-permute-start.25 = (bf16[120,512]{1,0:T(8,128)(2,1)S(1)}, bf16[120,512]{1,0:T(8,128)(2,1)S(1)}, u32[]{:S(2)}, u32[]{:S(2)}) collective-permute-start(bf16[120,512]{1,0:T(8,128)(2,1)S(1)} %get-tuple-element.147), channel_id=1, source_target_pairs={{0,8},{4,12},{8,0},{12,4},{16,24},{20,28},{24,16},{28,20},{1,9},{5... | collective-permute-start | bytes 368648 | tf_op jit(solution)/shard_map/ppermute | solution.py:30
  132.0 2.2 %collective-permute-done.27 = bf16[120,512]{1,0:T(8,128)(2,1)S(1)} collective-permute-done((bf16[120,512]{1,0:T(8,128)(2,1)S(1)}, bf16[120,512]{1,0:T(8,128)(2,1)S(1)}, u32[]{:S(2)}, u32[]{:S(2)}) %collective-permute-start.27) | collective-permute-done | bytes 122912 | tf_op jit(solution)/shard_map/ppermute | solution.py:30
  134.2 1.4 collective-permute-done.25
  135.6 0.8 collective-permute-done.26
  136.9 1.3 collective-permute-done.28
  138.8 0.7 add_convert_fusion
  (133 shorter events, 13.4 us)
Async XLA Ops:
  1.7 14.1 %collective-permute-start = (bf16[168,512]{1,0:T(8,128)(2,1)S(1)}, bf16[168,512]{1,0:T(8,128)(2,1)S(1)}, u32[]{:S(2)}, u32[]{:S(2)}) collective-permute-start(bf16[168,512]{1,0:T(8,128)(2,1)S(1)} %pad_maximum_fusion.11.refs_0_), channel_id=1, source_target_pairs={{0,3},{1,2},{2,1},{3,0},{4,7},{5,6},{6,5},{7,4},{8,11},{9,10},{10,... | collective-permute-start | bytes 516104 | tf_op jit(solution)/shard_map/ppermute | solution.py:34
  6.8 9.2 %collective-permute-start.1 = (bf16[168,512]{1,0:T(8,128)(2,1)S(1)}, bf16[168,512]{1,0:T(8,128)(2,1)S(1)}, u32[]{:S(2)}, u32[]{:S(2)}) collective-permute-start(bf16[168,512]{1,0:T(8,128)(2,1)S(1)} %pad_maximum_fusion.11.refs_0_), channel_id=1, source_target_pairs={{0,1},{1,0},{2,3},{3,2},{4,5},{5,4},{6,7},{7,6},{8,9},{9,8},{10,11... | collective-permute-start | bytes 516104 | tf_op jit(solution)/shard_map/ppermute | solution.py:34
  6.8 14.6 %collective-permute-start.2 = (bf16[168,512]{1,0:T(8,128)(2,1)S(1)}, bf16[168,512]{1,0:T(8,128)(2,1)S(1)}, u32[]{:S(2)}, u32[]{:S(2)}) collective-permute-start(bf16[168,512]{1,0:T(8,128)(2,1)S(1)} %pad_maximum_fusion.11.refs_0_), channel_id=1, source_target_pairs={{0,2},{1,3},{2,0},{3,1},{4,6},{5,7},{6,4},{7,5},{8,10},{9,11},{10,... | collective-permute-start | bytes 516104 | tf_op jit(solution)/shard_map/ppermute | solution.py:34
  8.4 15.7 %collective-permute-start.3 = (bf16[256,512]{1,0:T(8,128)(2,1)S(1)}, bf16[256,512]{1,0:T(8,128)(2,1)S(1)}, u32[]{:S(2)}, u32[]{:S(2)}) collective-permute-start(bf16[256,512]{1,0:T(8,128)(2,1)S(1)} %bitcast.97), channel_id=1, source_target_pairs={{0,8},{4,12},{8,0},{12,4},{16,24},{20,28},{24,16},{28,20},{1,9},{5... | collective-permute-start | bytes 786440 | tf_op jit(solution)/shard_map/ppermute | solution.py:30
  10.1 14.0 %collective-permute-start.4 = (bf16[256,512]{1,0:T(8,128)(2,1)S(1)}, bf16[256,512]{1,0:T(8,128)(2,1)S(1)}, u32[]{:S(2)}, u32[]{:S(2)}) collective-permute-start(bf16[256,512]{1,0:T(8,128)(2,1)S(1)} %bitcast.98), channel_id=1, source_target_pairs={{0,16},{4,20},{8,24},{12,28},{16,0},{20,4},{24,8},{28,12},{1,17},{... | collective-permute-start | bytes 786440 | tf_op jit(solution)/shard_map/ppermute | solution.py:30
  21.4 8.6 %collective-permute-start.6 = (bf16[256,512]{1,0:T(8,128)(2,1)S(1)}, bf16[256,512]{1,0:T(8,128)(2,1)S(1)}, u32[]{:S(2)}, u32[]{:S(2)}) collective-permute-start(bf16[256,512]{1,0:T(8,128)(2,1)S(1)} %bitcast.99), channel_id=1, source_target_pairs={{0,24},{4,28},{8,16},{12,20},{16,8},{20,12},{24,0},{28,4},{1,25},{... | collective-permute-start | bytes 786440 | tf_op jit(solution)/shard_map/ppermute | solution.py:30
  24.7 2.6 %copy-start = (bf16[1,1408,2048]{2,1,0:T(8,128)(2,1)S(1)}, bf16[1,1408,2048]{2,1,0:T(8,128)(2,1)}, u32[]{:S(2)}) copy-start(bf16[1,1408,2048]{2,1,0:T(8,128)(2,1)} %param.17) | copy-start | bytes 17301508
  25.2 1.6 %collective-permute-start.10 = (bf16[64,2048]{1,0:T(8,128)(2,1)S(1)}, bf16[64,2048]{1,0:T(8,128)(2,1)S(1)}, u32[]{:S(2)}, u32[]{:S(2)}) collective-permute-start(bf16[64,2048]{1,0:T(8,128)(2,1)S(1)} %slice.134), channel_id=1, source_target_pairs={{0,4},{4,0},{8,12},{12,8},{16,20},{20,16},{24,28},{28,24},{1,5},{5... | collective-permute-start | bytes 786440 | tf_op jit(solution)/shard_map/ppermute | solution.py:30
  25.3 4.0 %collective-permute-start.5 = (bf16[3,64,2048]{2,1,0:T(8,128)(2,1)S(1)}, bf16[3,64,2048]{2,1,0:T(8,128)(2,1)S(1)}, u32[]{:S(2)}, u32[]{:S(2)}) collective-permute-start(bf16[3,64,2048]{2,1,0:T(8,128)(2,1)S(1)} %bitcast.103), channel_id=1, source_target_pairs={{0,4},{4,0},{8,12},{12,8},{16,20},{20,16},{24,28},{28,24},{1,5},{5... | collective-permute-start | bytes 2359304 | tf_op jit(solution)/shard_map/ppermute | solution.py:30
  26.8 4.3 %slice-start.2 = ((s8[5767168]{0:T(1024)(128)(4,1)}), s8[4194304]{0:T(1024)(128)(4,1)S(1)}, s32[]{:S(2)}) async-start(s8[5767168]{0:T(1024)(128)(4,1)} %bitcast.116), calls=%async_computation.2 | async-start | bytes 8388608
  27.3 3.8 %slice-start.3 = ((s8[5767168]{0:T(1024)(128)(4,1)}), s8[1572864]{0:T(1024)(128)(4,1)S(1)}, s32[]{:S(2)}) async-start(s8[5767168]{0:T(1024)(128)(4,1)} %bitcast.116), calls=%async_computation.3 | async-start | bytes 3145728
  29.4 13.6 %collective-permute-start.8 = (bf16[128,2048]{1,0:T(8,128)(2,1)S(1)}, bf16[128,2048]{1,0:T(8,128)(2,1)S(1)}, u32[]{:S(2)}, u32[]{:S(2)}) collective-permute-start(bf16[128,2048]{1,0:T(8,128)(2,1)S(1)} %pad_maximum_fusion.5), channel_id=1, source_target_pairs={{0,16},{4,20},{8,24},{12,28},{16,0},{20,4},{24,8},{28,12},{1,17},{... | collective-permute-start | bytes 1572872 | tf_op jit(solution)/shard_map/ppermute | solution.py:30
  30.0 13.4 %collective-permute-start.7 = (bf16[128,2048]{1,0:T(8,128)(2,1)S(1)}, bf16[128,2048]{1,0:T(8,128)(2,1)S(1)}, u32[]{:S(2)}, u32[]{:S(2)}) collective-permute-start(bf16[128,2048]{1,0:T(8,128)(2,1)S(1)} %pad_maximum_fusion.4), channel_id=1, source_target_pairs={{0,8},{4,12},{8,0},{12,4},{16,24},{20,28},{24,16},{28,20},{1,9},{5... | collective-permute-start | bytes 1572872 | tf_op jit(solution)/shard_map/ppermute | solution.py:30
  33.1 14.0 %collective-permute-start.11 = (bf16[120,1408]{1,0:T(8,128)(2,1)S(1)}, bf16[120,1408]{1,0:T(8,128)(2,1)S(1)}, u32[]{:S(2)}, u32[]{:S(2)}) collective-permute-start(bf16[120,1408]{1,0:T(8,128)(2,1)S(1)} %fusion.17), channel_id=1, source_target_pairs={{0,3},{1,2},{2,1},{3,0},{4,7},{5,6},{6,5},{7,4},{8,11},{9,10},{10,... | collective-permute-start | bytes 1013768 | tf_op jit(solution)/shard_map/ppermute | solution.py:34
  35.4 15.6 %collective-permute-start.13 = (bf16[120,1408]{1,0:T(8,128)(2,1)S(1)}, bf16[120,1408]{1,0:T(8,128)(2,1)S(1)}, u32[]{:S(2)}, u32[]{:S(2)}) collective-permute-start(bf16[120,1408]{1,0:T(8,128)(2,1)S(1)} %fusion.17), channel_id=1, source_target_pairs={{0,1},{1,0},{2,3},{3,2},{4,5},{5,4},{6,7},{7,6},{8,9},{9,8},{10,11... | collective-permute-start | bytes 1013768 | tf_op jit(solution)/shard_map/ppermute | solution.py:34
  35.5 27.7 %collective-permute-start.14 = (bf16[120,1408]{1,0:T(8,128)(2,1)S(1)}, bf16[120,1408]{1,0:T(8,128)(2,1)S(1)}, u32[]{:S(2)}, u32[]{:S(2)}) collective-permute-start(bf16[120,1408]{1,0:T(8,128)(2,1)S(1)} %fusion.17), channel_id=1, source_target_pairs={{0,2},{3,1},{4,6},{7,5},{8,10},{11,9},{12,14},{15,13},{16,18},{19,... | collective-permute-start | bytes 1013768 | tf_op jit(solution)/shard_map/ppermute | solution.py:34
  43.5 2.7 %collective-permute-start.12 = (bf16[4,256,512]{2,1,0:T(8,128)(2,1)S(1)}, bf16[4,256,512]{2,1,0:T(8,128)(2,1)S(1)}, u32[]{:S(2)}, u32[]{:S(2)}) collective-permute-start(bf16[4,256,512]{2,1,0:T(8,128)(2,1)S(1)} %get-tuple-element.132), channel_id=1, source_target_pairs={{0,4},{4,0},{8,12},{12,8},{16,20},{20,16},{24,28},{28,24},{1,5},{5... | collective-permute-start | bytes 3145736 | tf_op jit(solution)/shard_map/ppermute | solution.py:30
  43.7 16.4 %collective-permute-start.9 = (bf16[128,2048]{1,0:T(8,128)(2,1)S(1)}, bf16[128,2048]{1,0:T(8,128)(2,1)S(1)}, u32[]{:S(2)}, u32[]{:S(2)}) collective-permute-start(bf16[128,2048]{1,0:T(8,128)(2,1)S(1)} %pad_maximum_fusion.6), channel_id=1, source_target_pairs={{0,24},{4,28},{8,16},{12,20},{16,8},{20,12},{24,0},{28,4},{1,25},{... | collective-permute-start | bytes 1572872 | tf_op jit(solution)/shard_map/ppermute | solution.py:30
  47.2 16.0 %collective-permute-start.15 = (bf16[120,1408]{1,0:T(8,128)(2,1)S(1)}, bf16[120,1408]{1,0:T(8,128)(2,1)S(1)}, u32[]{:S(2)}, u32[]{:S(2)}) collective-permute-start(bf16[120,1408]{1,0:T(8,128)(2,1)S(1)} %collective-permute-done.11), channel_id=1, source_target_pairs={{1,0},{2,3},{5,4},{6,7},{9,8},{10,11},{13,12},{14,15},{17,16},{18,... | collective-permute-start | bytes 1013768 | tf_op jit(solution)/shard_map/ppermute | solution.py:34
  55.0 16.9 %collective-permute-start.20 = (bf16[248,1408]{1,0:T(8,128)(2,1)S(1)}, bf16[248,1408]{1,0:T(8,128)(2,1)S(1)}, u32[]{:S(2)}, u32[]{:S(2)}) collective-permute-start(bf16[248,1408]{1,0:T(8,128)(2,1)S(1)} %pad_maximum_fusion.3), channel_id=1, source_target_pairs={{1,2},{2,1},{5,6},{6,5},{9,10},{10,9},{13,14},{14,13},{17,18},{18,... | collective-permute-start | bytes 2095112 | tf_op jit(solution)/shard_map/ppermute | solution.py:34
  55.7 38.4 %collective-permute-start.19 = (bf16[248,1408]{1,0:T(8,128)(2,1)S(1)}, bf16[248,1408]{1,0:T(8,128)(2,1)S(1)}, u32[]{:S(2)}, u32[]{:S(2)}) collective-permute-start(bf16[248,1408]{1,0:T(8,128)(2,1)S(1)} %pad_maximum_fusion.3), channel_id=1, source_target_pairs={{0,1},{1,0},{2,3},{3,2},{4,5},{5,4},{6,7},{7,6},{8,9},{9,8},{10,11... | collective-permute-start | bytes 2095112 | tf_op jit(solution)/shard_map/ppermute | solution.py:34
  60.1 35.2 %collective-permute-start.18 = (bf16[248,1408]{1,0:T(8,128)(2,1)S(1)}, bf16[248,1408]{1,0:T(8,128)(2,1)S(1)}, u32[]{:S(2)}, u32[]{:S(2)}) collective-permute-start(bf16[248,1408]{1,0:T(8,128)(2,1)S(1)} %pad_maximum_fusion.3), channel_id=1, source_target_pairs={{0,2},{3,1},{4,6},{7,5},{8,10},{11,9},{12,14},{15,13},{16,18},{19,... | collective-permute-start | bytes 2095112 | tf_op jit(solution)/shard_map/ppermute | solution.py:34
  63.2 5.9 %slice-start = ((s8[5767168]{0:T(1024)(128)(4,1)}), s8[4194304]{0:T(1024)(128)(4,1)S(1)}, s32[]{:S(2)}) async-start(s8[5767168]{0:T(1024)(128)(4,1)} %bitcast.91), calls=%async_computation | async-start | bytes 8388608
  65.2 3.9 %slice-start.1 = ((s8[5767168]{0:T(1024)(128)(4,1)}), s8[1572864]{0:T(1024)(128)(4,1)S(1)}, s32[]{:S(2)}) async-start(s8[5767168]{0:T(1024)(128)(4,1)} %bitcast.91), calls=%async_computation.1 | async-start | bytes 3145728
  67.2 42.6 %collective-permute-start.24 = (bf16[120,1408]{1,0:T(8,128)(2,1)S(1)}, bf16[120,1408]{1,0:T(8,128)(2,1)S(1)}, u32[]{:S(2)}, u32[]{:S(2)}) collective-permute-start(bf16[120,1408]{1,0:T(8,128)(2,1)S(1)} %multiply_convert_fusion.1), channel_id=1, source_target_pairs={{0,1},{1,0},{2,3},{3,2},{4,5},{5,4},{6,7},{7,6},{8,9},{9,8},{10,11... | collective-permute-start | bytes 1013768 | tf_op jit(solution)/shard_map/ppermute | solution.py:34
  67.2 41.1 %collective-permute-start.17 = (bf16[120,1408]{1,0:T(8,128)(2,1)S(1)}, bf16[120,1408]{1,0:T(8,128)(2,1)}, u32[]{:S(2)}, u32[]{:S(2)}) collective-permute-start(bf16[120,1408]{1,0:T(8,128)(2,1)S(1)} %multiply_convert_fusion.1), channel_id=1, source_target_pairs={{0,3},{1,2},{2,1},{3,0},{4,7},{5,6},{6,5},{7,4},{8,11},{9,10},{10,... | collective-permute-start | bytes 1013768 | tf_op jit(solution)/shard_map/ppermute | solution.py:34
  69.1 1.0 copy-start.6
  71.9 54.5 %collective-permute-start.16 = (bf16[120,1408]{1,0:T(8,128)(2,1)S(1)}, bf16[120,1408]{1,0:T(8,128)(2,1)}, u32[]{:S(2)}, u32[]{:S(2)}) collective-permute-start(bf16[120,1408]{1,0:T(8,128)(2,1)S(1)} %multiply_convert_fusion.1), channel_id=1, source_target_pairs={{0,2},{3,1},{4,6},{7,5},{8,10},{11,9},{12,14},{15,13},{16,18},{19,... | collective-permute-start | bytes 1013768 | tf_op jit(solution)/shard_map/ppermute | solution.py:34
  94.0 29.3 %collective-permute-start.23 = (bf16[248,1408]{1,0:T(8,128)(2,1)S(1)}, bf16[248,1408]{1,0:T(8,128)(2,1)S(1)}, u32[]{:S(2)}, u32[]{:S(2)}) collective-permute-start(bf16[248,1408]{1,0:T(8,128)(2,1)S(1)} %collective-permute-done.20), channel_id=1, source_target_pairs={{1,0},{2,3},{5,4},{6,7},{9,8},{10,11},{13,12},{14,15},{17,16},{18,... | collective-permute-start | bytes 2095112 | tf_op jit(solution)/shard_map/ppermute | solution.py:34
  95.3 27.8 %collective-permute-start.22 = (bf16[248,1408]{1,0:T(8,128)(2,1)S(1)}, bf16[248,1408]{1,0:T(8,128)(2,1)S(1)}, u32[]{:S(2)}, u32[]{:S(2)}) collective-permute-start(bf16[248,1408]{1,0:T(8,128)(2,1)S(1)} %collective-permute-done.18), channel_id=1, source_target_pairs={{1,0},{2,3},{5,4},{6,7},{9,8},{10,11},{13,12},{14,15},{17,16},{18,... | collective-permute-start | bytes 2095112 | tf_op jit(solution)/shard_map/ppermute | solution.py:34
  108.4 18.5 %collective-permute-start.21 = (bf16[120,1408]{1,0:T(8,128)(2,1)}, bf16[120,1408]{1,0:T(8,128)(2,1)}, u32[]{:S(2)}, u32[]{:S(2)}) collective-permute-start(bf16[120,1408]{1,0:T(8,128)(2,1)} %collective-permute-done.17), channel_id=1, source_target_pairs={{1,0},{2,3},{5,4},{6,7},{9,8},{10,11},{13,12},{14,15},{17,16},{18,... | collective-permute-start | bytes 1013768 | tf_op jit(solution)/shard_map/ppermute | solution.py:34
  126.4 3.1 %copy-start.5 = (bf16[240,512]{1,0:T(8,128)(2,1)S(1)}, bf16[240,512]{1,0:T(8,128)(2,1)}, u32[]{:S(2)}) copy-start(bf16[240,512]{1,0:T(8,128)(2,1)} %fusion.21) | copy-start | bytes 737284
  128.3 8.4 %copy-start.4 = (bf16[240,160]{0,1:T(8,128)(2,1)S(1)}, bf16[240,160]{0,1:T(8,128)(2,1)}, u32[]{:S(2)}) copy-start(bf16[240,160]{0,1:T(8,128)(2,1)} %get-tuple-element.122) | copy-start | bytes 230404
  128.3 5.8 %collective-permute-start.27 = (bf16[120,512]{1,0:T(8,128)(2,1)S(1)}, bf16[120,512]{1,0:T(8,128)(2,1)S(1)}, u32[]{:S(2)}, u32[]{:S(2)}) collective-permute-start(bf16[120,512]{1,0:T(8,128)(2,1)S(1)} %add_convert_fusion.1), channel_id=1, source_target_pairs={{0,24},{4,28},{8,16},{12,20},{16,8},{20,12},{24,0},{28,4},{1,25},{... | collective-permute-start | bytes 368648 | tf_op jit(solution)/shard_map/ppermute | solution.py:30
  129.5 8.7 %copy-start.3 = (bf16[240,160]{0,1:T(8,128)(2,1)S(1)}, bf16[240,160]{0,1:T(8,128)(2,1)}, u32[]{:S(2)}) copy-start(bf16[240,160]{0,1:T(8,128)(2,1)} %get-tuple-element.123) | copy-start | bytes 230404
  129.5 6.1 %collective-permute-start.25 = (bf16[120,512]{1,0:T(8,128)(2,1)S(1)}, bf16[120,512]{1,0:T(8,128)(2,1)S(1)}, u32[]{:S(2)}, u32[]{:S(2)}) collective-permute-start(bf16[120,512]{1,0:T(8,128)(2,1)S(1)} %get-tuple-element.147), channel_id=1, source_target_pairs={{0,8},{4,12},{8,0},{12,4},{16,24},{20,28},{24,16},{28,20},{1,9},{5... | collective-permute-start | bytes 368648 | tf_op jit(solution)/shard_map/ppermute | solution.py:30
  131.5 4.9 %collective-permute-start.26 = (bf16[120,512]{1,0:T(8,128)(2,1)S(1)}, bf16[120,512]{1,0:T(8,128)(2,1)S(1)}, u32[]{:S(2)}, u32[]{:S(2)}) collective-permute-start(bf16[120,512]{1,0:T(8,128)(2,1)S(1)} %get-tuple-element.148), channel_id=1, source_target_pairs={{0,16},{4,20},{8,24},{12,28},{16,0},{20,4},{24,8},{28,12},{1,17},{... | collective-permute-start | bytes 368648 | tf_op jit(solution)/shard_map/ppermute | solution.py:30
  136.4 2.0 %copy-start.2 = (bf16[240,160]{0,1:T(8,128)(2,1)S(1)}, bf16[240,160]{0,1:T(8,128)(2,1)}, u32[]{:S(2)}) copy-start(bf16[240,160]{0,1:T(8,128)(2,1)} %get-tuple-element.124) | copy-start | bytes 230404
  136.4 2.1 %copy-start.1 = (bf16[240,160]{0,1:T(8,128)(2,1)S(1)}, bf16[240,160]{0,1:T(8,128)(2,1)}, u32[]{:S(2)}) copy-start(bf16[240,160]{0,1:T(8,128)(2,1)} %get-tuple-element.116) | copy-start | bytes 230404
  136.5 1.6 %collective-permute-start.28 = (bf16[4,60,512]{2,1,0:T(8,128)(2,1)S(1)}, bf16[4,60,512]{2,1,0:T(8,128)(2,1)S(1)}, u32[]{:S(2)}, u32[]{:S(2)}) collective-permute-start(bf16[4,60,512]{2,1,0:T(8,128)(2,1)S(1)} %get-tuple-element.146), channel_id=1, source_target_pairs={{0,4},{4,0},{8,12},{12,8},{16,20},{20,16},{24,28},{28,24},{1,5},{5... | collective-permute-start | bytes 737288 | tf_op jit(solution)/shard_map/ppermute | solution.py:30

commit v6 on v5

--- a/solution.py
+++ b/solution.py
@@ -223,7 +223,7 @@
         for offset in range(chips)
     ]
     if line:
-        pairs[1], by_chip[-1] = tie(pairs[1], by_chip[-1])
+        pairs[1], pairs[2], by_chip[-1] = tie(pairs[1], pairs[2], by_chip[-1])
     for offset in range(1, chips):
         if offset == chips - 1:
             pairs[1:] = tie(*pairs[1:])
@@ -358,8 +358,8 @@
         facing_down = lax.dynamic_slice(
             late_down, ((col_at ^ 2) * hidden_part, 0), (hidden_part, width_part)
         )
-        facing, passed, branch, part, facing_down, place_weights = tie(
-            facing, passed, branch, part, facing_down, place_weights
+        facing, passed, branch, part, facing_down = tie(
+            facing, passed, branch, part, facing_down
         )
         out = part + jnp.dot(facing + passed, facing_down, preferred_element_type=jnp.float32)
     else:

time: 140 us -> 138 us (0.986)
  waiting for transfers between devices: 42.6 us -> 40.8 us
  starting transfers between devices: 62.4 us -> 64 us
    ppermute x13, waiting for transfers between devices: 11.1 us -> 9.12 us  [row_xor(): lax.ppermute(value, 'row', [(i, i ^ by) for i in range(lax.axis_size('row...]
  transfers between devices with their start and end apart: 29 -> 29, of which waited for: 14 -> 16; matrix products, arithmetic and copies ran while one was open for 20% -> 20% of each run, Pallas kernels for 0% -> 0%
where the time goes in v6:
time: 138 us
  starting transfers between devices  64 us (46%)
  waiting for transfers between devices  40.8 us (30%)
  matrix products  19.9 us (14%)
  other arithmetic  7.08 us (5%)
  local copies, waits for them, and re-layouts  4.9 us (4%)
    ppermute x16, starting transfers between devices, along(): return lax.ppermute(value, 'col', pairs)  49.5 us
    ppermute x16, waiting for transfers between devices, along(): return lax.ppermute(value, 'col', pairs)  31.7 us
    ppermute x13, starting transfers between devices, row_xor(): lax.ppermute(value, 'row', [(i, i ^ by) for i in range(lax.axis_size('row...  14.6 us
    dot_general x7, matrix products, contract_last(): lax.dot_general(left, right, (((1,), (1,)), ((), ())), preferred_element_...  12.1 us
    ppermute x13, waiting for transfers between devices, row_xor(): lax.ppermute(value, 'row', [(i, i ^ by) for i in range(lax.axis_size('row...  9.12 us
    dot_general x3, matrix products, block_sum(): return jnp.dot(whole, unit_down, preferred_element_type=jnp.float32)  4.14 us
  transfers between devices with their start and end apart: 29, of which 16 were waited for; matrix products, arithmetic and copies ran while one was open for 20% of the time, Pallas kernels for 0%

profile of v6, /device:TPU:0, one launch (start us, length us, event | category | flops | bytes accessed | tf_op | source)
XLA Modules:
  0.0 137.9 jit_solution(10384886612756916854)
XLA Ops:
  0.7 0.9 pad_maximum_fusion.11.refs_0_
  1.7 5.1 %collective-permute-start = (bf16[168,512]{1,0:T(8,128)(2,1)S(1)}, bf16[168,512]{1,0:T(8,128)(2,1)S(1)}, u32[]{:S(2)}, u32[]{:S(2)}) collective-permute-start(bf16[168,512]{1,0:T(8,128)(2,1)S(1)} %pad_maximum_fusion.11.refs_0_), channel_id=1, source_target_pairs={{0,3},{1,2},{2,1},{3,0},{4,7},{5,6},{6,5},{7,4},{8,11},{9,10},{10,... | collective-permute-start | bytes 516104 | tf_op jit(solution)/shard_map/ppermute | solution.py:34
  7.4 1.0 pad_maximum_fusion.10
  8.4 1.7 %collective-permute-start.3 = (bf16[256,512]{1,0:T(8,128)(2,1)S(1)}, bf16[256,512]{1,0:T(8,128)(2,1)S(1)}, u32[]{:S(2)}, u32[]{:S(2)}) collective-permute-start(bf16[256,512]{1,0:T(8,128)(2,1)S(1)} %bitcast.93), channel_id=1, source_target_pairs={{0,8},{4,12},{8,0},{12,4},{16,24},{20,28},{24,16},{28,20},{1,9},{5... | collective-permute-start | bytes 786440 | tf_op jit(solution)/shard_map/ppermute | solution.py:30
  10.1 1.5 %collective-permute-start.4 = (bf16[256,512]{1,0:T(8,128)(2,1)S(1)}, bf16[256,512]{1,0:T(8,128)(2,1)S(1)}, u32[]{:S(2)}, u32[]{:S(2)}) collective-permute-start(bf16[256,512]{1,0:T(8,128)(2,1)S(1)} %bitcast.94), channel_id=1, source_target_pairs={{0,16},{4,20},{8,24},{12,28},{16,0},{20,4},{24,8},{28,12},{1,17},{... | collective-permute-start | bytes 786440 | tf_op jit(solution)/shard_map/ppermute | solution.py:30
  11.6 0.8 copy.29
  13.0 0.7 multiply_add_fusion
  13.7 0.7 copy.31
  14.7 0.7 select_reduce_fusion.2
  15.9 5.4 %collective-permute-done.2.refs_3_ = bf16[168,512]{1,0:T(8,128)(2,1)S(1)} collective-permute-done((bf16[168,512]{1,0:T(8,128)(2,1)S(1)}, bf16[168,512]{1,0:T(8,128)(2,1)S(1)}, u32[]{:S(2)}, u32[]{:S(2)}) %collective-permute-start.2) | collective-permute-done | bytes 172064 | tf_op jit(solution)/shard_map/ppermute | solution.py:34
  21.4 2.4 %collective-permute-start.6 = (bf16[256,512]{1,0:T(8,128)(2,1)S(1)}, bf16[256,512]{1,0:T(8,128)(2,1)S(1)}, u32[]{:S(2)}, u32[]{:S(2)}) collective-permute-start(bf16[256,512]{1,0:T(8,128)(2,1)S(1)} %bitcast.95), channel_id=1, source_target_pairs={{0,24},{4,28},{8,16},{12,20},{16,8},{20,12},{24,0},{28,4},{1,25},{... | collective-permute-start | bytes 786440 | tf_op jit(solution)/shard_map/ppermute | solution.py:30
  25.9 0.9 collective-permute-done.10
  27.3 1.9 %fusion.10 = f32[120,1408]{1,0:T(8,128)S(1)} fusion(bf16[120,2048]{1,0:T(8,128)(2,1)S(1)} %pad_maximum_fusion.7, bf16[1,1408,2048]{2,1,0:T(8,128)(2,1)S(1)} %copy-done), kind=kOutput, calls=%fused_computation.10 | convolution fusion | flops 692060160 | bytes 6934528 | tf_op jit(solution)/shard_map/dot_general | solution.py:19
  29.6 1.5 %collective-permute-start.7 = (bf16[128,2048]{1,0:T(8,128)(2,1)S(1)}, bf16[128,2048]{1,0:T(8,128)(2,1)S(1)}, u32[]{:S(2)}, u32[]{:S(2)}) collective-permute-start(bf16[128,2048]{1,0:T(8,128)(2,1)S(1)} %pad_maximum_fusion.4), channel_id=1, source_target_pairs={{0,8},{4,12},{8,0},{12,4},{16,24},{20,28},{24,16},{28,20},{1,9},{5... | collective-permute-start | bytes 1572872 | tf_op jit(solution)/shard_map/ppermute | solution.py:30
  31.1 1.5 %collective-permute-start.8 = (bf16[128,2048]{1,0:T(8,128)(2,1)S(1)}, bf16[128,2048]{1,0:T(8,128)(2,1)S(1)}, u32[]{:S(2)}, u32[]{:S(2)}) collective-permute-start(bf16[128,2048]{1,0:T(8,128)(2,1)S(1)} %pad_maximum_fusion.5), channel_id=1, source_target_pairs={{0,16},{4,20},{8,24},{12,28},{16,0},{20,4},{24,8},{28,12},{1,17},{... | collective-permute-start | bytes 1572872 | tf_op jit(solution)/shard_map/ppermute | solution.py:30
  32.6 2.0 %fusion.17 = bf16[120,1408]{1,0:T(8,128)(2,1)S(1)} fusion(bf16[120,2048]{1,0:T(8,128)(2,1)S(1)} %pad_maximum_fusion.7, bf16[1,1408,2048]{2,1,0:T(8,128)(2,1)S(1)} %bitcast.113, f32[120,1408]{1,0:T(8,128)S(1)} %fusion.10), kind=kOutput, calls=%fused_computation.17 | convolution fusion | flops 693073920 | bytes 7272448 | tf_op jit(solution)/shard_map/dot_general | solution.py:19
  34.6 2.4 %collective-permute-start.11 = (bf16[120,1408]{1,0:T(8,128)(2,1)S(1)}, bf16[120,1408]{1,0:T(8,128)(2,1)S(1)}, u32[]{:S(2)}, u32[]{:S(2)}) collective-permute-start(bf16[120,1408]{1,0:T(8,128)(2,1)S(1)} %fusion.17), channel_id=1, source_target_pairs={{0,3},{1,2},{2,1},{3,0},{4,7},{5,6},{6,5},{7,4},{8,11},{9,10},{10,... | collective-permute-start | bytes 1013768 | tf_op jit(solution)/shard_map/ppermute | solution.py:34
  37.0 4.0 %collective-permute-start.14 = (bf16[120,1408]{1,0:T(8,128)(2,1)S(1)}, bf16[120,1408]{1,0:T(8,128)(2,1)S(1)}, u32[]{:S(2)}, u32[]{:S(2)}) collective-permute-start(bf16[120,1408]{1,0:T(8,128)(2,1)S(1)} %fusion.17), channel_id=1, source_target_pairs={{0,2},{3,1},{4,6},{7,5},{8,10},{11,9},{12,14},{15,13},{16,18},{19,... | collective-permute-start | bytes 1013768 | tf_op jit(solution)/shard_map/ppermute | solution.py:34
  41.0 2.0 %collective-permute-done.7 = bf16[128,2048]{1,0:T(8,128)(2,1)S(1)} collective-permute-done((bf16[128,2048]{1,0:T(8,128)(2,1)S(1)}, bf16[128,2048]{1,0:T(8,128)(2,1)S(1)}, u32[]{:S(2)}, u32[]{:S(2)}) %collective-permute-start.7) | collective-permute-done | bytes 524320 | tf_op jit(solution)/shard_map/ppermute | solution.py:30
  43.6 1.5 %collective-permute-start.9 = (bf16[128,2048]{1,0:T(8,128)(2,1)S(1)}, bf16[128,2048]{1,0:T(8,128)(2,1)S(1)}, u32[]{:S(2)}, u32[]{:S(2)}) collective-permute-start(bf16[128,2048]{1,0:T(8,128)(2,1)S(1)} %pad_maximum_fusion.6), channel_id=1, source_target_pairs={{0,24},{4,28},{8,16},{12,20},{16,8},{20,12},{24,0},{28,4},{1,25},{... | collective-permute-start | bytes 1572872 | tf_op jit(solution)/shard_map/ppermute | solution.py:30
  45.5 0.7 collective-permute-done.12
  47.4 1.3 collective-permute-start.15
  48.6 4.0 %collective-permute-done.13 = bf16[120,1408]{1,0:T(8,128)(2,1)S(1)} collective-permute-done((bf16[120,1408]{1,0:T(8,128)(2,1)S(1)}, bf16[120,1408]{1,0:T(8,128)(2,1)S(1)}, u32[]{:S(2)}, u32[]{:S(2)}) %collective-permute-start.13) | collective-permute-done | bytes 337952 | tf_op jit(solution)/shard_map/ppermute | solution.py:34
  52.6 1.8 %fusion.8 = f32[240,1408]{1,0:T(8,128)S(1)} fusion(bf16[240,2048]{1,0:T(8,128)(2,1)S(1)} %pad_maximum_fusion.2, bf16[1,1408,2048]{2,1,0:T(8,128)(2,1)S(1)} %copy-done), kind=kOutput, calls=%fused_computation.8 | convolution fusion | flops 1384120320 | bytes 8101888 | tf_op jit(solution)/shard_map/dot_general | solution.py:19
  54.4 2.0 %multiply_convert_fusion = bf16[240,1408]{1,0:T(8,128)(2,1)S(1)} fusion(f32[240,1408]{1,0:T(8,128)S(1)} %fusion.8, bf16[240,2048]{1,0:T(8,128)(2,1)S(1)} %pad_maximum_fusion.2, bf16[1,1408,2048]{2,1,0:T(8,128)(2,1)S(1)} %bitcast.113), kind=kOutput, calls=%fused_computation.20 | convolution fusion | flops 1386147840 | bytes 8777728 | tf_op jit(solution)/shard_map/dot_general | solution.py:19
  56.5 0.7 collective-permute-start.20
  57.2 4.4 %collective-permute-start.19 = (bf16[248,1408]{1,0:T(8,128)(2,1)S(1)}, bf16[248,1408]{1,0:T(8,128)(2,1)S(1)}, u32[]{:S(2)}, u32[]{:S(2)}) collective-permute-start(bf16[248,1408]{1,0:T(8,128)(2,1)S(1)} %pad_maximum_fusion.3), channel_id=1, source_target_pairs={{0,1},{1,0},{2,3},{3,2},{4,5},{5,4},{6,7},{7,6},{8,9},{9,8},{10,11... | collective-permute-start | bytes 2095112 | tf_op jit(solution)/shard_map/ppermute | solution.py:34
  61.6 3.0 %collective-permute-start.18 = (bf16[248,1408]{1,0:T(8,128)(2,1)S(1)}, bf16[248,1408]{1,0:T(8,128)(2,1)S(1)}, u32[]{:S(2)}, u32[]{:S(2)}) collective-permute-start(bf16[248,1408]{1,0:T(8,128)(2,1)S(1)} %pad_maximum_fusion.3), channel_id=1, source_target_pairs={{0,2},{3,1},{4,6},{7,5},{8,10},{11,9},{12,14},{15,13},{16,18},{19,... | collective-permute-start | bytes 2095112 | tf_op jit(solution)/shard_map/ppermute | solution.py:34
  64.7 1.9 %fusion.6 = f32[120,1408]{1,0:T(8,128)S(1)} fusion(bf16[120,2048]{1,0:T(8,128)(2,1)S(1)} %pad_maximum_fusion.8, bf16[1,1408,2048]{2,1,0:T(8,128)(2,1)S(1)} %copy-done), kind=kOutput, calls=%fused_computation.6 | convolution fusion | flops 692060160 | bytes 6934528 | tf_op jit(solution)/shard_map/dot_general | solution.py:19
  66.7 2.0 %multiply_convert_fusion.1 = bf16[120,1408]{1,0:T(8,128)(2,1)S(1)} fusion(f32[120,1408]{1,0:T(8,128)S(1)} %fusion.6, bf16[120,2048]{1,0:T(8,128)(2,1)S(1)} %pad_maximum_fusion.8, bf16[1,1408,2048]{2,1,0:T(8,128)(2,1)S(1)} %bitcast.113), kind=kOutput, calls=%fused_computation.34 | convolution fusion | flops 693073920 | bytes 7272448 | tf_op jit(solution)/shard_map/dot_general | solution.py:19
  68.7 1.6 %collective-permute-start.17 = (bf16[120,1408]{1,0:T(8,128)(2,1)S(1)}, bf16[120,1408]{1,0:T(8,128)(2,1)}, u32[]{:S(2)}, u32[]{:S(2)}) collective-permute-start(bf16[120,1408]{1,0:T(8,128)(2,1)S(1)} %multiply_convert_fusion.1), channel_id=1, source_target_pairs={{0,3},{1,2},{2,1},{3,0},{4,7},{5,6},{6,5},{7,4},{8,11},{9,10},{10,... | collective-permute-start | bytes 1013768 | tf_op jit(solution)/shard_map/ppermute | solution.py:34
  70.6 0.9 convolution_convert_fusion.2
  71.8 22.5 %collective-permute-start.16 = (bf16[120,1408]{1,0:T(8,128)(2,1)S(1)}, bf16[120,1408]{1,0:T(8,128)(2,1)}, u32[]{:S(2)}, u32[]{:S(2)}) collective-permute-start(bf16[120,1408]{1,0:T(8,128)(2,1)S(1)} %multiply_convert_fusion.1), channel_id=1, source_target_pairs={{0,2},{3,1},{4,6},{7,5},{8,10},{11,9},{12,14},{15,13},{16,18},{19,... | collective-permute-start | bytes 1013768 | tf_op jit(solution)/shard_map/ppermute | solution.py:34
  94.3 1.3 collective-permute-start.23
  95.6 1.3 collective-permute-start.22
  96.9 11.4 %collective-permute-done.17 = bf16[120,1408]{1,0:T(8,128)(2,1)} collective-permute-done((bf16[120,1408]{1,0:T(8,128)(2,1)S(1)}, bf16[120,1408]{1,0:T(8,128)(2,1)}, u32[]{:S(2)}, u32[]{:S(2)}) %collective-permute-start.17) | collective-permute-done | bytes 337952 | tf_op jit(solution)/shard_map/ppermute | solution.py:34
  108.3 1.3 collective-permute-start.21
  109.8 1.0 constant_dynamic-update-slice_fusion
  111.0 0.9 fusion.71
  112.0 10.0 %collective-permute-done.22 = bf16[248,1408]{1,0:T(8,128)(2,1)S(1)} collective-permute-done((bf16[248,1408]{1,0:T(8,128)(2,1)S(1)}, bf16[248,1408]{1,0:T(8,128)(2,1)S(1)}, u32[]{:S(2)}, u32[]{:S(2)}) %collective-permute-start.22) | collective-permute-done | bytes 698400 | tf_op jit(solution)/shard_map/ppermute | solution.py:34
  122.5 2.3 %fusion.21 = bf16[240,512]{1,0:T(8,128)(2,1)} fusion(bf16[248,5632]{1,0:T(8,128)(2,1)S(1)} %add_dynamic-update-slice_fusion, bf16[1,5632,512]{2,1,0:T(8,128)(2,1)S(1)} %bitcast.88), kind=kOutput, calls=%fused_computation.22 | convolution fusion | flops 1384243200 | bytes 8716288 | tf_op jit(solution)/shard_map/dot_general | solution.py:299
  125.7 1.4 %fusion.26 = f32[120,512]{1,0:T(8,128)S(1)} fusion(bf16[1408,512]{1,0:T(8,128)(2,1)S(1)} %constant_dynamic-slice_fusion, bf16[120,1408]{1,0:T(8,128)(2,1)} %collective-permute-done.16, bf16[120,1408]{1,0:T(8,128)(2,1)} %collective-permute-done.21), kind=kOutput, calls=%fused_computation.43 | convolution fusion | flops 173184000 | bytes 2363392 | tf_op jit(solution)/shard_map/dot_general | solution.py:364
  127.2 2.1 %collective-permute-start.27 = (bf16[120,512]{1,0:T(8,128)(2,1)S(1)}, bf16[120,512]{1,0:T(8,128)(2,1)S(1)}, u32[]{:S(2)}, u32[]{:S(2)}) collective-permute-start(bf16[120,512]{1,0:T(8,128)(2,1)S(1)} %add_convert_fusion.1), channel_id=1, source_target_pairs={{0,24},{4,28},{8,16},{12,20},{16,8},{20,12},{24,0},{28,4},{1,25},{... | collective-permute-start | bytes 368648 | tf_op jit(solution)/shard_map/ppermute | solution.py:30
  130.0 0.9 collective-permute-start.26
  131.1 2.0 %collective-permute-done.27 = bf16[120,512]{1,0:T(8,128)(2,1)S(1)} collective-permute-done((bf16[120,512]{1,0:T(8,128)(2,1)S(1)}, bf16[120,512]{1,0:T(8,128)(2,1)S(1)}, u32[]{:S(2)}, u32[]{:S(2)}) %collective-permute-start.27) | collective-permute-done | bytes 122912 | tf_op jit(solution)/shard_map/ppermute | solution.py:30
  133.0 1.2 collective-permute-done.25
  135.6 1.1 collective-permute-done.28
  137.1 0.7 add_convert_fusion
  (123 shorter events, 12.5 us)
Async XLA Ops:
  1.7 14.1 %collective-permute-start = (bf16[168,512]{1,0:T(8,128)(2,1)S(1)}, bf16[168,512]{1,0:T(8,128)(2,1)S(1)}, u32[]{:S(2)}, u32[]{:S(2)}) collective-permute-start(bf16[168,512]{1,0:T(8,128)(2,1)S(1)} %pad_maximum_fusion.11.refs_0_), channel_id=1, source_target_pairs={{0,3},{1,2},{2,1},{3,0},{4,7},{5,6},{6,5},{7,4},{8,11},{9,10},{10,... | collective-permute-start | bytes 516104 | tf_op jit(solution)/shard_map/ppermute | solution.py:34
  6.8 9.2 %collective-permute-start.1 = (bf16[168,512]{1,0:T(8,128)(2,1)S(1)}, bf16[168,512]{1,0:T(8,128)(2,1)S(1)}, u32[]{:S(2)}, u32[]{:S(2)}) collective-permute-start(bf16[168,512]{1,0:T(8,128)(2,1)S(1)} %pad_maximum_fusion.11.refs_0_), channel_id=1, source_target_pairs={{0,1},{1,0},{2,3},{3,2},{4,5},{5,4},{6,7},{7,6},{8,9},{9,8},{10,11... | collective-permute-start | bytes 516104 | tf_op jit(solution)/shard_map/ppermute | solution.py:34
  6.8 14.6 %collective-permute-start.2 = (bf16[168,512]{1,0:T(8,128)(2,1)S(1)}, bf16[168,512]{1,0:T(8,128)(2,1)S(1)}, u32[]{:S(2)}, u32[]{:S(2)}) collective-permute-start(bf16[168,512]{1,0:T(8,128)(2,1)S(1)} %pad_maximum_fusion.11.refs_0_), channel_id=1, source_target_pairs={{0,2},{1,3},{2,0},{3,1},{4,6},{5,7},{6,4},{7,5},{8,10},{9,11},{10,... | collective-permute-start | bytes 516104 | tf_op jit(solution)/shard_map/ppermute | solution.py:34
  8.4 15.7 %collective-permute-start.3 = (bf16[256,512]{1,0:T(8,128)(2,1)S(1)}, bf16[256,512]{1,0:T(8,128)(2,1)S(1)}, u32[]{:S(2)}, u32[]{:S(2)}) collective-permute-start(bf16[256,512]{1,0:T(8,128)(2,1)S(1)} %bitcast.93), channel_id=1, source_target_pairs={{0,8},{4,12},{8,0},{12,4},{16,24},{20,28},{24,16},{28,20},{1,9},{5... | collective-permute-start | bytes 786440 | tf_op jit(solution)/shard_map/ppermute | solution.py:30
  10.1 14.0 %collective-permute-start.4 = (bf16[256,512]{1,0:T(8,128)(2,1)S(1)}, bf16[256,512]{1,0:T(8,128)(2,1)S(1)}, u32[]{:S(2)}, u32[]{:S(2)}) collective-permute-start(bf16[256,512]{1,0:T(8,128)(2,1)S(1)} %bitcast.94), channel_id=1, source_target_pairs={{0,16},{4,20},{8,24},{12,28},{16,0},{20,4},{24,8},{28,12},{1,17},{... | collective-permute-start | bytes 786440 | tf_op jit(solution)/shard_map/ppermute | solution.py:30
  21.4 8.3 %collective-permute-start.6 = (bf16[256,512]{1,0:T(8,128)(2,1)S(1)}, bf16[256,512]{1,0:T(8,128)(2,1)S(1)}, u32[]{:S(2)}, u32[]{:S(2)}) collective-permute-start(bf16[256,512]{1,0:T(8,128)(2,1)S(1)} %bitcast.95), channel_id=1, source_target_pairs={{0,24},{4,28},{8,16},{12,20},{16,8},{20,12},{24,0},{28,4},{1,25},{... | collective-permute-start | bytes 786440 | tf_op jit(solution)/shard_map/ppermute | solution.py:30
  24.7 2.6 %copy-start = (bf16[1,1408,2048]{2,1,0:T(8,128)(2,1)S(1)}, bf16[1,1408,2048]{2,1,0:T(8,128)(2,1)}, u32[]{:S(2)}) copy-start(bf16[1,1408,2048]{2,1,0:T(8,128)(2,1)} %param.17) | copy-start | bytes 17301508
  25.2 1.6 %collective-permute-start.10 = (bf16[64,2048]{1,0:T(8,128)(2,1)S(1)}, bf16[64,2048]{1,0:T(8,128)(2,1)S(1)}, u32[]{:S(2)}, u32[]{:S(2)}) collective-permute-start(bf16[64,2048]{1,0:T(8,128)(2,1)S(1)} %slice.134), channel_id=1, source_target_pairs={{0,4},{4,0},{8,12},{12,8},{16,20},{20,16},{24,28},{28,24},{1,5},{5... | collective-permute-start | bytes 786440 | tf_op jit(solution)/shard_map/ppermute | solution.py:30
  25.3 4.0 %collective-permute-start.5 = (bf16[3,64,2048]{2,1,0:T(8,128)(2,1)S(1)}, bf16[3,64,2048]{2,1,0:T(8,128)(2,1)S(1)}, u32[]{:S(2)}, u32[]{:S(2)}) collective-permute-start(bf16[3,64,2048]{2,1,0:T(8,128)(2,1)S(1)} %bitcast.99), channel_id=1, source_target_pairs={{0,4},{4,0},{8,12},{12,8},{16,20},{20,16},{24,28},{28,24},{1,5},{5... | collective-permute-start | bytes 2359304 | tf_op jit(solution)/shard_map/ppermute | solution.py:30
  26.8 5.9 %slice-start.2 = ((s8[5767168]{0:T(1024)(128)(4,1)}), s8[4194304]{0:T(1024)(128)(4,1)S(1)}, s32[]{:S(2)}) async-start(s8[5767168]{0:T(1024)(128)(4,1)} %bitcast.112), calls=%async_computation.2 | async-start | bytes 8388608
  27.3 5.3 %slice-start.3 = ((s8[5767168]{0:T(1024)(128)(4,1)}), s8[1572864]{0:T(1024)(128)(4,1)S(1)}, s32[]{:S(2)}) async-start(s8[5767168]{0:T(1024)(128)(4,1)} %bitcast.112), calls=%async_computation.3 | async-start | bytes 3145728
  29.6 13.4 %collective-permute-start.7 = (bf16[128,2048]{1,0:T(8,128)(2,1)S(1)}, bf16[128,2048]{1,0:T(8,128)(2,1)S(1)}, u32[]{:S(2)}, u32[]{:S(2)}) collective-permute-start(bf16[128,2048]{1,0:T(8,128)(2,1)S(1)} %pad_maximum_fusion.4), channel_id=1, source_target_pairs={{0,8},{4,12},{8,0},{12,4},{16,24},{20,28},{24,16},{28,20},{1,9},{5... | collective-permute-start | bytes 1572872 | tf_op jit(solution)/shard_map/ppermute | solution.py:30
  31.1 12.2 %collective-permute-start.8 = (bf16[128,2048]{1,0:T(8,128)(2,1)S(1)}, bf16[128,2048]{1,0:T(8,128)(2,1)S(1)}, u32[]{:S(2)}, u32[]{:S(2)}) collective-permute-start(bf16[128,2048]{1,0:T(8,128)(2,1)S(1)} %pad_maximum_fusion.5), channel_id=1, source_target_pairs={{0,16},{4,20},{8,24},{12,28},{16,0},{20,4},{24,8},{28,12},{1,17},{... | collective-permute-start | bytes 1572872 | tf_op jit(solution)/shard_map/ppermute | solution.py:30
  34.6 12.7 %collective-permute-start.11 = (bf16[120,1408]{1,0:T(8,128)(2,1)S(1)}, bf16[120,1408]{1,0:T(8,128)(2,1)S(1)}, u32[]{:S(2)}, u32[]{:S(2)}) collective-permute-start(bf16[120,1408]{1,0:T(8,128)(2,1)S(1)} %fusion.17), channel_id=1, source_target_pairs={{0,3},{1,2},{2,1},{3,0},{4,7},{5,6},{6,5},{7,4},{8,11},{9,10},{10,... | collective-permute-start | bytes 1013768 | tf_op jit(solution)/shard_map/ppermute | solution.py:34
  37.0 15.6 %collective-permute-start.13 = (bf16[120,1408]{1,0:T(8,128)(2,1)S(1)}, bf16[120,1408]{1,0:T(8,128)(2,1)S(1)}, u32[]{:S(2)}, u32[]{:S(2)}) collective-permute-start(bf16[120,1408]{1,0:T(8,128)(2,1)S(1)} %fusion.17), channel_id=1, source_target_pairs={{0,1},{1,0},{2,3},{3,2},{4,5},{5,4},{6,7},{7,6},{8,9},{9,8},{10,11... | collective-permute-start | bytes 1013768 | tf_op jit(solution)/shard_map/ppermute | solution.py:34
  37.0 27.7 %collective-permute-start.14 = (bf16[120,1408]{1,0:T(8,128)(2,1)S(1)}, bf16[120,1408]{1,0:T(8,128)(2,1)S(1)}, u32[]{:S(2)}, u32[]{:S(2)}) collective-permute-start(bf16[120,1408]{1,0:T(8,128)(2,1)S(1)} %fusion.17), channel_id=1, source_target_pairs={{0,2},{3,1},{4,6},{7,5},{8,10},{11,9},{12,14},{15,13},{16,18},{19,... | collective-permute-start | bytes 1013768 | tf_op jit(solution)/shard_map/ppermute | solution.py:34
  43.5 2.7 %collective-permute-start.12 = (bf16[4,256,512]{2,1,0:T(8,128)(2,1)S(1)}, bf16[4,256,512]{2,1,0:T(8,128)(2,1)S(1)}, u32[]{:S(2)}, u32[]{:S(2)}) collective-permute-start(bf16[4,256,512]{2,1,0:T(8,128)(2,1)S(1)} %get-tuple-element.126), channel_id=1, source_target_pairs={{0,4},{4,0},{8,12},{12,8},{16,20},{20,16},{24,28},{28,24},{1,5},{5... | collective-permute-start | bytes 3145736 | tf_op jit(solution)/shard_map/ppermute | solution.py:30
  43.6 18.0 %collective-permute-start.9 = (bf16[128,2048]{1,0:T(8,128)(2,1)S(1)}, bf16[128,2048]{1,0:T(8,128)(2,1)S(1)}, u32[]{:S(2)}, u32[]{:S(2)}) collective-permute-start(bf16[128,2048]{1,0:T(8,128)(2,1)S(1)} %pad_maximum_fusion.6), channel_id=1, source_target_pairs={{0,24},{4,28},{8,16},{12,20},{16,8},{20,12},{24,0},{28,4},{1,25},{... | collective-permute-start | bytes 1572872 | tf_op jit(solution)/shard_map/ppermute | solution.py:30
  47.4 17.4 %collective-permute-start.15 = (bf16[120,1408]{1,0:T(8,128)(2,1)S(1)}, bf16[120,1408]{1,0:T(8,128)(2,1)S(1)}, u32[]{:S(2)}, u32[]{:S(2)}) collective-permute-start(bf16[120,1408]{1,0:T(8,128)(2,1)S(1)} %collective-permute-done.11), channel_id=1, source_target_pairs={{1,0},{2,3},{5,4},{6,7},{9,8},{10,11},{13,12},{14,15},{17,16},{18,... | collective-permute-start | bytes 1013768 | tf_op jit(solution)/shard_map/ppermute | solution.py:34
  56.5 15.3 %collective-permute-start.20 = (bf16[248,1408]{1,0:T(8,128)(2,1)S(1)}, bf16[248,1408]{1,0:T(8,128)(2,1)S(1)}, u32[]{:S(2)}, u32[]{:S(2)}) collective-permute-start(bf16[248,1408]{1,0:T(8,128)(2,1)S(1)} %pad_maximum_fusion.3), channel_id=1, source_target_pairs={{1,2},{2,1},{5,6},{6,5},{9,10},{10,9},{13,14},{14,13},{17,18},{18,... | collective-permute-start | bytes 2095112 | tf_op jit(solution)/shard_map/ppermute | solution.py:34
  57.2 37.1 %collective-permute-start.19 = (bf16[248,1408]{1,0:T(8,128)(2,1)S(1)}, bf16[248,1408]{1,0:T(8,128)(2,1)S(1)}, u32[]{:S(2)}, u32[]{:S(2)}) collective-permute-start(bf16[248,1408]{1,0:T(8,128)(2,1)S(1)} %pad_maximum_fusion.3), channel_id=1, source_target_pairs={{0,1},{1,0},{2,3},{3,2},{4,5},{5,4},{6,7},{7,6},{8,9},{9,8},{10,11... | collective-permute-start | bytes 2095112 | tf_op jit(solution)/shard_map/ppermute | solution.py:34
  61.6 34.0 %collective-permute-start.18 = (bf16[248,1408]{1,0:T(8,128)(2,1)S(1)}, bf16[248,1408]{1,0:T(8,128)(2,1)S(1)}, u32[]{:S(2)}, u32[]{:S(2)}) collective-permute-start(bf16[248,1408]{1,0:T(8,128)(2,1)S(1)} %pad_maximum_fusion.3), channel_id=1, source_target_pairs={{0,2},{3,1},{4,6},{7,5},{8,10},{11,9},{12,14},{15,13},{16,18},{19,... | collective-permute-start | bytes 2095112 | tf_op jit(solution)/shard_map/ppermute | solution.py:34
  64.7 5.8 %slice-start = ((s8[5767168]{0:T(1024)(128)(4,1)}), s8[4194304]{0:T(1024)(128)(4,1)S(1)}, s32[]{:S(2)}) async-start(s8[5767168]{0:T(1024)(128)(4,1)} %bitcast.87), calls=%async_computation | async-start | bytes 8388608
  66.7 3.9 %slice-start.1 = ((s8[5767168]{0:T(1024)(128)(4,1)}), s8[1572864]{0:T(1024)(128)(4,1)S(1)}, s32[]{:S(2)}) async-start(s8[5767168]{0:T(1024)(128)(4,1)} %bitcast.87), calls=%async_computation.1 | async-start | bytes 3145728
  68.7 41.1 %collective-permute-start.24 = (bf16[120,1408]{1,0:T(8,128)(2,1)S(1)}, bf16[120,1408]{1,0:T(8,128)(2,1)S(1)}, u32[]{:S(2)}, u32[]{:S(2)}) collective-permute-start(bf16[120,1408]{1,0:T(8,128)(2,1)S(1)} %multiply_convert_fusion.1), channel_id=1, source_target_pairs={{0,1},{1,0},{2,3},{3,2},{4,5},{5,4},{6,7},{7,6},{8,9},{9,8},{10,11... | collective-permute-start | bytes 1013768 | tf_op jit(solution)/shard_map/ppermute | solution.py:34
  68.7 39.6 %collective-permute-start.17 = (bf16[120,1408]{1,0:T(8,128)(2,1)S(1)}, bf16[120,1408]{1,0:T(8,128)(2,1)}, u32[]{:S(2)}, u32[]{:S(2)}) collective-permute-start(bf16[120,1408]{1,0:T(8,128)(2,1)S(1)} %multiply_convert_fusion.1), channel_id=1, source_target_pairs={{0,3},{1,2},{2,1},{3,0},{4,7},{5,6},{6,5},{7,4},{8,11},{9,10},{10,... | collective-permute-start | bytes 1013768 | tf_op jit(solution)/shard_map/ppermute | solution.py:34
  71.8 53.4 %collective-permute-start.16 = (bf16[120,1408]{1,0:T(8,128)(2,1)S(1)}, bf16[120,1408]{1,0:T(8,128)(2,1)}, u32[]{:S(2)}, u32[]{:S(2)}) collective-permute-start(bf16[120,1408]{1,0:T(8,128)(2,1)S(1)} %multiply_convert_fusion.1), channel_id=1, source_target_pairs={{0,2},{3,1},{4,6},{7,5},{8,10},{11,9},{12,14},{15,13},{16,18},{19,... | collective-permute-start | bytes 1013768 | tf_op jit(solution)/shard_map/ppermute | solution.py:34
  94.3 27.9 %collective-permute-start.23 = (bf16[248,1408]{1,0:T(8,128)(2,1)S(1)}, bf16[248,1408]{1,0:T(8,128)(2,1)S(1)}, u32[]{:S(2)}, u32[]{:S(2)}) collective-permute-start(bf16[248,1408]{1,0:T(8,128)(2,1)S(1)} %collective-permute-done.20), channel_id=1, source_target_pairs={{1,0},{2,3},{5,4},{6,7},{9,8},{10,11},{13,12},{14,15},{17,16},{18,... | collective-permute-start | bytes 2095112 | tf_op jit(solution)/shard_map/ppermute | solution.py:34
  95.6 26.4 %collective-permute-start.22 = (bf16[248,1408]{1,0:T(8,128)(2,1)S(1)}, bf16[248,1408]{1,0:T(8,128)(2,1)S(1)}, u32[]{:S(2)}, u32[]{:S(2)}) collective-permute-start(bf16[248,1408]{1,0:T(8,128)(2,1)S(1)} %collective-permute-done.18), channel_id=1, source_target_pairs={{1,0},{2,3},{5,4},{6,7},{9,8},{10,11},{13,12},{14,15},{17,16},{18,... | collective-permute-start | bytes 2095112 | tf_op jit(solution)/shard_map/ppermute | solution.py:34
  108.3 17.4 %collective-permute-start.21 = (bf16[120,1408]{1,0:T(8,128)(2,1)}, bf16[120,1408]{1,0:T(8,128)(2,1)}, u32[]{:S(2)}, u32[]{:S(2)}) collective-permute-start(bf16[120,1408]{1,0:T(8,128)(2,1)} %collective-permute-done.17), channel_id=1, source_target_pairs={{1,0},{2,3},{5,4},{6,7},{9,8},{10,11},{13,12},{14,15},{17,16},{18,... | collective-permute-start | bytes 1013768 | tf_op jit(solution)/shard_map/ppermute | solution.py:34
  124.9 4.5 %copy-start.1 = (bf16[240,512]{1,0:T(8,128)(2,1)S(1)}, bf16[240,512]{1,0:T(8,128)(2,1)}, u32[]{:S(2)}) copy-start(bf16[240,512]{1,0:T(8,128)(2,1)} %fusion.21) | copy-start | bytes 737284
  125.2 5.7 %copy-start.2 = (f32[160,2]{0,1:T(2,128)S(1)}, f32[160,2]{0,1:T(2,128)}, u32[]{:S(2)}) copy-start(f32[160,2]{0,1:T(2,128)} %param.16) | copy-start | bytes 3844
  127.2 5.8 %collective-permute-start.27 = (bf16[120,512]{1,0:T(8,128)(2,1)S(1)}, bf16[120,512]{1,0:T(8,128)(2,1)S(1)}, u32[]{:S(2)}, u32[]{:S(2)}) collective-permute-start(bf16[120,512]{1,0:T(8,128)(2,1)S(1)} %add_convert_fusion.1), channel_id=1, source_target_pairs={{0,24},{4,28},{8,16},{12,20},{16,8},{20,12},{24,0},{28,4},{1,25},{... | collective-permute-start | bytes 368648 | tf_op jit(solution)/shard_map/ppermute | solution.py:30
  129.3 4.9 %collective-permute-start.25 = (bf16[120,512]{1,0:T(8,128)(2,1)S(1)}, bf16[120,512]{1,0:T(8,128)(2,1)S(1)}, u32[]{:S(2)}, u32[]{:S(2)}) collective-permute-start(bf16[120,512]{1,0:T(8,128)(2,1)S(1)} %get-tuple-element.141), channel_id=1, source_target_pairs={{0,8},{4,12},{8,0},{12,4},{16,24},{20,28},{24,16},{28,20},{1,9},{5... | collective-permute-start | bytes 368648 | tf_op jit(solution)/shard_map/ppermute | solution.py:30
  130.0 4.9 %collective-permute-start.26 = (bf16[120,512]{1,0:T(8,128)(2,1)S(1)}, bf16[120,512]{1,0:T(8,128)(2,1)S(1)}, u32[]{:S(2)}, u32[]{:S(2)}) collective-permute-start(bf16[120,512]{1,0:T(8,128)(2,1)S(1)} %get-tuple-element.142), channel_id=1, source_target_pairs={{0,16},{4,20},{8,24},{12,28},{16,0},{20,4},{24,8},{28,12},{1,17},{... | collective-permute-start | bytes 368648 | tf_op jit(solution)/shard_map/ppermute | solution.py:30
  135.1 1.6 %collective-permute-start.28 = (bf16[4,60,512]{2,1,0:T(8,128)(2,1)S(1)}, bf16[4,60,512]{2,1,0:T(8,128)(2,1)S(1)}, u32[]{:S(2)}, u32[]{:S(2)}) collective-permute-start(bf16[4,60,512]{2,1,0:T(8,128)(2,1)S(1)} %get-tuple-element.140), channel_id=1, source_target_pairs={{0,4},{4,0},{8,12},{12,8},{16,20},{20,16},{24,28},{28,24},{1,5},{5... | collective-permute-start | bytes 737288 | tf_op jit(solution)/shard_map/ppermute | solution.py:30

commit v7 on v6

--- a/solution.py
+++ b/solution.py
@@ -226,7 +226,7 @@
         pairs[1], pairs[2], by_chip[-1] = tie(pairs[1], pairs[2], by_chip[-1])
     for offset in range(1, chips):
         if offset == chips - 1:
-            pairs[1:] = tie(*pairs[1:])
+            pairs[1], pairs[-1] = tie(pairs[1], pairs[-1])
         pairs[offset] = row_xor(pairs[offset], 2 * offset)
 
     def hidden_of(offsets, earlier):

time: 138 us -> 138 us (level)
  no operation moved by 1% of the time
where the time goes in v7:
time: 138 us
  starting transfers between devices  64 us (46%)
  waiting for transfers between devices  40.8 us (30%)
  matrix products  19.9 us (14%)
  other arithmetic  7.08 us (5%)
  local copies, waits for them, and re-layouts  4.9 us (4%)
    ppermute x16, starting transfers between devices, along(): return lax.ppermute(value, 'col', pairs)  49.5 us
    ppermute x16, waiting for transfers between devices, along(): return lax.ppermute(value, 'col', pairs)  31.7 us
    ppermute x13, starting transfers between devices, row_xor(): lax.ppermute(value, 'row', [(i, i ^ by) for i in range(lax.axis_size('row...  14.6 us
    dot_general x7, matrix products, contract_last(): lax.dot_general(left, right, (((1,), (1,)), ((), ())), preferred_element_...  12.1 us
    ppermute x13, waiting for transfers between devices, row_xor(): lax.ppermute(value, 'row', [(i, i ^ by) for i in range(lax.axis_size('row...  9.12 us
    dot_general x3, matrix products, block_sum(): return jnp.dot(whole, unit_down, preferred_element_type=jnp.float32)  4.14 us
  transfers between devices with their start and end apart: 29, of which 16 were waited for; matrix products, arithmetic and copies ran while one was open for 20% of the time, Pallas kernels for 0%

profile of v7, /device:TPU:0, one launch (start us, length us, event | category | flops | bytes accessed | tf_op | source)
XLA Modules:
  0.0 137.9 jit_solution(10384886612756916854)
XLA Ops:
  0.7 0.9 pad_maximum_fusion.11.refs_0_
  1.7 5.1 %collective-permute-start = (bf16[168,512]{1,0:T(8,128)(2,1)S(1)}, bf16[168,512]{1,0:T(8,128)(2,1)S(1)}, u32[]{:S(2)}, u32[]{:S(2)}) collective-permute-start(bf16[168,512]{1,0:T(8,128)(2,1)S(1)} %pad_maximum_fusion.11.refs_0_), channel_id=1, source_target_pairs={{0,3},{1,2},{2,1},{3,0},{4,7},{5,6},{6,5},{7,4},{8,11},{9,10},{10,... | collective-permute-start | bytes 516104 | tf_op jit(solution)/shard_map/ppermute | solution.py:34
  7.4 1.0 pad_maximum_fusion.10
  8.4 1.7 %collective-permute-start.3 = (bf16[256,512]{1,0:T(8,128)(2,1)S(1)}, bf16[256,512]{1,0:T(8,128)(2,1)S(1)}, u32[]{:S(2)}, u32[]{:S(2)}) collective-permute-start(bf16[256,512]{1,0:T(8,128)(2,1)S(1)} %bitcast.93), channel_id=1, source_target_pairs={{0,8},{4,12},{8,0},{12,4},{16,24},{20,28},{24,16},{28,20},{1,9},{5... | collective-permute-start | bytes 786440 | tf_op jit(solution)/shard_map/ppermute | solution.py:30
  10.1 1.5 %collective-permute-start.4 = (bf16[256,512]{1,0:T(8,128)(2,1)S(1)}, bf16[256,512]{1,0:T(8,128)(2,1)S(1)}, u32[]{:S(2)}, u32[]{:S(2)}) collective-permute-start(bf16[256,512]{1,0:T(8,128)(2,1)S(1)} %bitcast.94), channel_id=1, source_target_pairs={{0,16},{4,20},{8,24},{12,28},{16,0},{20,4},{24,8},{28,12},{1,17},{... | collective-permute-start | bytes 786440 | tf_op jit(solution)/shard_map/ppermute | solution.py:30
  11.6 0.8 copy.29
  13.0 0.7 multiply_add_fusion
  13.7 0.7 copy.31
  14.7 0.7 select_reduce_fusion.2
  15.9 5.4 %collective-permute-done.2.refs_3_ = bf16[168,512]{1,0:T(8,128)(2,1)S(1)} collective-permute-done((bf16[168,512]{1,0:T(8,128)(2,1)S(1)}, bf16[168,512]{1,0:T(8,128)(2,1)S(1)}, u32[]{:S(2)}, u32[]{:S(2)}) %collective-permute-start.2) | collective-permute-done | bytes 172064 | tf_op jit(solution)/shard_map/ppermute | solution.py:34
  21.4 2.4 %collective-permute-start.6 = (bf16[256,512]{1,0:T(8,128)(2,1)S(1)}, bf16[256,512]{1,0:T(8,128)(2,1)S(1)}, u32[]{:S(2)}, u32[]{:S(2)}) collective-permute-start(bf16[256,512]{1,0:T(8,128)(2,1)S(1)} %bitcast.95), channel_id=1, source_target_pairs={{0,24},{4,28},{8,16},{12,20},{16,8},{20,12},{24,0},{28,4},{1,25},{... | collective-permute-start | bytes 786440 | tf_op jit(solution)/shard_map/ppermute | solution.py:30
  25.9 0.9 collective-permute-done.9
  27.3 1.9 %fusion.10 = f32[120,1408]{1,0:T(8,128)S(1)} fusion(bf16[120,2048]{1,0:T(8,128)(2,1)S(1)} %pad_maximum_fusion.7, bf16[1,1408,2048]{2,1,0:T(8,128)(2,1)S(1)} %copy-done), kind=kOutput, calls=%fused_computation.10 | convolution fusion | flops 692060160 | bytes 6934528 | tf_op jit(solution)/shard_map/dot_general | solution.py:19
  29.6 1.5 %collective-permute-start.7 = (bf16[128,2048]{1,0:T(8,128)(2,1)S(1)}, bf16[128,2048]{1,0:T(8,128)(2,1)S(1)}, u32[]{:S(2)}, u32[]{:S(2)}) collective-permute-start(bf16[128,2048]{1,0:T(8,128)(2,1)S(1)} %pad_maximum_fusion.4), channel_id=1, source_target_pairs={{0,8},{4,12},{8,0},{12,4},{16,24},{20,28},{24,16},{28,20},{1,9},{5... | collective-permute-start | bytes 1572872 | tf_op jit(solution)/shard_map/ppermute | solution.py:30
  31.1 1.5 %collective-permute-start.10 = (bf16[128,2048]{1,0:T(8,128)(2,1)S(1)}, bf16[128,2048]{1,0:T(8,128)(2,1)S(1)}, u32[]{:S(2)}, u32[]{:S(2)}) collective-permute-start(bf16[128,2048]{1,0:T(8,128)(2,1)S(1)} %pad_maximum_fusion.5), channel_id=1, source_target_pairs={{0,16},{4,20},{8,24},{12,28},{16,0},{20,4},{24,8},{28,12},{1,17},{... | collective-permute-start | bytes 1572872 | tf_op jit(solution)/shard_map/ppermute | solution.py:30
  32.6 2.0 %fusion.17 = bf16[120,1408]{1,0:T(8,128)(2,1)S(1)} fusion(bf16[120,2048]{1,0:T(8,128)(2,1)S(1)} %pad_maximum_fusion.7, bf16[1,1408,2048]{2,1,0:T(8,128)(2,1)S(1)} %bitcast.113, f32[120,1408]{1,0:T(8,128)S(1)} %fusion.10), kind=kOutput, calls=%fused_computation.17 | convolution fusion | flops 693073920 | bytes 7272448 | tf_op jit(solution)/shard_map/dot_general | solution.py:19
  34.6 2.4 %collective-permute-start.11 = (bf16[120,1408]{1,0:T(8,128)(2,1)S(1)}, bf16[120,1408]{1,0:T(8,128)(2,1)S(1)}, u32[]{:S(2)}, u32[]{:S(2)}) collective-permute-start(bf16[120,1408]{1,0:T(8,128)(2,1)S(1)} %fusion.17), channel_id=1, source_target_pairs={{0,3},{1,2},{2,1},{3,0},{4,7},{5,6},{6,5},{7,4},{8,11},{9,10},{10,... | collective-permute-start | bytes 1013768 | tf_op jit(solution)/shard_map/ppermute | solution.py:34
  37.0 4.0 %collective-permute-start.14 = (bf16[120,1408]{1,0:T(8,128)(2,1)S(1)}, bf16[120,1408]{1,0:T(8,128)(2,1)S(1)}, u32[]{:S(2)}, u32[]{:S(2)}) collective-permute-start(bf16[120,1408]{1,0:T(8,128)(2,1)S(1)} %fusion.17), channel_id=1, source_target_pairs={{0,2},{3,1},{4,6},{7,5},{8,10},{11,9},{12,14},{15,13},{16,18},{19,... | collective-permute-start | bytes 1013768 | tf_op jit(solution)/shard_map/ppermute | solution.py:34
  41.0 2.0 %collective-permute-done.7 = bf16[128,2048]{1,0:T(8,128)(2,1)S(1)} collective-permute-done((bf16[128,2048]{1,0:T(8,128)(2,1)S(1)}, bf16[128,2048]{1,0:T(8,128)(2,1)S(1)}, u32[]{:S(2)}, u32[]{:S(2)}) %collective-permute-start.7) | collective-permute-done | bytes 524320 | tf_op jit(solution)/shard_map/ppermute | solution.py:30
  43.6 1.5 %collective-permute-start.8 = (bf16[128,2048]{1,0:T(8,128)(2,1)S(1)}, bf16[128,2048]{1,0:T(8,128)(2,1)S(1)}, u32[]{:S(2)}, u32[]{:S(2)}) collective-permute-start(bf16[128,2048]{1,0:T(8,128)(2,1)S(1)} %pad_maximum_fusion.6), channel_id=1, source_target_pairs={{0,24},{4,28},{8,16},{12,20},{16,8},{20,12},{24,0},{28,4},{1,25},{... | collective-permute-start | bytes 1572872 | tf_op jit(solution)/shard_map/ppermute | solution.py:30
  45.5 0.7 collective-permute-done.12
  47.4 1.3 collective-permute-start.15
  48.6 4.0 %collective-permute-done.13 = bf16[120,1408]{1,0:T(8,128)(2,1)S(1)} collective-permute-done((bf16[120,1408]{1,0:T(8,128)(2,1)S(1)}, bf16[120,1408]{1,0:T(8,128)(2,1)S(1)}, u32[]{:S(2)}, u32[]{:S(2)}) %collective-permute-start.13) | collective-permute-done | bytes 337952 | tf_op jit(solution)/shard_map/ppermute | solution.py:34
  52.6 1.8 %fusion.8 = f32[240,1408]{1,0:T(8,128)S(1)} fusion(bf16[240,2048]{1,0:T(8,128)(2,1)S(1)} %pad_maximum_fusion.2, bf16[1,1408,2048]{2,1,0:T(8,128)(2,1)S(1)} %copy-done), kind=kOutput, calls=%fused_computation.8 | convolution fusion | flops 1384120320 | bytes 8101888 | tf_op jit(solution)/shard_map/dot_general | solution.py:19
  54.4 2.0 %multiply_convert_fusion = bf16[240,1408]{1,0:T(8,128)(2,1)S(1)} fusion(f32[240,1408]{1,0:T(8,128)S(1)} %fusion.8, bf16[240,2048]{1,0:T(8,128)(2,1)S(1)} %pad_maximum_fusion.2, bf16[1,1408,2048]{2,1,0:T(8,128)(2,1)S(1)} %bitcast.113), kind=kOutput, calls=%fused_computation.20 | convolution fusion | flops 1386147840 | bytes 8777728 | tf_op jit(solution)/shard_map/dot_general | solution.py:19
  56.5 0.7 collective-permute-start.20
  57.2 4.4 %collective-permute-start.19 = (bf16[248,1408]{1,0:T(8,128)(2,1)S(1)}, bf16[248,1408]{1,0:T(8,128)(2,1)S(1)}, u32[]{:S(2)}, u32[]{:S(2)}) collective-permute-start(bf16[248,1408]{1,0:T(8,128)(2,1)S(1)} %pad_maximum_fusion.3), channel_id=1, source_target_pairs={{0,1},{1,0},{2,3},{3,2},{4,5},{5,4},{6,7},{7,6},{8,9},{9,8},{10,11... | collective-permute-start | bytes 2095112 | tf_op jit(solution)/shard_map/ppermute | solution.py:34
  61.6 3.0 %collective-permute-start.18 = (bf16[248,1408]{1,0:T(8,128)(2,1)S(1)}, bf16[248,1408]{1,0:T(8,128)(2,1)S(1)}, u32[]{:S(2)}, u32[]{:S(2)}) collective-permute-start(bf16[248,1408]{1,0:T(8,128)(2,1)S(1)} %pad_maximum_fusion.3), channel_id=1, source_target_pairs={{0,2},{3,1},{4,6},{7,5},{8,10},{11,9},{12,14},{15,13},{16,18},{19,... | collective-permute-start | bytes 2095112 | tf_op jit(solution)/shard_map/ppermute | solution.py:34
  64.7 1.9 %fusion.6 = f32[120,1408]{1,0:T(8,128)S(1)} fusion(bf16[120,2048]{1,0:T(8,128)(2,1)S(1)} %pad_maximum_fusion.8, bf16[1,1408,2048]{2,1,0:T(8,128)(2,1)S(1)} %copy-done), kind=kOutput, calls=%fused_computation.6 | convolution fusion | flops 692060160 | bytes 6934528 | tf_op jit(solution)/shard_map/dot_general | solution.py:19
  66.7 2.0 %multiply_convert_fusion.1 = bf16[120,1408]{1,0:T(8,128)(2,1)S(1)} fusion(f32[120,1408]{1,0:T(8,128)S(1)} %fusion.6, bf16[120,2048]{1,0:T(8,128)(2,1)S(1)} %pad_maximum_fusion.8, bf16[1,1408,2048]{2,1,0:T(8,128)(2,1)S(1)} %bitcast.113), kind=kOutput, calls=%fused_computation.34 | convolution fusion | flops 693073920 | bytes 7272448 | tf_op jit(solution)/shard_map/dot_general | solution.py:19
  68.7 1.6 %collective-permute-start.17 = (bf16[120,1408]{1,0:T(8,128)(2,1)S(1)}, bf16[120,1408]{1,0:T(8,128)(2,1)}, u32[]{:S(2)}, u32[]{:S(2)}) collective-permute-start(bf16[120,1408]{1,0:T(8,128)(2,1)S(1)} %multiply_convert_fusion.1), channel_id=1, source_target_pairs={{0,3},{1,2},{2,1},{3,0},{4,7},{5,6},{6,5},{7,4},{8,11},{9,10},{10,... | collective-permute-start | bytes 1013768 | tf_op jit(solution)/shard_map/ppermute | solution.py:34
  70.6 0.9 convolution_convert_fusion.2
  71.8 22.5 %collective-permute-start.16 = (bf16[120,1408]{1,0:T(8,128)(2,1)S(1)}, bf16[120,1408]{1,0:T(8,128)(2,1)}, u32[]{:S(2)}, u32[]{:S(2)}) collective-permute-start(bf16[120,1408]{1,0:T(8,128)(2,1)S(1)} %multiply_convert_fusion.1), channel_id=1, source_target_pairs={{0,2},{3,1},{4,6},{7,5},{8,10},{11,9},{12,14},{15,13},{16,18},{19,... | collective-permute-start | bytes 1013768 | tf_op jit(solution)/shard_map/ppermute | solution.py:34
  94.3 1.3 collective-permute-start.23
  95.6 1.3 collective-permute-start.22
  96.9 11.4 %collective-permute-done.17 = bf16[120,1408]{1,0:T(8,128)(2,1)} collective-permute-done((bf16[120,1408]{1,0:T(8,128)(2,1)S(1)}, bf16[120,1408]{1,0:T(8,128)(2,1)}, u32[]{:S(2)}, u32[]{:S(2)}) %collective-permute-start.17) | collective-permute-done | bytes 337952 | tf_op jit(solution)/shard_map/ppermute | solution.py:34
  108.3 1.3 collective-permute-start.21
  109.8 1.0 constant_dynamic-update-slice_fusion
  111.0 0.9 fusion.71
  112.0 10.0 %collective-permute-done.22 = bf16[248,1408]{1,0:T(8,128)(2,1)S(1)} collective-permute-done((bf16[248,1408]{1,0:T(8,128)(2,1)S(1)}, bf16[248,1408]{1,0:T(8,128)(2,1)S(1)}, u32[]{:S(2)}, u32[]{:S(2)}) %collective-permute-start.22) | collective-permute-done | bytes 698400 | tf_op jit(solution)/shard_map/ppermute | solution.py:34
  122.5 2.3 %fusion.21 = bf16[240,512]{1,0:T(8,128)(2,1)} fusion(bf16[248,5632]{1,0:T(8,128)(2,1)S(1)} %add_dynamic-update-slice_fusion, bf16[1,5632,512]{2,1,0:T(8,128)(2,1)S(1)} %bitcast.88), kind=kOutput, calls=%fused_computation.22 | convolution fusion | flops 1384243200 | bytes 8716288 | tf_op jit(solution)/shard_map/dot_general | solution.py:299
  125.7 1.4 %fusion.26 = f32[120,512]{1,0:T(8,128)S(1)} fusion(bf16[1408,512]{1,0:T(8,128)(2,1)S(1)} %constant_dynamic-slice_fusion, bf16[120,1408]{1,0:T(8,128)(2,1)} %collective-permute-done.16, bf16[120,1408]{1,0:T(8,128)(2,1)} %collective-permute-done.21), kind=kOutput, calls=%fused_computation.43 | convolution fusion | flops 173184000 | bytes 2363392 | tf_op jit(solution)/shard_map/dot_general | solution.py:364
  127.2 2.1 %collective-permute-start.27 = (bf16[120,512]{1,0:T(8,128)(2,1)S(1)}, bf16[120,512]{1,0:T(8,128)(2,1)S(1)}, u32[]{:S(2)}, u32[]{:S(2)}) collective-permute-start(bf16[120,512]{1,0:T(8,128)(2,1)S(1)} %add_convert_fusion.1), channel_id=1, source_target_pairs={{0,24},{4,28},{8,16},{12,20},{16,8},{20,12},{24,0},{28,4},{1,25},{... | collective-permute-start | bytes 368648 | tf_op jit(solution)/shard_map/ppermute | solution.py:30
  130.0 0.9 collective-permute-start.26
  131.1 2.0 %collective-permute-done.27 = bf16[120,512]{1,0:T(8,128)(2,1)S(1)} collective-permute-done((bf16[120,512]{1,0:T(8,128)(2,1)S(1)}, bf16[120,512]{1,0:T(8,128)(2,1)S(1)}, u32[]{:S(2)}, u32[]{:S(2)}) %collective-permute-start.27) | collective-permute-done | bytes 122912 | tf_op jit(solution)/shard_map/ppermute | solution.py:30
  133.0 1.2 collective-permute-done.25
  135.6 1.1 collective-permute-done.28
  137.1 0.7 add_convert_fusion
  (123 shorter events, 12.5 us)
Async XLA Ops:
  1.7 14.1 %collective-permute-start = (bf16[168,512]{1,0:T(8,128)(2,1)S(1)}, bf16[168,512]{1,0:T(8,128)(2,1)S(1)}, u32[]{:S(2)}, u32[]{:S(2)}) collective-permute-start(bf16[168,512]{1,0:T(8,128)(2,1)S(1)} %pad_maximum_fusion.11.refs_0_), channel_id=1, source_target_pairs={{0,3},{1,2},{2,1},{3,0},{4,7},{5,6},{6,5},{7,4},{8,11},{9,10},{10,... | collective-permute-start | bytes 516104 | tf_op jit(solution)/shard_map/ppermute | solution.py:34
  6.8 9.2 %collective-permute-start.1 = (bf16[168,512]{1,0:T(8,128)(2,1)S(1)}, bf16[168,512]{1,0:T(8,128)(2,1)S(1)}, u32[]{:S(2)}, u32[]{:S(2)}) collective-permute-start(bf16[168,512]{1,0:T(8,128)(2,1)S(1)} %pad_maximum_fusion.11.refs_0_), channel_id=1, source_target_pairs={{0,1},{1,0},{2,3},{3,2},{4,5},{5,4},{6,7},{7,6},{8,9},{9,8},{10,11... | collective-permute-start | bytes 516104 | tf_op jit(solution)/shard_map/ppermute | solution.py:34
  6.8 14.6 %collective-permute-start.2 = (bf16[168,512]{1,0:T(8,128)(2,1)S(1)}, bf16[168,512]{1,0:T(8,128)(2,1)S(1)}, u32[]{:S(2)}, u32[]{:S(2)}) collective-permute-start(bf16[168,512]{1,0:T(8,128)(2,1)S(1)} %pad_maximum_fusion.11.refs_0_), channel_id=1, source_target_pairs={{0,2},{1,3},{2,0},{3,1},{4,6},{5,7},{6,4},{7,5},{8,10},{9,11},{10,... | collective-permute-start | bytes 516104 | tf_op jit(solution)/shard_map/ppermute | solution.py:34
  8.4 15.7 %collective-permute-start.3 = (bf16[256,512]{1,0:T(8,128)(2,1)S(1)}, bf16[256,512]{1,0:T(8,128)(2,1)S(1)}, u32[]{:S(2)}, u32[]{:S(2)}) collective-permute-start(bf16[256,512]{1,0:T(8,128)(2,1)S(1)} %bitcast.93), channel_id=1, source_target_pairs={{0,8},{4,12},{8,0},{12,4},{16,24},{20,28},{24,16},{28,20},{1,9},{5... | collective-permute-start | bytes 786440 | tf_op jit(solution)/shard_map/ppermute | solution.py:30
  10.1 14.0 %collective-permute-start.4 = (bf16[256,512]{1,0:T(8,128)(2,1)S(1)}, bf16[256,512]{1,0:T(8,128)(2,1)S(1)}, u32[]{:S(2)}, u32[]{:S(2)}) collective-permute-start(bf16[256,512]{1,0:T(8,128)(2,1)S(1)} %bitcast.94), channel_id=1, source_target_pairs={{0,16},{4,20},{8,24},{12,28},{16,0},{20,4},{24,8},{28,12},{1,17},{... | collective-permute-start | bytes 786440 | tf_op jit(solution)/shard_map/ppermute | solution.py:30
  21.4 8.3 %collective-permute-start.6 = (bf16[256,512]{1,0:T(8,128)(2,1)S(1)}, bf16[256,512]{1,0:T(8,128)(2,1)S(1)}, u32[]{:S(2)}, u32[]{:S(2)}) collective-permute-start(bf16[256,512]{1,0:T(8,128)(2,1)S(1)} %bitcast.95), channel_id=1, source_target_pairs={{0,24},{4,28},{8,16},{12,20},{16,8},{20,12},{24,0},{28,4},{1,25},{... | collective-permute-start | bytes 786440 | tf_op jit(solution)/shard_map/ppermute | solution.py:30
  24.7 2.6 %copy-start = (bf16[1,1408,2048]{2,1,0:T(8,128)(2,1)S(1)}, bf16[1,1408,2048]{2,1,0:T(8,128)(2,1)}, u32[]{:S(2)}) copy-start(bf16[1,1408,2048]{2,1,0:T(8,128)(2,1)} %param.17) | copy-start | bytes 17301508
  25.2 1.6 %collective-permute-start.9 = (bf16[64,2048]{1,0:T(8,128)(2,1)S(1)}, bf16[64,2048]{1,0:T(8,128)(2,1)S(1)}, u32[]{:S(2)}, u32[]{:S(2)}) collective-permute-start(bf16[64,2048]{1,0:T(8,128)(2,1)S(1)} %slice.134), channel_id=1, source_target_pairs={{0,4},{4,0},{8,12},{12,8},{16,20},{20,16},{24,28},{28,24},{1,5},{5... | collective-permute-start | bytes 786440 | tf_op jit(solution)/shard_map/ppermute | solution.py:30
  25.3 4.0 %collective-permute-start.5 = (bf16[3,64,2048]{2,1,0:T(8,128)(2,1)S(1)}, bf16[3,64,2048]{2,1,0:T(8,128)(2,1)S(1)}, u32[]{:S(2)}, u32[]{:S(2)}) collective-permute-start(bf16[3,64,2048]{2,1,0:T(8,128)(2,1)S(1)} %bitcast.99), channel_id=1, source_target_pairs={{0,4},{4,0},{8,12},{12,8},{16,20},{20,16},{24,28},{28,24},{1,5},{5... | collective-permute-start | bytes 2359304 | tf_op jit(solution)/shard_map/ppermute | solution.py:30
  26.8 5.9 %slice-start.2 = ((s8[5767168]{0:T(1024)(128)(4,1)}), s8[4194304]{0:T(1024)(128)(4,1)S(1)}, s32[]{:S(2)}) async-start(s8[5767168]{0:T(1024)(128)(4,1)} %bitcast.112), calls=%async_computation.2 | async-start | bytes 8388608
  27.3 5.3 %slice-start.3 = ((s8[5767168]{0:T(1024)(128)(4,1)}), s8[1572864]{0:T(1024)(128)(4,1)S(1)}, s32[]{:S(2)}) async-start(s8[5767168]{0:T(1024)(128)(4,1)} %bitcast.112), calls=%async_computation.3 | async-start | bytes 3145728
  29.6 13.4 %collective-permute-start.7 = (bf16[128,2048]{1,0:T(8,128)(2,1)S(1)}, bf16[128,2048]{1,0:T(8,128)(2,1)S(1)}, u32[]{:S(2)}, u32[]{:S(2)}) collective-permute-start(bf16[128,2048]{1,0:T(8,128)(2,1)S(1)} %pad_maximum_fusion.4), channel_id=1, source_target_pairs={{0,8},{4,12},{8,0},{12,4},{16,24},{20,28},{24,16},{28,20},{1,9},{5... | collective-permute-start | bytes 1572872 | tf_op jit(solution)/shard_map/ppermute | solution.py:30
  31.1 12.2 %collective-permute-start.10 = (bf16[128,2048]{1,0:T(8,128)(2,1)S(1)}, bf16[128,2048]{1,0:T(8,128)(2,1)S(1)}, u32[]{:S(2)}, u32[]{:S(2)}) collective-permute-start(bf16[128,2048]{1,0:T(8,128)(2,1)S(1)} %pad_maximum_fusion.5), channel_id=1, source_target_pairs={{0,16},{4,20},{8,24},{12,28},{16,0},{20,4},{24,8},{28,12},{1,17},{... | collective-permute-start | bytes 1572872 | tf_op jit(solution)/shard_map/ppermute | solution.py:30
  34.6 12.7 %collective-permute-start.11 = (bf16[120,1408]{1,0:T(8,128)(2,1)S(1)}, bf16[120,1408]{1,0:T(8,128)(2,1)S(1)}, u32[]{:S(2)}, u32[]{:S(2)}) collective-permute-start(bf16[120,1408]{1,0:T(8,128)(2,1)S(1)} %fusion.17), channel_id=1, source_target_pairs={{0,3},{1,2},{2,1},{3,0},{4,7},{5,6},{6,5},{7,4},{8,11},{9,10},{10,... | collective-permute-start | bytes 1013768 | tf_op jit(solution)/shard_map/ppermute | solution.py:34
  37.0 15.6 %collective-permute-start.13 = (bf16[120,1408]{1,0:T(8,128)(2,1)S(1)}, bf16[120,1408]{1,0:T(8,128)(2,1)S(1)}, u32[]{:S(2)}, u32[]{:S(2)}) collective-permute-start(bf16[120,1408]{1,0:T(8,128)(2,1)S(1)} %fusion.17), channel_id=1, source_target_pairs={{0,1},{1,0},{2,3},{3,2},{4,5},{5,4},{6,7},{7,6},{8,9},{9,8},{10,11... | collective-permute-start | bytes 1013768 | tf_op jit(solution)/shard_map/ppermute | solution.py:34
  37.0 27.7 %collective-permute-start.14 = (bf16[120,1408]{1,0:T(8,128)(2,1)S(1)}, bf16[120,1408]{1,0:T(8,128)(2,1)S(1)}, u32[]{:S(2)}, u32[]{:S(2)}) collective-permute-start(bf16[120,1408]{1,0:T(8,128)(2,1)S(1)} %fusion.17), channel_id=1, source_target_pairs={{0,2},{3,1},{4,6},{7,5},{8,10},{11,9},{12,14},{15,13},{16,18},{19,... | collective-permute-start | bytes 1013768 | tf_op jit(solution)/shard_map/ppermute | solution.py:34
  43.5 2.7 %collective-permute-start.12 = (bf16[4,256,512]{2,1,0:T(8,128)(2,1)S(1)}, bf16[4,256,512]{2,1,0:T(8,128)(2,1)S(1)}, u32[]{:S(2)}, u32[]{:S(2)}) collective-permute-start(bf16[4,256,512]{2,1,0:T(8,128)(2,1)S(1)} %get-tuple-element.124), channel_id=1, source_target_pairs={{0,4},{4,0},{8,12},{12,8},{16,20},{20,16},{24,28},{28,24},{1,5},{5... | collective-permute-start | bytes 3145736 | tf_op jit(solution)/shard_map/ppermute | solution.py:30
  43.6 18.0 %collective-permute-start.8 = (bf16[128,2048]{1,0:T(8,128)(2,1)S(1)}, bf16[128,2048]{1,0:T(8,128)(2,1)S(1)}, u32[]{:S(2)}, u32[]{:S(2)}) collective-permute-start(bf16[128,2048]{1,0:T(8,128)(2,1)S(1)} %pad_maximum_fusion.6), channel_id=1, source_target_pairs={{0,24},{4,28},{8,16},{12,20},{16,8},{20,12},{24,0},{28,4},{1,25},{... | collective-permute-start | bytes 1572872 | tf_op jit(solution)/shard_map/ppermute | solution.py:30
  47.4 17.4 %collective-permute-start.15 = (bf16[120,1408]{1,0:T(8,128)(2,1)S(1)}, bf16[120,1408]{1,0:T(8,128)(2,1)S(1)}, u32[]{:S(2)}, u32[]{:S(2)}) collective-permute-start(bf16[120,1408]{1,0:T(8,128)(2,1)S(1)} %collective-permute-done.11), channel_id=1, source_target_pairs={{1,0},{2,3},{5,4},{6,7},{9,8},{10,11},{13,12},{14,15},{17,16},{18,... | collective-permute-start | bytes 1013768 | tf_op jit(solution)/shard_map/ppermute | solution.py:34
  56.5 15.3 %collective-permute-start.20 = (bf16[248,1408]{1,0:T(8,128)(2,1)S(1)}, bf16[248,1408]{1,0:T(8,128)(2,1)S(1)}, u32[]{:S(2)}, u32[]{:S(2)}) collective-permute-start(bf16[248,1408]{1,0:T(8,128)(2,1)S(1)} %pad_maximum_fusion.3), channel_id=1, source_target_pairs={{1,2},{2,1},{5,6},{6,5},{9,10},{10,9},{13,14},{14,13},{17,18},{18,... | collective-permute-start | bytes 2095112 | tf_op jit(solution)/shard_map/ppermute | solution.py:34
  57.2 37.1 %collective-permute-start.19 = (bf16[248,1408]{1,0:T(8,128)(2,1)S(1)}, bf16[248,1408]{1,0:T(8,128)(2,1)S(1)}, u32[]{:S(2)}, u32[]{:S(2)}) collective-permute-start(bf16[248,1408]{1,0:T(8,128)(2,1)S(1)} %pad_maximum_fusion.3), channel_id=1, source_target_pairs={{0,1},{1,0},{2,3},{3,2},{4,5},{5,4},{6,7},{7,6},{8,9},{9,8},{10,11... | collective-permute-start | bytes 2095112 | tf_op jit(solution)/shard_map/ppermute | solution.py:34
  61.6 34.0 %collective-permute-start.18 = (bf16[248,1408]{1,0:T(8,128)(2,1)S(1)}, bf16[248,1408]{1,0:T(8,128)(2,1)S(1)}, u32[]{:S(2)}, u32[]{:S(2)}) collective-permute-start(bf16[248,1408]{1,0:T(8,128)(2,1)S(1)} %pad_maximum_fusion.3), channel_id=1, source_target_pairs={{0,2},{3,1},{4,6},{7,5},{8,10},{11,9},{12,14},{15,13},{16,18},{19,... | collective-permute-start | bytes 2095112 | tf_op jit(solution)/shard_map/ppermute | solution.py:34
  64.7 5.8 %slice-start = ((s8[5767168]{0:T(1024)(128)(4,1)}), s8[4194304]{0:T(1024)(128)(4,1)S(1)}, s32[]{:S(2)}) async-start(s8[5767168]{0:T(1024)(128)(4,1)} %bitcast.87), calls=%async_computation | async-start | bytes 8388608
  66.7 3.9 %slice-start.1 = ((s8[5767168]{0:T(1024)(128)(4,1)}), s8[1572864]{0:T(1024)(128)(4,1)S(1)}, s32[]{:S(2)}) async-start(s8[5767168]{0:T(1024)(128)(4,1)} %bitcast.87), calls=%async_computation.1 | async-start | bytes 3145728
  68.7 41.1 %collective-permute-start.24 = (bf16[120,1408]{1,0:T(8,128)(2,1)S(1)}, bf16[120,1408]{1,0:T(8,128)(2,1)S(1)}, u32[]{:S(2)}, u32[]{:S(2)}) collective-permute-start(bf16[120,1408]{1,0:T(8,128)(2,1)S(1)} %multiply_convert_fusion.1), channel_id=1, source_target_pairs={{0,1},{1,0},{2,3},{3,2},{4,5},{5,4},{6,7},{7,6},{8,9},{9,8},{10,11... | collective-permute-start | bytes 1013768 | tf_op jit(solution)/shard_map/ppermute | solution.py:34
  68.7 39.6 %collective-permute-start.17 = (bf16[120,1408]{1,0:T(8,128)(2,1)S(1)}, bf16[120,1408]{1,0:T(8,128)(2,1)}, u32[]{:S(2)}, u32[]{:S(2)}) collective-permute-start(bf16[120,1408]{1,0:T(8,128)(2,1)S(1)} %multiply_convert_fusion.1), channel_id=1, source_target_pairs={{0,3},{1,2},{2,1},{3,0},{4,7},{5,6},{6,5},{7,4},{8,11},{9,10},{10,... | collective-permute-start | bytes 1013768 | tf_op jit(solution)/shard_map/ppermute | solution.py:34
  71.8 53.4 %collective-permute-start.16 = (bf16[120,1408]{1,0:T(8,128)(2,1)S(1)}, bf16[120,1408]{1,0:T(8,128)(2,1)}, u32[]{:S(2)}, u32[]{:S(2)}) collective-permute-start(bf16[120,1408]{1,0:T(8,128)(2,1)S(1)} %multiply_convert_fusion.1), channel_id=1, source_target_pairs={{0,2},{3,1},{4,6},{7,5},{8,10},{11,9},{12,14},{15,13},{16,18},{19,... | collective-permute-start | bytes 1013768 | tf_op jit(solution)/shard_map/ppermute | solution.py:34
  94.3 27.9 %collective-permute-start.23 = (bf16[248,1408]{1,0:T(8,128)(2,1)S(1)}, bf16[248,1408]{1,0:T(8,128)(2,1)S(1)}, u32[]{:S(2)}, u32[]{:S(2)}) collective-permute-start(bf16[248,1408]{1,0:T(8,128)(2,1)S(1)} %collective-permute-done.20), channel_id=1, source_target_pairs={{1,0},{2,3},{5,4},{6,7},{9,8},{10,11},{13,12},{14,15},{17,16},{18,... | collective-permute-start | bytes 2095112 | tf_op jit(solution)/shard_map/ppermute | solution.py:34
  95.6 26.4 %collective-permute-start.22 = (bf16[248,1408]{1,0:T(8,128)(2,1)S(1)}, bf16[248,1408]{1,0:T(8,128)(2,1)S(1)}, u32[]{:S(2)}, u32[]{:S(2)}) collective-permute-start(bf16[248,1408]{1,0:T(8,128)(2,1)S(1)} %collective-permute-done.18), channel_id=1, source_target_pairs={{1,0},{2,3},{5,4},{6,7},{9,8},{10,11},{13,12},{14,15},{17,16},{18,... | collective-permute-start | bytes 2095112 | tf_op jit(solution)/shard_map/ppermute | solution.py:34
  108.3 17.4 %collective-permute-start.21 = (bf16[120,1408]{1,0:T(8,128)(2,1)}, bf16[120,1408]{1,0:T(8,128)(2,1)}, u32[]{:S(2)}, u32[]{:S(2)}) collective-permute-start(bf16[120,1408]{1,0:T(8,128)(2,1)} %collective-permute-done.17), channel_id=1, source_target_pairs={{1,0},{2,3},{5,4},{6,7},{9,8},{10,11},{13,12},{14,15},{17,16},{18,... | collective-permute-start | bytes 1013768 | tf_op jit(solution)/shard_map/ppermute | solution.py:34
  124.9 4.5 %copy-start.1 = (bf16[240,512]{1,0:T(8,128)(2,1)S(1)}, bf16[240,512]{1,0:T(8,128)(2,1)}, u32[]{:S(2)}) copy-start(bf16[240,512]{1,0:T(8,128)(2,1)} %fusion.21) | copy-start | bytes 737284
  125.2 5.7 %copy-start.2 = (f32[160,2]{0,1:T(2,128)S(1)}, f32[160,2]{0,1:T(2,128)}, u32[]{:S(2)}) copy-start(f32[160,2]{0,1:T(2,128)} %param.16) | copy-start | bytes 3844
  127.2 5.8 %collective-permute-start.27 = (bf16[120,512]{1,0:T(8,128)(2,1)S(1)}, bf16[120,512]{1,0:T(8,128)(2,1)S(1)}, u32[]{:S(2)}, u32[]{:S(2)}) collective-permute-start(bf16[120,512]{1,0:T(8,128)(2,1)S(1)} %add_convert_fusion.1), channel_id=1, source_target_pairs={{0,24},{4,28},{8,16},{12,20},{16,8},{20,12},{24,0},{28,4},{1,25},{... | collective-permute-start | bytes 368648 | tf_op jit(solution)/shard_map/ppermute | solution.py:30
  129.3 4.9 %collective-permute-start.25 = (bf16[120,512]{1,0:T(8,128)(2,1)S(1)}, bf16[120,512]{1,0:T(8,128)(2,1)S(1)}, u32[]{:S(2)}, u32[]{:S(2)}) collective-permute-start(bf16[120,512]{1,0:T(8,128)(2,1)S(1)} %get-tuple-element.139), channel_id=1, source_target_pairs={{0,8},{4,12},{8,0},{12,4},{16,24},{20,28},{24,16},{28,20},{1,9},{5... | collective-permute-start | bytes 368648 | tf_op jit(solution)/shard_map/ppermute | solution.py:30
  130.0 4.9 %collective-permute-start.26 = (bf16[120,512]{1,0:T(8,128)(2,1)S(1)}, bf16[120,512]{1,0:T(8,128)(2,1)S(1)}, u32[]{:S(2)}, u32[]{:S(2)}) collective-permute-start(bf16[120,512]{1,0:T(8,128)(2,1)S(1)} %get-tuple-element.140), channel_id=1, source_target_pairs={{0,16},{4,20},{8,24},{12,28},{16,0},{20,4},{24,8},{28,12},{1,17},{... | collective-permute-start | bytes 368648 | tf_op jit(solution)/shard_map/ppermute | solution.py:30
  135.1 1.6 %collective-permute-start.28 = (bf16[4,60,512]{2,1,0:T(8,128)(2,1)S(1)}, bf16[4,60,512]{2,1,0:T(8,128)(2,1)S(1)}, u32[]{:S(2)}, u32[]{:S(2)}) collective-permute-start(bf16[4,60,512]{2,1,0:T(8,128)(2,1)S(1)} %get-tuple-element.138), channel_id=1, source_target_pairs={{0,4},{4,0},{8,12},{12,8},{16,20},{20,16},{24,28},{28,24},{1,5},{5... | collective-permute-start | bytes 737288 | tf_op jit(solution)/shard_map/ppermute | solution.py:30
